TPU v7x, 256 devices: a whole 4x4x8 slice. The times are simulated.
256 devices in a mesh: clu: 32 (over x, y, core), blk: 8 (over z).
Axes of the slice: x: 4, y: 4, z: 8, core: 2. Of those that a mesh axis runs over, the one named last changes fastest.
Arguments:
- embeddings: float32 [131072, 768], P(('clu', 'blk')), may hold values from -6 to 6
- cluster_ids: int32 [131072, 1], P(('clu', 'blk')), may hold values from 0 to 31; in each aligned block of 512 rows (0 to 511, 512 to 1023, ...) at most 32 rows name the same one
- ranks: int32 [131072], P(('clu', 'blk')), may hold values from 0 to 1048575
Outputs:
- nearest: float32 [131072], P(('clu', 'blk'))
Inputs may be any that keep to these rules, and one draw needn't show every extreme that they name: `cluster_ids`: at most 32 of the rows held by one device name the same cluster, and in every draw some device's rows name one cluster exactly 32 times.
All inputs are finite; a program needn't handle non-finite values.
Results may differ from a plain program's by a relative error of at most 0.0012.
Values may be sent and summed in bfloat16 or wider, within the bound.
No kernel may reach another device: no remote copies, remote signals or barrier semaphores. Data moves between devices by JAX's collectives and lax.ppermute only.
A program may use at most 64 MiB of HBM per device.

v0:
```python
import math

import jax
import jax.numpy as jnp
from jax import lax
from jax.sharding import PartitionSpec as P


def normalize_rows(rows):
    norms = jnp.sum(rows * rows, axis=1, keepdims=True)
    return (rows * lax.rsqrt(norms + 1e-06)).astype(jnp.bfloat16)


def pair_scores(queries, keys):
    return jnp.einsum("md,nd->mn", queries, keys, preferred_element_type=jnp.float32)


def row_best(queries, query_rank, keys, key_rank):
    scores = pair_scores(queries, keys)
    allowed = (key_rank[None, :] >= 0) & (key_rank[None, :] < query_rank[:, None])
    return jnp.max(jnp.where(allowed, scores, -1.0), axis=1)


def on_device(embeddings, cluster_ids, ranks):
    rows_dev = embeddings.shape[0]
    groups = lax.axis_size("clu")
    capacity = 2 * rows_dev // groups
    slots = groups * capacity
    target = cluster_ids[:, 0]
    onehot = (target[:, None] == jnp.arange(groups, dtype=jnp.int32)[None, :]).astype(jnp.int32)
    before_count = jnp.cumsum(onehot, axis=0) - onehot
    slot_index = jnp.sum(before_count * onehot, axis=1)
    position = target * capacity + slot_index
    source_row = (
        jnp.zeros((slots,), jnp.int32).at[position].set(jnp.arange(rows_dev, dtype=jnp.int32))
    )
    occupied = jnp.zeros((slots,), jnp.bool_).at[position].set(True)
    slot_rank = jnp.where(occupied, ranks[source_row], -1).reshape(groups, capacity)
    outgoing = jnp.where(occupied[:, None], embeddings[source_row], 0.0)
    arrived, arrived_rank = (
        lax.all_to_all(
            outgoing.reshape(groups, capacity, -1), "clu", split_axis=0, concat_axis=0, tiled=True
        ),
        lax.all_to_all(slot_rank, "clu", split_axis=0, concat_axis=0, tiled=True),
    )
    queries = normalize_rows(arrived.reshape(slots, -1))
    query_rank = arrived_rank.reshape(slots)
    initial = jnp.full((slots,), -1.0, jnp.float32)
    running = initial
    keys = lax.all_gather(queries, "blk", axis=0, tiled=True)
    key_rank = lax.all_gather(query_rank, "blk", axis=0, tiled=True)
    count = keys.shape[0]
    block_rows = math.gcd(count, 512)
    key_parts = keys.reshape(count // block_rows, block_rows, keys.shape[1])
    rank_parts = key_rank.reshape(count // block_rows, block_rows)

    def one_part(current, item):
        return (jnp.maximum(current, row_best(queries, query_rank, item[0], item[1])), None)

    running, _ = lax.scan(one_part, running, (key_parts, rank_parts))
    homeward = lax.all_to_all(
        running.reshape(groups, capacity), "clu", split_axis=0, concat_axis=0, tiled=True
    )
    return homeward.reshape(slots)[position]


def solution(mesh):
    return jax.shard_map(
        on_device,
        mesh=mesh,
        in_specs=(P(("clu", "blk"), None), P(("clu", "blk"), None), P(("clu", "blk"))),
        out_specs=P(("clu", "blk")),
        check_vma=False,
    )
```

profile of v0, /device:TPU:1, one launch (start us, length us, event | category | flops | bytes accessed | tf_op | source)
XLA Modules:
  0.0 272.7 jit_solution(4361021403391592314)
XLA Ops:
  6.5 0.8 fusion.8
  7.3 1.2 reduce-window.6
  8.5 0.2 slice_reduce_fusion
  8.8 0.8 fusion.7
  9.6 0.7 compare_select_fusion
  10.3 2.4 scatter_custom_fusion.1
  12.7 2.4 scatter_custom_fusion
  15.2 0.1 broadcast_in_dim.48
  15.3 5.3 %gather_fusion.1 = f32[1024,768]{1,0:T(8,128)} fusion(f32[512,768]{1,0:T(8,128)S(1)} %copy-done, s32[1024]{0:T(1024)S(1)} %fusion.9), kind=kCustom, calls=%fused_computation.1 | custom fusion | bytes 6295552 | tf_op jit(solution)/shard_map/gather | solution.py:39
  20.5 2.2 broadcast_select_fusion
  22.7 47.8 %all_to_all.26 = f32[32,32,768]{2,1,0:T(8,128)S(1)} all-to-all(f32[32,32,768]{2,1,0:T(8,128)S(1)} %broadcast_select_fusion), channel_id=1, replica_groups=mesh['clu'=32,'blk'=8] {'clu'}, dimensions={0} | all-to-all | bytes 6291456 | tf_op jit(solution)/shard_map/all_to_all | solution.py:41
  70.5 1.7 copy-done.2
  72.2 0.3 multiply_reduce_fusion
  72.5 0.1 rsqrt.12
  72.5 3.3 %fusion.4 = bf16[1024,768]{1,0:T(8,128)(2,1)} fusion(f32[32,32,768]{2,1,0:T(8,128)} %copy-done.2, f32[1024]{0:T(1024)S(1)} %rsqrt.12), kind=kLoop, calls=%fused_computation.14 | loop fusion | flops 1572864 | bytes 4722688 | tf_op jit(solution)/shard_map/convert_element_type | solution.py:11
  75.9 6.9 %gather_fusion = s32[1024]{0:T(1024)S(1)} fusion(s32[512]{0:T(512)S(1)} %copy-done.1, s32[1024]{0:T(1024)S(1)} %fusion.9), kind=kCustom, calls=%fused_computation | custom fusion | bytes 12288 | tf_op jit(solution)/shard_map/gather | solution.py:38
  82.8 0.7 all_to_all.17
  83.5 4.0 %all-to-all-start = ((s32[32,1,32]{2,1,0:T(1,128)}), s32[32,1,32]{2,1,0:T(1,128)S(1)}, u32[]{:S(2)}, u32[]{:S(2)}) async-start(s32[32,1,32]{2,1,0:T(1,128)} %all_to_all.17), calls=%async_computation | async-start | bytes 32768 | tf_op jit(solution)/shard_map/all_to_all | solution.py:44
  87.4 6.9 %all-to-all-done = s32[32,1,32]{2,1,0:T(1,128)S(1)} async-done(((s32[32,1,32]{2,1,0:T(1,128)}), s32[32,1,32]{2,1,0:T(1,128)S(1)}, u32[]{:S(2)}, u32[]{:S(2)}) %all-to-all-start) | async-done | bytes 4128 | tf_op jit(solution)/shard_map/all_to_all | solution.py:44
  94.4 0.6 broadcast.83
  94.9 0.7 reduce.11
  95.6 0.1 reshape.65
  95.7 24.3 %all_gather.6 = s32[8192]{0:T(1024)S(1)} all-gather(s32[1024]{0:T(1024)S(1)} %reshape.65), channel_id=1, replica_groups=mesh['clu'=32,'blk'=8] {'blk'}, dimensions={0}, use_global_device_ids=true | all-gather | bytes 36864 | tf_op jit(solution)/shard_map/all_gather | solution.py:51
  120.1 88.9 %all-gather.2.cloned.1.call-done = bf16[8192,768]{1,0:T(8,128)(2,1)} async-done(((bf16[1024,768]{1,0:T(8,128)(2,1)}), bf16[8192,768]{1,0:T(8,128)(2,1)}) %all-gather.2.cloned.1.call-update) | async-done | bytes 12582928 | tf_op jit(solution)/shard_map/all_gather | solution.py:50
  209.0 37.0 %while.12 = (s32[]{:T(128)}, f32[1024]{0:T(1024)S(1)}, s32[16,512]{1,0:T(8,128)S(1)}, s32[32,32]{1,0:T(8,128)}, bf16[16,512,768]{2,1,0:T(8,128)(2,1)}, /*index=5...) while((s32[]{:T(128)}, f32[1024]{0:T(1024)S(1)}, ...), condition=%wide.wide.region_8.9_spmd.clone, body=%wide.wide.region_6.8_spmd.clone.sunk | while | flops 807405056 | bytes 2387063 | solution.py:60
  209.0 2.2 fusion.23
  211.3 2.2 fusion.23
  213.6 2.2 fusion.23
  215.9 2.2 fusion.23
  218.2 2.2 fusion.23
  220.6 2.2 fusion.23
  222.9 2.2 fusion.23
  225.2 2.2 fusion.23
  227.5 2.2 fusion.23
  229.8 2.2 fusion.23
  232.1 2.2 fusion.23
  234.5 2.2 fusion.23
  236.8 2.2 fusion.23
  239.1 2.2 fusion.23
  241.4 2.2 fusion.23
  243.7 2.2 fusion.23
  246.0 0.7 all_to_all.21
  246.7 7.6 %all-to-all-start.2 = ((f32[32,1,32]{2,1,0:T(1,128)}), f32[32,1,32]{2,1,0:T(1,128)S(1)}, u32[]{:S(2)}, u32[]{:S(2)}) async-start(f32[32,1,32]{2,1,0:T(1,128)} %all_to_all.21), calls=%async_computation.2 | async-start | bytes 32768 | tf_op jit(solution)/shard_map/all_to_all | solution.py:61
  254.3 6.9 %all-to-all-done.2 = f32[32,1,32]{2,1,0:T(1,128)S(1)} async-done(((f32[32,1,32]{2,1,0:T(1,128)}), f32[32,1,32]{2,1,0:T(1,128)S(1)}, u32[]{:S(2)}, u32[]{:S(2)}) %all-to-all-start.2) | async-done | bytes 4128 | tf_op jit(solution)/shard_map/all_to_all | solution.py:61
  261.2 0.5 broadcast.84
  261.7 0.7 reduce.12
  262.4 0.1 reshape.69
  262.5 3.4 %gather_fusion.2 = f32[512]{0:T(512)} fusion(f32[1024]{0:T(1024)S(1)} %reshape.69, s32[1024]{0:T(1024)S(1)} %pad_clamp_fusion), kind=kCustom, calls=%fused_computation.2 | custom fusion | bytes 6144 | tf_op jit(solution)/shard_map/gather | solution.py:64
  (54 shorter events, 0.7 us)
Async XLA Ops:
  6.5 8.7 %copy-start = (f32[512,768]{1,0:T(8,128)S(1)}, f32[512,768]{1,0:T(8,128)}, u32[]{:S(2)}) copy-start(f32[512,768]{1,0:T(8,128)} %param.5) | copy-start | bytes 4718596
  6.5 202.4 %all-gather.2.cloned.1.call-start = ((), (), s32[]{:S(2)}) async-start(), calls=%async_computation.3 | async-start | bytes 14155776 | tf_op jit(solution)/shard_map/all_gather | solution.py:50
  70.5 1.7 copy-start.2
  72.5 3.4 %copy-start.1 = (s32[512]{0:T(512)S(1)}, s32[512]{0:T(512)}, u32[]{:S(2)}) copy-start(s32[512]{0:T(512)} %param.7) | copy-start | bytes 6148
  75.9 133.1 %copy-start.3 = (bf16[1024,768]{1,0:T(8,128)(2,1)S(1)}, bf16[1024,768]{1,0:T(8,128)(2,1)}, u32[]{:S(2)}) copy-start(bf16[1024,768]{1,0:T(8,128)(2,1)} %fusion.4) | copy-start | bytes 4718596
  83.5 10.9 %all-to-all-start = ((s32[32,1,32]{2,1,0:T(1,128)}), s32[32,1,32]{2,1,0:T(1,128)S(1)}, u32[]{:S(2)}, u32[]{:S(2)}) async-start(s32[32,1,32]{2,1,0:T(1,128)} %all_to_all.17), calls=%async_computation | async-start | bytes 32768 | tf_op jit(solution)/shard_map/all_to_all | solution.py:44
  94.4 114.6 %copy-start.4 = (s32[32,1,32]{2,1,0:T(1,128)}, s32[32,1,32]{2,1,0:T(1,128)S(1)}, u32[]{:S(2)}) copy-start(s32[32,1,32]{2,1,0:T(1,128)S(1)} %all-to-all-done) | copy-start | bytes 12292
  246.7 14.5 %all-to-all-start.2 = ((f32[32,1,32]{2,1,0:T(1,128)}), f32[32,1,32]{2,1,0:T(1,128)S(1)}, u32[]{:S(2)}, u32[]{:S(2)}) async-start(f32[32,1,32]{2,1,0:T(1,128)} %all_to_all.21), calls=%async_computation.2 | async-start | bytes 32768 | tf_op jit(solution)/shard_map/all_to_all | solution.py:61
Sparse Core Ops, SparseCore 0:
  76.0 132.8 all-gather.1
where the time goes:
time: 274 us; the launch traced here: 273 us
  waiting for transfers between devices  103 us (38%)
  blocking collectives  72.1 us (26%)
  matrix products  35.9 us (13%)
  local copies, waits for them, and re-layouts  25.2 us (9%)
  between operations  13.5 us (5%)
  starting transfers between devices  11.5 us (4%)
  other arithmetic  11.2 us (4%)
    all_gather x1, waiting for transfers between devices, on_device(): keys = lax.all_gather(queries, 'blk', axis=0, tiled=True)  88.9 us
    all_to_all x1, blocking collectives, on_device(): lax.all_to_all(outgoing.reshape(groups, capacity, -1), 'clu', split_axis=...  47.8 us
    dot_general x16, matrix products, pair_scores(): jnp.einsum('md,nd->mn', queries, keys, preferred_element_type=jnp.float32)  35.9 us
    all_gather x1, blocking collectives, on_device(): key_rank = lax.all_gather(query_rank, 'blk', axis=0, tiled=True)  24.3 us
    all_to_all x1, starting transfers between devices, on_device(): lax.all_to_all(running.reshape(groups, capacity), 'clu', split_axis=0, co...  7.57 us
    all_to_all x1, waiting for transfers between devices, on_device(): lax.all_to_all(slot_rank, 'clu', split_axis=0, concat_axis=0, tiled=True)  6.93 us
    all_to_all x1, waiting for transfers between devices, on_device(): lax.all_to_all(running.reshape(groups, capacity), 'clu', split_axis=0, co...  6.93 us
    gather x1, local copies, waits for them, and re-layouts, on_device(): ranks[source_row]  6.86 us
  transfers between devices with their start and end apart: 3, of which 3 were waited for; matrix products, arithmetic and copies ran while one was open for 3% of the time, Pallas kernels for 0%

commit v1 on v0

v1 whole, which is shorter than its diff:
```python
import functools

import jax
import jax.numpy as jnp
from jax import lax
from jax.experimental import pallas as pl
from jax.experimental.pallas import tpu as pltpu
from jax.sharding import Mesh, PartitionSpec as P

D = 768
ROWS = 512
GROUPS = 32
HALF = 16
PARTS = D // 128
SIZE = {"x": 4, "y": 4, "c": 2, "z": 8}
LIMIT = 60 * 1024 * 1024
NT = (((1,), (1,)), ((), ()))
NN = (((1,), (0,)), ((), ()))


def dot(a, b, dims):
    return lax.dot_general(a, b, dims, preferred_element_type=jnp.float32)


def to_lanes(column):
    return jnp.broadcast_to(column, (column.shape[0], 128)).T[0:1, :]


def pack_kernel(emb_ref, ids_ref, rank_ref, first_ref, second_ref, pos_ref):
    rows = emb_ref[...]
    norms = jnp.sum(rows * rows, axis=1, keepdims=True)
    unit = (rows * lax.rsqrt(norms + 1e-06)).astype(jnp.bfloat16)

    lane = lax.broadcasted_iota(jnp.int32, (ROWS, 128), 1)
    target = ids_ref[...]
    member = (target == lane).astype(jnp.float32)
    earlier = lax.broadcasted_iota(jnp.int32, (ROWS, ROWS), 1) < lax.broadcasted_iota(
        jnp.int32, (ROWS, ROWS), 0
    )
    before = dot(earlier.astype(jnp.bfloat16), member.astype(jnp.bfloat16), NN)
    slot = jnp.sum(before * member, axis=1, keepdims=True).astype(jnp.int32)
    position = (slot // HALF) * (GROUPS * HALF) + target * HALF + slot % HALF
    pos_ref[...] = position

    at = to_lanes(position.astype(jnp.float32)).astype(jnp.int32)
    rank = rank_ref[...]
    high, mid, low = (rank >> 14) - 128, (rank >> 7) & 127, rank & 127

    def rank_lanes(start):
        parts = jnp.where(lane == start, high, 0)
        parts = jnp.where(lane == start + 1, mid, parts)
        return jnp.where(lane == start + 2, low, parts).astype(jnp.float32).astype(jnp.bfloat16)

    def pick(half):
        slots = lax.broadcasted_iota(jnp.int32, (GROUPS * HALF, ROWS), 0) + half * GROUPS * HALF
        return (slots == at).astype(jnp.float32).astype(jnp.bfloat16)

    ranks = jnp.zeros((GROUPS * HALF, 128), jnp.float32)
    for half, out_ref in enumerate((first_ref, second_ref)):
        chosen = pick(half)
        moved = dot(chosen, unit, NN).astype(jnp.bfloat16)
        for part in range(PARTS):
            out_ref[:, part * HALF : (part + 1) * HALF, :] = moved[
                :, part * 128 : (part + 1) * 128
            ].reshape(GROUPS, HALF, 128)
        ranks += dot(chosen, rank_lanes(3 * half), NN)
    first_ref[:, D // 8 :, :] = ranks.astype(jnp.bfloat16).reshape(GROUPS, HALF, 128)


def vmem(count):
    return [pl.BlockSpec(memory_space=pltpu.VMEM)] * count


def pack(embeddings, ids, ranks):
    return pl.pallas_call(
        pack_kernel,
        out_shape=(
            jax.ShapeDtypeStruct((GROUPS, D // 8 + HALF, 128), jnp.bfloat16),
            jax.ShapeDtypeStruct((GROUPS, D // 8, 128), jnp.bfloat16),
            jax.ShapeDtypeStruct((ROWS, 1), jnp.int32),
        ),
        in_specs=vmem(3),
        out_specs=tuple(vmem(3)),
        compiler_params=pltpu.CompilerParams(vmem_limit_bytes=LIMIT),
        name="pack",
    )(embeddings, ids, ranks)


def keys_of(ref):
    wide = [
        ref[:, part * HALF : (part + 1) * HALF, :].reshape(GROUPS * HALF, 128)
        for part in range(PARTS)
    ]
    return jnp.concatenate(wide, axis=1)


def rank_weights(shape, axis, start):
    place = lax.broadcasted_iota(jnp.int32, shape, axis) - start
    weights = jnp.where(place == 0, 16384.0, jnp.where(place == 1, 128.0, 1.0))
    return jnp.where((place >= 0) & (place < 3), weights, 0.0).astype(jnp.bfloat16)


def score_kernel(names, pairs, finals, *refs):
    firsts = sorted({name[0] for name in names})
    data = dict(zip(names, refs))
    carried = refs[len(names)]
    out_ref = refs[len(names) + 1]
    keys = {name: keys_of(data[name]) for name in names}
    by_row, by_lane = {}, {}
    for block in firsts:
        tile = data[block + "0"][:, D // 8 :, :].reshape(GROUPS * HALF, 128)
        for half in range(2):
            name = block + str(half)
            if name in names:
                by_row[name] = dot(tile, rank_weights((128, 128), 0, 3 * half), NN)
                by_lane[name] = dot(rank_weights((8, 128), 1, 3 * half), tile, NT)[0:1]
    best_row, best_lane = {}, {}
    for rows, columns, forward, backward in pairs:
        scores = dot(keys[rows], keys[columns], NT)
        row_rank = jnp.concatenate([by_row[rows]] * 4, axis=1)
        lane_rank = by_lane[columns]
        if forward:
            kept = jnp.where(lane_rank < row_rank, scores, -1.0)
            folded = functools.reduce(
                jnp.maximum, [kept[:, 128 * i : 128 * (i + 1)] for i in range(4)]
            )
            best_row[rows] = jnp.maximum(best_row[rows], folded) if rows in best_row else folded
        if backward:
            kept = jnp.where(row_rank < lane_rank, scores, -1.0)
            folded = jnp.max(kept, axis=0, keepdims=True)
            if columns in best_lane:
                folded = jnp.maximum(best_lane[columns], folded)
            best_lane[columns] = folded
    for index, name in enumerate(finals):
        value = carried[index : index + 1, :]
        if name in best_lane:
            value = jnp.maximum(value, best_lane[name])
        if name in best_row:
            value = jnp.maximum(value, jnp.max(best_row[name].T, axis=0, keepdims=True))
        out_ref[index : index + 1, :] = value


FINALS = ("o0", "o1", "s0", "s1", "b0", "b1", "z0", "z1")


def score(blocks, pairs, carried):
    names = tuple(sorted(blocks))
    return pl.pallas_call(
        functools.partial(score_kernel, names, pairs, FINALS),
        out_shape=jax.ShapeDtypeStruct((8, GROUPS * HALF), jnp.float32),
        in_specs=vmem(len(names) + 1),
        out_specs=vmem(1)[0],
        compiler_params=pltpu.CompilerParams(vmem_limit_bytes=LIMIT),
        cost_estimate=pl.CostEstimate(
            flops=2 * len(pairs) * 512 * 512 * D, bytes_accessed=800000 * len(names), transcendentals=0
        ),
        name="score" + str(len(pairs)),
    )(*[blocks[name] for name in names], carried)


FIRST = (
    ("o0", "o0", True, False),
    ("o0", "s0", True, False),
    ("o0", "b0", True, True),
    ("s0", "b0", True, True),
    ("z0", "b0", True, True),
)
SECOND = (
    ("o1", "o1", True, False),
    ("o0", "o1", True, True),
    ("o1", "s1", True, False),
    ("o0", "s1", True, True),
    ("o0", "b1", True, True),
    ("o1", "b0", True, True),
    ("o1", "b1", True, True),
    ("s0", "b1", True, True),
    ("s1", "b0", True, True),
    ("s1", "b1", True, True),
    ("z0", "b1", True, True),
    ("z1", "b0", True, True),
    ("z1", "b1", True, True),
)

FROM_NEXT = [
    (((x + 1) % 4) * 2 + (c if x < 2 else 1 - c), x * 2 + c) for x in range(4) for c in range(2)
]
FROM_LAST = [(((x - 1) % 4) * 2 + c, x * 2 + c) for x in range(4) for c in range(2)]
SWAP = [(x * 2 + 1 - c, x * 2 + c) for x in range(4) for c in range(2)]


def back(pairs):
    return [(there, here) for here, there in pairs]


def send(array, pairs):
    return lax.ppermute(array, ("x", "c"), pairs)


def spread(part):
    return send(part, SWAP), send(part, FROM_NEXT), send(part, FROM_LAST)


def to_home(array):
    return lax.all_to_all(array, ("y", "z"), split_axis=0, concat_axis=0, tiled=True)


def on_device(embeddings, cluster_ids, ranks):
    first, second, position = pack(embeddings, cluster_ids, ranks.reshape(ROWS, 1))
    o0 = to_home(first)
    s0, b0, z0 = spread(o0)
    o1 = to_home(second)
    s1, b1, z1 = spread(o1)
    best = jnp.full((8, GROUPS * HALF), -1.0, jnp.float32)
    best = score(dict(o0=o0, s0=s0, b0=b0, z0=z0), FIRST, best)
    best = score(dict(o0=o0, s0=s0, b0=b0, z0=z0, o1=o1, s1=s1, b1=b1, z1=z1), SECOND, best)
    own = functools.reduce(
        jnp.maximum,
        [
            best[0:2],
            send(best[2:4], back(SWAP)),
            send(best[4:6], back(FROM_NEXT)),
            send(best[6:8], back(FROM_LAST)),
        ],
    )
    own = own.reshape(2, GROUPS, HALF).transpose(1, 0, 2).reshape(GROUPS, 2 * HALF)
    home = to_home(own).reshape(GROUPS, 2, HALF).transpose(1, 0, 2).reshape(2 * GROUPS * HALF)
    return home[position[:, 0]]


def solution(mesh):
    fine = Mesh(mesh.devices.reshape(tuple(SIZE.values())), tuple(SIZE))
    rows = P(tuple(SIZE))
    return jax.shard_map(
        on_device,
        mesh=fine,
        in_specs=(P(tuple(SIZE), None), P(tuple(SIZE), None), rows),
        out_specs=rows,
        check_vma=False,
    )
```

time: 274 us -> 137 us (0.50)
  waiting for transfers between devices: 103 us -> 39.3 us
  blocking collectives: 72.1 us -> 34 us
  matrix products: 35.9 us -> 0 us
  starting transfers between devices: 11.5 us -> 32.6 us
  Pallas kernels: 0 us -> 20 us
  local copies, waits for them, and re-layouts: 25.2 us -> 9.32 us
  between operations: 13.5 us -> 0.06 us
  other arithmetic: 11.2 us -> 0.88 us
    all_gather x1 -> x0, waiting for transfers between devices: 88.9 us -> none  [on_device(): keys = lax.all_gather(queries, 'blk', axis=0, tiled=True)]
    dot_general x16 -> x0, matrix products: 35.9 us -> none  [pair_scores(): jnp.einsum('md,nd->mn', queries, keys, preferred_element_type=jnp.float32)]
    all_gather x1 -> x0, blocking collectives: 24.3 us -> none  [on_device(): key_rank = lax.all_gather(query_rank, 'blk', axis=0, tiled=True)]
    pallas_call x0 -> x3, Pallas kernels: none -> 20 us  [the longest x2 15.1 us: score(): pl.pallas_call(functools.partial(score_kernel, names, pairs, FINALS), out...]
    ppermute x0 -> x9, starting transfers between devices: none -> 15.6 us  [send(): return lax.ppermute(array, ('x', 'c'), pairs)]
    ppermute x0 -> x9, waiting for transfers between devices: none -> 15.3 us  [send(): return lax.ppermute(array, ('x', 'c'), pairs)]
    all_to_all x1, blocking collectives: 47.8 us -> 34 us  [to_home(): lax.all_to_all(array, ('y', 'z'), split_axis=0, concat_axis=0, tiled=True)]
    gather x3 -> x1, local copies, waits for them, and re-layouts: 15.5 us -> 3.42 us  [on_device(): return home[position[:, 0]]]
  transfers between devices with their start and end apart: 3 -> 11, of which waited for: 3 -> 6; matrix products, arithmetic and copies ran while one was open for 3% -> 1% of each run, Pallas kernels for 0% -> 4%
where the time goes in v1:
time: 137 us; the launch traced here: 136 us
  waiting for transfers between devices  39.3 us (29%)
  blocking collectives  34 us (25%)
  starting transfers between devices  32.6 us (24%)
  Pallas kernels  20 us (15%)
  local copies, waits for them, and re-layouts  9.32 us (7%)
    all_to_all x1, blocking collectives, to_home(): lax.all_to_all(array, ('y', 'z'), split_axis=0, concat_axis=0, tiled=True)  34 us
    all_to_all x2, waiting for transfers between devices, to_home(): lax.all_to_all(array, ('y', 'z'), split_axis=0, concat_axis=0, tiled=True)  24 us
    all_to_all x2, starting transfers between devices, to_home(): lax.all_to_all(array, ('y', 'z'), split_axis=0, concat_axis=0, tiled=True)  17.1 us
    ppermute x9, starting transfers between devices, send(): return lax.ppermute(array, ('x', 'c'), pairs)  15.6 us
    ppermute x9, waiting for transfers between devices, send(): return lax.ppermute(array, ('x', 'c'), pairs)  15.3 us
    pallas_call x2, Pallas kernels, score(): pl.pallas_call(functools.partial(score_kernel, names, pairs, FINALS), out...  15.1 us
    pallas_call x1, Pallas kernels, pack(): pl.pallas_call(pack_kernel, out_shape=(jax.ShapeDtypeStruct((GROUPS, D //...  4.84 us
    gather x1, local copies, waits for them, and re-layouts, on_device(): return home[position[:, 0]]  3.42 us
  transfers between devices with their start and end apart: 11, of which 6 were waited for; matrix products, arithmetic and copies ran while one was open for 1% of the time, Pallas kernels for 4%

profile of v1, /device:TPU:1, one launch (start us, length us, event | category | flops | bytes accessed | tf_op | source)
XLA Modules:
  0.0 136.2 jit_solution(6891925858797653428)
XLA Ops:
  0.0 1.5 %copy.9.ids_ref = s32[512,1]{1,0:T(8,128)} copy(s32[512,1]{0,1:T(1,128)} %param.4) | data formatting | bytes 4096 | tf_op args[1]
  1.5 1.5 %copy.10.rank_ref = s32[512,1]{1,0:T(8,128)} copy(s32[512,1]{0,1:T(1,128)} %bitcast.9) | data formatting | bytes 4096 | tf_op jit(solution)/shard_map/reshape | solution.py:208
  3.1 4.8 %pack.1 = (bf16[32,112,128]{2,1,0:T(8,128)(2,1)}, bf16[32,96,128]{2,1,0:T(8,128)(2,1)}, s32[512,1]{1,0:T(8,128)}) custom-call(f32[512,768]{1,0:T(8,128)} %emb_ref.1, s32[512,1]{1,0:T(8,128)} %copy.9.ids_ref, s32[512,1]{1,0:T(8,128)} %copy.10.rank_ref), custom_call_target="tpu_custom_call" | custom-call | tf_op jit(solution)/shard_map/pack/pallas_call | solution.py:75
  7.9 34.0 %all_to_all.19.refs_1_.refs_2_ = bf16[32,112,128]{2,1,0:T(8,128)(2,1)S(1)} all-to-all(bf16[32,112,128]{2,1,0:T(8,128)(2,1)} %get-tuple-element.8), channel_id=1, replica_groups=mesh['x'=4,'y'=4,'c'=2,'z'=8] {'y','z'}, dimensions={0} | all-to-all | bytes 1835008 | tf_op jit(solution)/shard_map/all_to_all | solution.py:204
  41.9 0.0 copy-start
  41.9 8.5 %all-to-all-start.1 = ((bf16[32,96,128]{2,1,0:T(8,128)(2,1)}), bf16[32,96,128]{2,1,0:T(8,128)(2,1)S(1)}, u32[]{:S(2)}, u32[]{:S(2)}) async-start(bf16[32,96,128]{2,1,0:T(8,128)(2,1)} %get-tuple-element.9), calls=%async_computation.1 | async-start | bytes 1572864 | tf_op jit(solution)/shard_map/all_to_all | solution.py:204
  50.4 1.3 collective-permute-start.4
  51.7 1.7 %collective-permute-start.2 = (bf16[32,112,128]{2,1,0:T(8,128)(2,1)S(1)}, bf16[32,112,128]{2,1,0:T(8,128)(2,1)S(1)}, u32[]{:S(2)}, u32[]{:S(2)}) collective-permute-start(bf16[32,112,128]{2,1,0:T(8,128)(2,1)S(1)} %all_to_all.19.refs_1_.refs_2_), channel_id=1, source_target_pairs={{8,0},{0,8},{72,64},{64,72},{136,128},{128,136},{200,192},{192,200... | collective-permute-start | bytes 2752520 | tf_op jit(solution)/shard_map/ppermute | solution.py:196
  53.4 1.4 collective-permute-start
  54.7 15.4 %all-to-all-done.1.refs_3_ = bf16[32,96,128]{2,1,0:T(8,128)(2,1)S(1)} async-done(((bf16[32,96,128]{2,1,0:T(8,128)(2,1)}), bf16[32,96,128]{2,1,0:T(8,128)(2,1)S(1)}, u32[]{:S(2)}, u32[]{:S(2)}) %all-to-all-start.1) | async-done | bytes 786464 | tf_op jit(solution)/shard_map/all_to_all | solution.py:204
  70.2 0.0 copy-start.1
  70.2 1.2 collective-permute-start.5
  71.4 4.8 %collective-permute-start.3 = (bf16[32,96,128]{2,1,0:T(8,128)(2,1)S(1)}, bf16[32,96,128]{2,1,0:T(8,128)(2,1)}, u32[]{:S(2)}, u32[]{:S(2)}) collective-permute-start(bf16[32,96,128]{2,1,0:T(8,128)(2,1)S(1)} %all-to-all-done.1.refs_3_), channel_id=1, source_target_pairs={{8,0},{0,8},{72,64},{64,72},{136,128},{128,136},{200,192},{192,200... | collective-permute-start | bytes 2359304 | tf_op jit(solution)/shard_map/ppermute | solution.py:196
  76.1 0.0 collective-permute-done.4.refs_3_.refs_6_
  76.2 0.0 copy-start.3
  76.2 1.6 %collective-permute-start.1 = (bf16[32,96,128]{2,1,0:T(8,128)(2,1)S(1)}, bf16[32,96,128]{2,1,0:T(8,128)(2,1)}, u32[]{:S(2)}, u32[]{:S(2)}) collective-permute-start(bf16[32,96,128]{2,1,0:T(8,128)(2,1)S(1)} %all-to-all-done.1.refs_3_), channel_id=1, source_target_pairs={{64,0},{72,8},{128,64},{136,72},{200,128},{192,136},{8,192},{0,200... | collective-permute-start | bytes 2359304 | tf_op jit(solution)/shard_map/ppermute | solution.py:196
  77.8 0.0 collective-permute-done.2.refs_2_.refs_4_
  77.8 0.0 copy-start.4
  77.8 0.0 collective-permute-done.refs_0_
  77.8 0.7 broadcast_in_dim.4.refs_4_
  78.5 0.0 copy-done
  78.5 0.0 copy-done.3
  78.5 0.2 copy-done.4
  78.7 5.3 %score5.1.refs_8_ = f32[8,512]{1,0:T(8,128)} custom-call(bf16[32,112,128]{2,1,0:T(8,128)(2,1)} %collective-permute-done.refs_0_, bf16[32,112,128]{2,1,0:T(8,128)(2,1)} %copy-done, bf16[32,112,128]{2,1,0:T(8,128)(2,1)} %copy-done.4, bf16[32,112,128]{2,1,0:T(8,128)(2,1)} %copy-done.3, f32[8,512]{1,0:T(8,128)} %broadcast_in_dim.4.refs_4_), custom_call_target="tpu_custom_call" | custom-call | flops 2013265920 | bytes 3200000 | tf_op jit(solution)/shard_map/score5/pallas_call | solution.py:148
  84.0 0.0 copy-done.1
  84.0 2.0 %collective-permute-done.5.refs_7_ = bf16[32,96,128]{2,1,0:T(8,128)(2,1)} collective-permute-done((bf16[32,96,128]{2,1,0:T(8,128)(2,1)S(1)}, bf16[32,96,128]{2,1,0:T(8,128)(2,1)}, u32[]{:S(2)}, u32[]{:S(2)}) %collective-permute-start.5) | collective-permute-done | bytes 786464 | tf_op jit(solution)/shard_map/ppermute | solution.py:196
  86.0 0.0 collective-permute-done.3.refs_5_
  86.0 9.1 %collective-permute-done.1.refs_1_ = bf16[32,96,128]{2,1,0:T(8,128)(2,1)} collective-permute-done((bf16[32,96,128]{2,1,0:T(8,128)(2,1)S(1)}, bf16[32,96,128]{2,1,0:T(8,128)(2,1)}, u32[]{:S(2)}, u32[]{:S(2)}) %collective-permute-start.1) | collective-permute-done | bytes 786464 | tf_op jit(solution)/shard_map/ppermute | solution.py:196
  95.1 9.9 %score13.1 = f32[8,512]{1,0:T(8,128)} custom-call(bf16[32,112,128]{2,1,0:T(8,128)(2,1)} %collective-permute-done.refs_0_, bf16[32,96,128]{2,1,0:T(8,128)(2,1)} %collective-permute-done.1.refs_1_, bf16[32,112,128]{2,1,0:T(8,128)(2,1)} %copy-done, bf16[32,96,128]{2,1,0:T(8,128)(2,1)} %copy-done.1, bf16[32,112,128]{2,1,0:T(8,128)(2,1)} %copy-done.4, ...), custom_call_target="tpu_custom_call" | custom-call | flops 5234491392 | bytes 6400000 | tf_op jit(solution)/shard_map/score13/pallas_call | solution.py:148
  105.0 0.8 fusion.3
  105.8 1.1 collective-permute-start.6
  106.9 2.5 %collective-permute-start.8 = (f32[2,512]{1,0:T(2,128)S(1)}, f32[2,512]{1,0:T(2,128)S(1)}, u32[]{:S(2)}, u32[]{:S(2)}) collective-permute-start(f32[2,512]{1,0:T(2,128)S(1)} %get-tuple-element.12), channel_id=1, source_target_pairs={{0,192},{8,200},{64,0},{72,8},{128,64},{136,72},{192,128},{200,136... | collective-permute-start | bytes 12296 | tf_op jit(solution)/shard_map/ppermute | solution.py:196
  109.4 0.0 collective-permute-start.7
  109.4 0.0 copy-done.2
  109.4 0.1 fusion
  109.6 0.0 collective-permute-done.6
  109.6 0.6 collective-permute-done.8
  110.2 3.5 %collective-permute-done.7 = f32[2,512]{1,0:T(2,128)S(1)} collective-permute-done((f32[2,512]{1,0:T(2,128)S(1)}, f32[2,512]{1,0:T(2,128)S(1)}, u32[]{:S(2)}, u32[]{:S(2)}) %collective-permute-start.7) | collective-permute-done | bytes 4128 | tf_op jit(solution)/shard_map/ppermute | solution.py:196
  113.7 0.7 fusion.2
  114.4 0.1 reshape.18
  114.5 0.1 copy.11
  114.6 0.7 copy.12
  115.3 8.6 %all-to-all-start.2 = ((f32[32,1,32]{2,1,0:T(1,128)}), f32[32,1,32]{2,1,0:T(1,128)S(1)}, u32[]{:S(2)}, u32[]{:S(2)}) async-start(f32[32,1,32]{2,1,0:T(1,128)} %copy.12), calls=%async_computation.2 | async-start | bytes 32768 | tf_op jit(solution)/shard_map/all_to_all | solution.py:204
  123.9 8.6 %all-to-all-done.2 = f32[32,1,32]{2,1,0:T(1,128)S(1)} async-done(((f32[32,1,32]{2,1,0:T(1,128)}), f32[32,1,32]{2,1,0:T(1,128)S(1)}, u32[]{:S(2)}, u32[]{:S(2)}) %all-to-all-start.2) | async-done | bytes 4128 | tf_op jit(solution)/shard_map/all_to_all | solution.py:204
  132.5 0.1 copy.13
  132.6 0.1 copy.14
  132.7 0.1 reshape.20
  132.7 3.4 %gather_fusion = f32[512]{0:T(512)} fusion(f32[1024]{0:T(1024)S(1)} %reshape.20, s32[1024]{0:T(1024)S(1)} %pad_clamp_fusion), kind=kCustom, calls=%fused_computation | custom fusion | bytes 6144 | tf_op jit(solution)/shard_map/gather | solution.py:227
  (2 shorter events, 0.0 us)
Async XLA Ops:
  41.9 36.6 %copy-start = (bf16[32,112,128]{2,1,0:T(8,128)(2,1)}, bf16[32,112,128]{2,1,0:T(8,128)(2,1)S(1)}, u32[]{:S(2)}) copy-start(bf16[32,112,128]{2,1,0:T(8,128)(2,1)S(1)} %all_to_all.19.refs_1_.refs_2_) | copy-start | bytes 2752516
  41.9 28.3 %all-to-all-start.1 = ((bf16[32,96,128]{2,1,0:T(8,128)(2,1)}), bf16[32,96,128]{2,1,0:T(8,128)(2,1)S(1)}, u32[]{:S(2)}, u32[]{:S(2)}) async-start(bf16[32,96,128]{2,1,0:T(8,128)(2,1)} %get-tuple-element.9), calls=%async_computation.1 | async-start | bytes 1572864 | tf_op jit(solution)/shard_map/all_to_all | solution.py:204
  50.4 25.8 %collective-permute-start.4 = (bf16[32,112,128]{2,1,0:T(8,128)(2,1)S(1)}, bf16[32,112,128]{2,1,0:T(8,128)(2,1)S(1)}, u32[]{:S(2)}, u32[]{:S(2)}) collective-permute-start(bf16[32,112,128]{2,1,0:T(8,128)(2,1)S(1)} %all_to_all.19.refs_1_.refs_2_), channel_id=1, source_target_pairs={{192,0},{200,8},{0,64},{8,72},{64,128},{72,136},{128,192},{136,200... | collective-permute-start | bytes 2752520 | tf_op jit(solution)/shard_map/ppermute | solution.py:196
  51.7 26.1 %collective-permute-start.2 = (bf16[32,112,128]{2,1,0:T(8,128)(2,1)S(1)}, bf16[32,112,128]{2,1,0:T(8,128)(2,1)S(1)}, u32[]{:S(2)}, u32[]{:S(2)}) collective-permute-start(bf16[32,112,128]{2,1,0:T(8,128)(2,1)S(1)} %all_to_all.19.refs_1_.refs_2_), channel_id=1, source_target_pairs={{8,0},{0,8},{72,64},{64,72},{136,128},{128,136},{200,192},{192,200... | collective-permute-start | bytes 2752520 | tf_op jit(solution)/shard_map/ppermute | solution.py:196
  53.4 24.4 %collective-permute-start = (bf16[32,112,128]{2,1,0:T(8,128)(2,1)S(1)}, bf16[32,112,128]{2,1,0:T(8,128)(2,1)}, u32[]{:S(2)}, u32[]{:S(2)}) collective-permute-start(bf16[32,112,128]{2,1,0:T(8,128)(2,1)S(1)} %all_to_all.19.refs_1_.refs_2_), channel_id=1, source_target_pairs={{64,0},{72,8},{128,64},{136,72},{200,128},{192,136},{8,192},{0,200... | collective-permute-start | bytes 2752520 | tf_op jit(solution)/shard_map/ppermute | solution.py:196
  70.2 13.8 %copy-start.1 = (bf16[32,96,128]{2,1,0:T(8,128)(2,1)}, bf16[32,96,128]{2,1,0:T(8,128)(2,1)S(1)}, u32[]{:S(2)}) copy-start(bf16[32,96,128]{2,1,0:T(8,128)(2,1)S(1)} %all-to-all-done.1.refs_3_) | copy-start | bytes 2359300
  70.2 15.8 %collective-permute-start.5 = (bf16[32,96,128]{2,1,0:T(8,128)(2,1)S(1)}, bf16[32,96,128]{2,1,0:T(8,128)(2,1)}, u32[]{:S(2)}, u32[]{:S(2)}) collective-permute-start(bf16[32,96,128]{2,1,0:T(8,128)(2,1)S(1)} %all-to-all-done.1.refs_3_), channel_id=1, source_target_pairs={{192,0},{200,8},{0,64},{8,72},{64,128},{72,136},{128,192},{136,200... | collective-permute-start | bytes 2359304 | tf_op jit(solution)/shard_map/ppermute | solution.py:196
  71.4 14.6 %collective-permute-start.3 = (bf16[32,96,128]{2,1,0:T(8,128)(2,1)S(1)}, bf16[32,96,128]{2,1,0:T(8,128)(2,1)}, u32[]{:S(2)}, u32[]{:S(2)}) collective-permute-start(bf16[32,96,128]{2,1,0:T(8,128)(2,1)S(1)} %all-to-all-done.1.refs_3_), channel_id=1, source_target_pairs={{8,0},{0,8},{72,64},{64,72},{136,128},{128,136},{200,192},{192,200... | collective-permute-start | bytes 2359304 | tf_op jit(solution)/shard_map/ppermute | solution.py:196
  76.2 2.3 %copy-start.3 = (bf16[32,112,128]{2,1,0:T(8,128)(2,1)}, bf16[32,112,128]{2,1,0:T(8,128)(2,1)S(1)}, u32[]{:S(2)}) copy-start(bf16[32,112,128]{2,1,0:T(8,128)(2,1)S(1)} %collective-permute-done.4.refs_3_.refs_6_) | copy-start | bytes 2752516
  76.2 19.0 %collective-permute-start.1 = (bf16[32,96,128]{2,1,0:T(8,128)(2,1)S(1)}, bf16[32,96,128]{2,1,0:T(8,128)(2,1)}, u32[]{:S(2)}, u32[]{:S(2)}) collective-permute-start(bf16[32,96,128]{2,1,0:T(8,128)(2,1)S(1)} %all-to-all-done.1.refs_3_), channel_id=1, source_target_pairs={{64,0},{72,8},{128,64},{136,72},{200,128},{192,136},{8,192},{0,200... | collective-permute-start | bytes 2359304 | tf_op jit(solution)/shard_map/ppermute | solution.py:196
  77.8 0.9 copy-start.4
  84.0 25.4 %copy-start.2 = (s32[512,1]{1,0:T(8,128)S(1)}, s32[512,1]{1,0:T(8,128)}, u32[]{:S(2)}) copy-start(s32[512,1]{1,0:T(8,128)} %get-tuple-element.10) | copy-start | bytes 6148
  105.8 3.8 %collective-permute-start.6 = (f32[2,512]{1,0:T(2,128)S(1)}, f32[2,512]{1,0:T(2,128)S(1)}, u32[]{:S(2)}, u32[]{:S(2)}) collective-permute-start(f32[2,512]{1,0:T(2,128)S(1)} %get-tuple-element.11), channel_id=1, source_target_pairs={{0,8},{8,0},{64,72},{72,64},{128,136},{136,128},{192,200},{200,192... | collective-permute-start | bytes 12296 | tf_op jit(solution)/shard_map/ppermute | solution.py:196
  106.9 3.3 %collective-permute-start.8 = (f32[2,512]{1,0:T(2,128)S(1)}, f32[2,512]{1,0:T(2,128)S(1)}, u32[]{:S(2)}, u32[]{:S(2)}) collective-permute-start(f32[2,512]{1,0:T(2,128)S(1)} %get-tuple-element.12), channel_id=1, source_target_pairs={{0,192},{8,200},{64,0},{72,8},{128,64},{136,72},{192,128},{200,136... | collective-permute-start | bytes 12296 | tf_op jit(solution)/shard_map/ppermute | solution.py:196
  109.4 4.3 %collective-permute-start.7 = (f32[2,512]{1,0:T(2,128)S(1)}, f32[2,512]{1,0:T(2,128)S(1)}, u32[]{:S(2)}, u32[]{:S(2)}) collective-permute-start(f32[2,512]{1,0:T(2,128)S(1)} %get-tuple-element.13), channel_id=1, source_target_pairs={{0,64},{8,72},{64,128},{72,136},{128,200},{136,192},{192,8},{200,0... | collective-permute-start | bytes 12296 | tf_op jit(solution)/shard_map/ppermute | solution.py:196
  115.3 17.2 %all-to-all-start.2 = ((f32[32,1,32]{2,1,0:T(1,128)}), f32[32,1,32]{2,1,0:T(1,128)S(1)}, u32[]{:S(2)}, u32[]{:S(2)}) async-start(f32[32,1,32]{2,1,0:T(1,128)} %copy.12), calls=%async_computation.2 | async-start | bytes 32768 | tf_op jit(solution)/shard_map/all_to_all | solution.py:204

commit v2 on v1

v2 whole, which is shorter than its diff:
```python
import functools

import jax
import jax.numpy as jnp
from jax import lax
from jax.experimental import pallas as pl
from jax.experimental.pallas import tpu as pltpu
from jax.sharding import Mesh, PartitionSpec as P

D = 768
ROWS = 512
GROUPS = 32
HALF = 16
SLOTS = 2 * HALF
PART = GROUPS * HALF
PARTS = D // 128
SIZE = {"x": 4, "y": 4, "c": 2, "z": 8}
LIMIT = 60 * 1024 * 1024
NT = (((1,), (1,)), ((), ()))
NN = (((1,), (0,)), ((), ()))
TN = (((0,), (0,)), ((), ()))
BLOCKS = ("o", "s", "b", "z")
FINALS = tuple(block + half for block in BLOCKS for half in "01")


def dot(a, b, dims):
    return lax.dot_general(a, b, dims, preferred_element_type=jnp.float32)


def iota(shape, axis):
    return lax.broadcasted_iota(jnp.int32, shape, axis)


def bits(mask):
    return mask.astype(jnp.float32).astype(jnp.bfloat16)


def three_parts(value):
    parts = []
    for _ in range(3):
        part = value.astype(jnp.bfloat16)
        parts.append(part)
        value = value - part.astype(jnp.float32)
    return parts


def place_rows(unit, slot_at, half, out_ref):
    slot, at = slot_at & (SLOTS - 1), slot_at // SLOTS
    row = jnp.where(slot // HALF == half, at * HALF + slot % HALF, -1)
    chosen = bits(iota((PART, ROWS), 0) == row)
    moved = dot(chosen, unit, NN).astype(jnp.bfloat16)
    for part in range(PARTS):
        out_ref[:, part * HALF : (part + 1) * HALF, :] = moved[
            :, part * 128 : (part + 1) * 128
        ].reshape(GROUPS, HALF, 128)
    return chosen


def pack_first(emb_ref, ids_ref, rank_ref, out_ref, unit_ref, pos_ref):
    rows = emb_ref[...]
    norms = jnp.sum(rows * rows, axis=1, keepdims=True)
    unit = (rows * lax.rsqrt(norms + 1e-06)).astype(jnp.bfloat16)
    unit_ref[...] = unit

    target = ids_ref[...]
    member = (iota((GROUPS, ROWS), 0) == target).astype(jnp.float32)
    earlier = bits(iota((ROWS, ROWS), 0) < iota((ROWS, ROWS), 1))
    before = dot(member.astype(jnp.bfloat16), earlier, NN)
    slot = jnp.sum(before * member, axis=0, keepdims=True).astype(jnp.int32)
    position = target * SLOTS + slot
    pos_ref[...] = position

    first = place_rows(unit, position, 0, out_ref)
    second = bits(
        iota((PART, ROWS), 0) == jnp.where(slot >= HALF, target * HALF + slot - HALF, -1)
    )
    rank = rank_ref[...]
    line = iota((128, ROWS), 0)
    ranks = jnp.zeros((PART, 128), jnp.float32)
    for half, chosen in enumerate((first, second)):
        parts = jnp.zeros((128, ROWS), jnp.int32)
        for index, part in enumerate(((rank >> 14) - 128, (rank >> 7) & 127, rank & 127)):
            parts = jnp.where(line == 3 * half + index, part, parts)
        ranks += dot(chosen, parts.astype(jnp.float32).astype(jnp.bfloat16), NT)
    out_ref[:, D // 8 :, :] = ranks.astype(jnp.bfloat16).reshape(GROUPS, HALF, 128)


def pack_second(unit_ref, pos_ref, out_ref):
    place_rows(unit_ref[...], pos_ref[...], 1, out_ref)


def vmem(count):
    return [pl.BlockSpec(memory_space=pltpu.VMEM)] * count


def call(kernel, name, shapes, *operands, flops=0):
    shapes = tuple(jax.ShapeDtypeStruct(shape, dtype) for shape, dtype in shapes)
    out = pl.pallas_call(
        kernel,
        out_shape=shapes,
        in_specs=vmem(len(operands)),
        out_specs=tuple(vmem(len(shapes))),
        compiler_params=pltpu.CompilerParams(vmem_limit_bytes=LIMIT),
        cost_estimate=pl.CostEstimate(
            flops=flops,
            bytes_accessed=sum(array.size * array.dtype.itemsize for array in operands),
            transcendentals=0,
        ),
        name=name,
    )(*operands)
    return out[0] if len(shapes) == 1 else out


def keys_of(ref):
    wide = [
        ref[:, part * HALF : (part + 1) * HALF, :].reshape(PART, 128) for part in range(PARTS)
    ]
    return jnp.concatenate(wide, axis=1)


def rank_weights(shape, axis, start):
    place = iota(shape, axis) - start
    weights = jnp.where(place == 0, 16384.0, jnp.where(place == 1, 128.0, 1.0))
    return jnp.where((place >= 0) & (place < 3), weights, 0.0).astype(jnp.bfloat16)


def homeward(best):
    stacked = jnp.concatenate(best, axis=0)
    widen = bits(iota((8, 128), 1) // HALF == iota((8, 128), 0))
    own_lane = iota((PART, 128), 1) % HALF == iota((PART, 128), 0) % HALF
    gather = bits(iota((GROUPS, PART), 1) // HALF == iota((GROUPS, PART), 0))
    total = jnp.zeros((GROUPS, 128), jnp.float32)
    for part in three_parts(stacked):
        lanes = jnp.where(own_lane, dot(part, widen, TN), 0.0).astype(jnp.bfloat16)
        total += dot(gather, lanes, NN)
    return total


def score_kernel(names, pairs, last, *refs):
    data = dict(zip(names, refs))
    carried = None if len(refs) == len(names) + 1 else refs[len(names)]
    out_ref = refs[-1]
    used = sorted({name for pair in pairs for name in pair[:2]})
    keys = {name: keys_of(data[name]) for name in used}
    by_row, by_lane = {}, {}
    for name in used:
        tile = data[name[0] + "0"][:, D // 8 :, :].reshape(PART, 128)
        start = 3 * int(name[1])
        by_row[name] = dot(tile, rank_weights((128, 128), 0, start), NN)
        by_lane[name] = dot(rank_weights((8, 128), 1, start), tile, NT)[0:1]
    best_row, best_lane = {}, {}
    for rows, columns, forward, backward in pairs:
        scores = dot(keys[rows], keys[columns], NT)
        row_rank = jnp.concatenate([by_row[rows]] * 4, axis=1)
        lane_rank = by_lane[columns]
        if forward:
            kept = jnp.where(lane_rank < row_rank, scores, -1.0)
            folded = functools.reduce(
                jnp.maximum, [kept[:, 128 * i : 128 * (i + 1)] for i in range(4)]
            )
            best_row[rows] = jnp.maximum(best_row[rows], folded) if rows in best_row else folded
        if backward:
            kept = jnp.where(row_rank < lane_rank, scores, -1.0)
            folded = jnp.max(kept, axis=0, keepdims=True)
            if columns in best_lane:
                folded = jnp.maximum(best_lane[columns], folded)
            best_lane[columns] = folded
    best = []
    for index, name in enumerate(FINALS):
        value = jnp.full((1, PART), -1.0) if carried is None else carried[index : index + 1, :]
        if name in best_lane:
            value = jnp.maximum(value, best_lane[name])
        if name in best_row:
            value = jnp.maximum(value, jnp.max(best_row[name].T, axis=0, keepdims=True))
        best.append(value)
    if last:
        out_ref[...] = homeward(best).reshape(GROUPS, 1, 128)
    else:
        out_ref[...] = jnp.concatenate(best, axis=0)


def score(blocks, pairs, carried, last, name):
    used = {half for pair in pairs for half in pair[:2]}
    names = tuple(sorted(used | {half[0] + "0" for half in used}))
    shape = ((GROUPS, 1, 128) if last else (8, PART), jnp.float32)
    operands = [blocks[half] for half in names] + ([] if carried is None else [carried])
    return call(
        functools.partial(score_kernel, names, pairs, last),
        name,
        [shape],
        *operands,
        flops=2 * len(pairs) * PART * PART * D,
    )


FIRST = (
    ("o0", "o0", True, False),
    ("o0", "s0", True, False),
    ("o0", "b0", True, True),
    ("s0", "b0", True, True),
    ("z0", "b0", True, True),
)
SECOND = (
    ("o1", "o1", True, False),
    ("o0", "o1", True, True),
    ("o1", "b0", True, True),
    ("o1", "s1", True, False),
    ("o0", "s1", True, True),
    ("s1", "b0", True, True),
)
THIRD = (
    ("o0", "b1", True, True),
    ("o1", "b1", True, True),
    ("s0", "b1", True, True),
    ("s1", "b1", True, True),
    ("z0", "b1", True, True),
    ("z1", "b0", True, True),
    ("z1", "b1", True, True),
)


def finish_kernel(own_ref, swap_ref, next_ref, last_ref, pos_ref, out_ref):
    block = iota((GROUPS, 128), 1) // SLOTS
    mine = last_ref[...].reshape(GROUPS, 128)
    for index, ref in enumerate((own_ref, swap_ref, next_ref)):
        mine = jnp.where(block == index, ref[...].reshape(GROUPS, 128), mine)
    position = pos_ref[...]
    member = bits(iota((GROUPS, ROWS), 0) == position // SLOTS)
    found = jnp.zeros((128, ROWS), jnp.float32)
    for part in three_parts(mine):
        found += dot(part, member, TN)
    best = functools.reduce(
        jnp.maximum, [found[SLOTS * index : SLOTS * (index + 1)] for index in range(4)]
    )
    here = iota((SLOTS, ROWS), 0) == (position & (SLOTS - 1))
    out_ref[...] = jnp.sum(jnp.where(here, best, 0.0), axis=0, keepdims=True)


FROM_NEXT = [
    (((x + 1) % 4) * 2 + (c if x < 2 else 1 - c), x * 2 + c) for x in range(4) for c in range(2)
]
FROM_LAST = [(((x - 1) % 4) * 2 + c, x * 2 + c) for x in range(4) for c in range(2)]
SWAP = [(x * 2 + 1 - c, x * 2 + c) for x in range(4) for c in range(2)]


def back(pairs):
    return [(there, here) for here, there in pairs]


def send(array, pairs):
    return lax.ppermute(array, ("x", "c"), pairs)


def to_home(array):
    return lax.all_to_all(array, ("y", "z"), split_axis=0, concat_axis=0, tiled=True)


def on_device(embeddings, cluster_ids, ranks):
    bf16 = jnp.bfloat16
    first, unit, position = call(
        pack_first,
        "pack_first",
        [((GROUPS, D // 8 + HALF, 128), bf16), ((ROWS, D), bf16), ((1, ROWS), jnp.int32)],
        embeddings,
        cluster_ids.reshape(1, ROWS),
        ranks.reshape(1, ROWS),
        flops=2 * PART * ROWS * D,
    )
    second = call(
        pack_second,
        "pack_second",
        [((GROUPS, D // 8, 128), bf16)],
        unit,
        position,
        flops=2 * PART * ROWS * D,
    )
    blocks = {}
    for half, packed in zip("01", (first, second)):
        blocks["o" + half] = home = to_home(packed)
        blocks["s" + half] = send(home, SWAP)
        blocks["b" + half] = send(home, FROM_NEXT)
        blocks["z" + half] = send(home, FROM_LAST)
    best = score(blocks, FIRST, None, False, "score_first")
    best = score(blocks, SECOND, best, False, "score_second")
    own = to_home(score(blocks, THIRD, best, True, "score_third"))
    nearest = call(
        finish_kernel,
        "finish",
        [((1, ROWS), jnp.float32)],
        own,
        send(own, back(SWAP)),
        send(own, back(FROM_NEXT)),
        send(own, back(FROM_LAST)),
        position,
    )
    return nearest.reshape(ROWS)


def solution(mesh):
    fine = Mesh(mesh.devices.reshape(tuple(SIZE.values())), tuple(SIZE))
    rows = P(tuple(SIZE))
    return jax.shard_map(
        on_device,
        mesh=fine,
        in_specs=(P(tuple(SIZE), None), P(tuple(SIZE), None), rows),
        out_specs=rows,
        check_vma=False,
    )
```

time: 137 us -> 125 us (0.912)
  blocking collectives: 34 us -> 15.2 us
  local copies, waits for them, and re-layouts: 9.32 us -> 2.11 us
  Pallas kernels: 20 us -> 26.8 us
  starting transfers between devices: 32.6 us -> 37.8 us
  waiting for transfers between devices: 39.3 us -> 41.7 us
    all_to_all x1, blocking collectives: 34 us -> 15.2 us  [to_home(): lax.all_to_all(array, ('y', 'z'), split_axis=0, concat_axis=0, tiled=True)]
    all_to_all x2, waiting for transfers between devices: 24 us -> 34.8 us  [to_home(): lax.all_to_all(array, ('y', 'z'), split_axis=0, concat_axis=0, tiled=True)]
    ppermute x9, waiting for transfers between devices: 15.3 us -> 6.96 us  [send(): return lax.ppermute(array, ('x', 'c'), pairs)]
    pallas_call x3 -> x6, Pallas kernels: 20 us -> 26.8 us  [call(): pl.pallas_call(kernel, out_shape=shapes, in_specs=vmem(len(operands)), ou...]
    all_to_all x2, starting transfers between devices: 17.1 us -> 20.5 us  [to_home(): lax.all_to_all(array, ('y', 'z'), split_axis=0, concat_axis=0, tiled=True)]
    gather x1 -> x0, local copies, waits for them, and re-layouts: 3.42 us -> none  [on_device(): return home[position[:, 0]]]
    ppermute x9, starting transfers between devices: 15.6 us -> 17.3 us  [send(): return lax.ppermute(array, ('x', 'c'), pairs)]
    reshape x3 -> x0, local copies, waits for them, and re-layouts: 1.69 us -> none  [the longest x1 1.53 us: on_device(): ranks.reshape(ROWS, 1)]
  transfers between devices with their start and end apart: 11 -> 11, of which waited for: 6 -> 4; matrix products, arithmetic and copies ran while one was open for 1% -> 0% of each run, Pallas kernels for 4% -> 11%
where the time goes in v2:
time: 125 us; the launch traced here: 124 us
  waiting for transfers between devices  41.7 us (33%)
  starting transfers between devices  37.8 us (30%)
  Pallas kernels  26.8 us (21%)
  blocking collectives  15.2 us (12%)
  local copies, waits for them, and re-layouts  2.11 us (2%)
    all_to_all x2, waiting for transfers between devices, to_home(): lax.all_to_all(array, ('y', 'z'), split_axis=0, concat_axis=0, tiled=True)  34.8 us
    pallas_call x6, Pallas kernels, call(): pl.pallas_call(kernel, out_shape=shapes, in_specs=vmem(len(operands)), ou...  26.8 us
    all_to_all x2, starting transfers between devices, to_home(): lax.all_to_all(array, ('y', 'z'), split_axis=0, concat_axis=0, tiled=True)  20.5 us
    ppermute x9, starting transfers between devices, send(): return lax.ppermute(array, ('x', 'c'), pairs)  17.3 us
    all_to_all x1, blocking collectives, to_home(): lax.all_to_all(array, ('y', 'z'), split_axis=0, concat_axis=0, tiled=True)  15.2 us
    ppermute x9, waiting for transfers between devices, send(): return lax.ppermute(array, ('x', 'c'), pairs)  6.96 us
  transfers between devices with their start and end apart: 11, of which 4 were waited for; matrix products, arithmetic and copies ran while one was open for 0% of the time, Pallas kernels for 11%

profile of v2, /device:TPU:1, one launch (start us, length us, event | category | flops | bytes accessed | tf_op | source)
XLA Modules:
  0.0 123.7 jit_solution(6116485343437346469)
XLA Ops:
  0.0 3.5 %pack_first.1 = (bf16[32,112,128]{2,1,0:T(8,128)(2,1)}, bf16[512,768]{1,0:T(8,128)(2,1)}, s32[1,512]{1,0:T(1,128)}) custom-call(f32[512,768]{1,0:T(8,128)} %emb_ref.1, s32[1,512]{1,0:T(1,128)} %bitcast.3, s32[1,512]{1,0:T(1,128)} %bitcast.4), custom_call_target="tpu_custom_call" | custom-call | flops 402653184 | bytes 1576960 | tf_op jit(solution)/shard_map/pack_first/pallas_call | solution.py:98
  3.5 12.0 %all-to-all-start = ((bf16[32,112,128]{2,1,0:T(8,128)(2,1)}), bf16[32,112,128]{2,1,0:T(8,128)(2,1)S(1)}, u32[]{:S(2)}, u32[]{:S(2)}) async-start(bf16[32,112,128]{2,1,0:T(8,128)(2,1)} %get-tuple-element.8), calls=%async_computation | async-start | bytes 1835008 | tf_op jit(solution)/shard_map/all_to_all | solution.py:255
  15.5 2.6 %pack_second.1 = bf16[32,96,128]{2,1,0:T(8,128)(2,1)} custom-call(bf16[512,768]{1,0:T(8,128)(2,1)} %get-tuple-element.9.unit_ref, s32[1,512]{1,0:T(1,128)} %get-tuple-element.10.pos_ref), custom_call_target="tpu_custom_call" | custom-call | flops 402653184 | bytes 788480 | tf_op jit(solution)/shard_map/pack_second/pallas_call | solution.py:98
  18.1 19.3 %all-to-all-done.refs_1_.refs_2_ = bf16[32,112,128]{2,1,0:T(8,128)(2,1)S(1)} async-done(((bf16[32,112,128]{2,1,0:T(8,128)(2,1)}), bf16[32,112,128]{2,1,0:T(8,128)(2,1)S(1)}, u32[]{:S(2)}, u32[]{:S(2)}) %all-to-all-start) | async-done | bytes 917536 | tf_op jit(solution)/shard_map/all_to_all | solution.py:255
  37.5 0.0 copy-start
  37.5 8.5 %all-to-all-start.1 = ((bf16[32,96,128]{2,1,0:T(8,128)(2,1)}), bf16[32,96,128]{2,1,0:T(8,128)(2,1)S(1)}, u32[]{:S(2)}, u32[]{:S(2)}) async-start(bf16[32,96,128]{2,1,0:T(8,128)(2,1)} %pack_second.1), calls=%async_computation.1 | async-start | bytes 1572864 | tf_op jit(solution)/shard_map/all_to_all | solution.py:255
  45.9 1.3 %collective-permute-start.4 = (bf16[32,112,128]{2,1,0:T(8,128)(2,1)S(1)}, bf16[32,112,128]{2,1,0:T(8,128)(2,1)S(1)}, u32[]{:S(2)}, u32[]{:S(2)}) collective-permute-start(bf16[32,112,128]{2,1,0:T(8,128)(2,1)S(1)} %all-to-all-done.refs_1_.refs_2_), channel_id=1, source_target_pairs={{192,0},{200,8},{0,64},{8,72},{64,128},{72,136},{128,192},{136,200... | collective-permute-start | bytes 2752520 | tf_op jit(solution)/shard_map/ppermute | solution.py:251
  47.2 1.7 %collective-permute-start.2 = (bf16[32,112,128]{2,1,0:T(8,128)(2,1)S(1)}, bf16[32,112,128]{2,1,0:T(8,128)(2,1)S(1)}, u32[]{:S(2)}, u32[]{:S(2)}) collective-permute-start(bf16[32,112,128]{2,1,0:T(8,128)(2,1)S(1)} %all-to-all-done.refs_1_.refs_2_), channel_id=1, source_target_pairs={{8,0},{0,8},{72,64},{64,72},{136,128},{128,136},{200,192},{192,200... | collective-permute-start | bytes 2752520 | tf_op jit(solution)/shard_map/ppermute | solution.py:251
  49.0 1.4 %collective-permute-start = (bf16[32,112,128]{2,1,0:T(8,128)(2,1)S(1)}, bf16[32,112,128]{2,1,0:T(8,128)(2,1)}, u32[]{:S(2)}, u32[]{:S(2)}) collective-permute-start(bf16[32,112,128]{2,1,0:T(8,128)(2,1)S(1)} %all-to-all-done.refs_1_.refs_2_), channel_id=1, source_target_pairs={{64,0},{72,8},{128,64},{136,72},{200,128},{192,136},{8,192},{0,200... | collective-permute-start | bytes 2752520 | tf_op jit(solution)/shard_map/ppermute | solution.py:251
  50.3 15.4 %all-to-all-done.1.refs_2_.refs_3_ = bf16[32,96,128]{2,1,0:T(8,128)(2,1)S(1)} async-done(((bf16[32,96,128]{2,1,0:T(8,128)(2,1)}), bf16[32,96,128]{2,1,0:T(8,128)(2,1)S(1)}, u32[]{:S(2)}, u32[]{:S(2)}) %all-to-all-start.1) | async-done | bytes 786464 | tf_op jit(solution)/shard_map/all_to_all | solution.py:255
  65.7 0.0 copy-start.1
  65.7 4.5 %collective-permute-start.3 = (bf16[32,96,128]{2,1,0:T(8,128)(2,1)S(1)}, bf16[32,96,128]{2,1,0:T(8,128)(2,1)}, u32[]{:S(2)}, u32[]{:S(2)}) collective-permute-start(bf16[32,96,128]{2,1,0:T(8,128)(2,1)S(1)} %all-to-all-done.1.refs_2_.refs_3_), channel_id=1, source_target_pairs={{8,0},{0,8},{72,64},{64,72},{136,128},{128,136},{200,192},{192,200... | collective-permute-start | bytes 2359304 | tf_op jit(solution)/shard_map/ppermute | solution.py:251
  70.2 1.2 collective-permute-start.5
  71.4 0.0 collective-permute-done.4.refs_3_.refs_6_
  71.4 0.0 copy-start.6
  71.4 1.6 %collective-permute-start.1 = (bf16[32,96,128]{2,1,0:T(8,128)(2,1)S(1)}, bf16[32,96,128]{2,1,0:T(8,128)(2,1)}, u32[]{:S(2)}, u32[]{:S(2)}) collective-permute-start(bf16[32,96,128]{2,1,0:T(8,128)(2,1)S(1)} %all-to-all-done.1.refs_2_.refs_3_), channel_id=1, source_target_pairs={{64,0},{72,8},{128,64},{136,72},{200,128},{192,136},{8,192},{0,200... | collective-permute-start | bytes 2359304 | tf_op jit(solution)/shard_map/ppermute | solution.py:251
  73.1 0.0 collective-permute-done.2.refs_2_.refs_3_.refs_4_
  73.1 0.0 copy-start.7
  73.1 0.0 collective-permute-done.refs_0_
  73.1 0.0 copy-done
  73.1 0.0 copy-done.6
  73.1 0.9 copy-done.7
  74.0 5.3 %score_first.1.refs_5_ = f32[8,512]{1,0:T(8,128)} custom-call(bf16[32,112,128]{2,1,0:T(8,128)(2,1)} %collective-permute-done.refs_0_, bf16[32,112,128]{2,1,0:T(8,128)(2,1)} %copy-done, bf16[32,112,128]{2,1,0:T(8,128)(2,1)} %copy-done.7, bf16[32,112,128]{2,1,0:T(8,128)(2,1)} %copy-done.6), custom_call_target="tpu_custom_call" | custom-call | flops 2013265920 | bytes 3670016 | tf_op jit(solution)/shard_map/score_first/pallas_call | solution.py:98
  79.3 0.0 copy-done.1
  79.3 0.0 collective-permute-done.3.refs_4_.refs_5_
  79.3 5.8 %score_second.1.refs_8_ = f32[8,512]{1,0:T(8,128)} custom-call(bf16[32,112,128]{2,1,0:T(8,128)(2,1)} %collective-permute-done.refs_0_, bf16[32,112,128]{2,1,0:T(8,128)(2,1)} %copy-done, bf16[32,96,128]{2,1,0:T(8,128)(2,1)} %copy-done.1, bf16[32,112,128]{2,1,0:T(8,128)(2,1)} %copy-done.7, bf16[32,96,128]{2,1,0:T(8,128)(2,1)} %collective-permute-done.3.refs_4_.refs_5_, ...), custom_call_target="tpu_custom_call" | custom-call | flops 2415919104 | bytes 4341760 | tf_op jit(solution)/shard_map/score_second/pallas_call | solution.py:98
  85.1 5.6 %collective-permute-done.5.refs_7_ = bf16[32,96,128]{2,1,0:T(8,128)(2,1)} collective-permute-done((bf16[32,96,128]{2,1,0:T(8,128)(2,1)S(1)}, bf16[32,96,128]{2,1,0:T(8,128)(2,1)}, u32[]{:S(2)}, u32[]{:S(2)}) %collective-permute-start.5) | collective-permute-done | bytes 786464 | tf_op jit(solution)/shard_map/ppermute | solution.py:251
  90.7 0.0 collective-permute-done.1.refs_1_
  90.7 7.9 %score_third.1 = f32[32,1,128]{2,1,0:T(1,128)} custom-call(bf16[32,112,128]{2,1,0:T(8,128)(2,1)} %collective-permute-done.refs_0_, bf16[32,96,128]{2,1,0:T(8,128)(2,1)} %collective-permute-done.1.refs_1_, bf16[32,112,128]{2,1,0:T(8,128)(2,1)} %copy-done, bf16[32,96,128]{2,1,0:T(8,128)(2,1)} %copy-done.1, bf16[32,112,128]{2,1,0:T(8,128)(2,1)} %copy-done.7, ...), custom_call_target="tpu_custom_call" | custom-call | flops 2818572288 | bytes 6832128 | tf_op jit(solution)/shard_map/score_third/pallas_call | solution.py:98
  98.6 15.2 %all_to_all.15.own_ref = f32[32,1,128]{2,1,0:T(1,128)S(1)} all-to-all(f32[32,1,128]{2,1,0:T(1,128)} %score_third.1), channel_id=1, replica_groups=mesh['x'=4,'y'=4,'c'=2,'z'=8] {'y','z'}, dimensions={0} | all-to-all | bytes 32768 | tf_op jit(solution)/shard_map/all_to_all | solution.py:255
  113.8 0.0 copy-start.2
  113.8 2.5 %collective-permute-start.8 = (f32[32,1,128]{2,1,0:T(1,128)S(1)}, f32[32,1,128]{2,1,0:T(1,128)S(1)}, u32[]{:S(2)}, u32[]{:S(2)}) collective-permute-start(f32[32,1,128]{2,1,0:T(1,128)S(1)} %all_to_all.15.own_ref), channel_id=1, source_target_pairs={{0,192},{8,200},{64,0},{72,8},{128,64},{136,72},{192,128},{200,136... | collective-permute-start | bytes 49160 | tf_op jit(solution)/shard_map/ppermute | solution.py:251
  116.4 0.0 collective-permute-start.7
  116.4 3.1 %collective-permute-start.6 = (f32[32,1,128]{2,1,0:T(1,128)S(1)}, f32[32,1,128]{2,1,0:T(1,128)S(1)}, u32[]{:S(2)}, u32[]{:S(2)}) collective-permute-start(f32[32,1,128]{2,1,0:T(1,128)S(1)} %all_to_all.15.own_ref), channel_id=1, source_target_pairs={{0,8},{8,0},{64,72},{72,64},{128,136},{136,128},{192,200},{200,192... | collective-permute-start | bytes 49160 | tf_op jit(solution)/shard_map/ppermute | solution.py:251
  119.4 0.0 collective-permute-done.8.last_ref
  119.4 0.0 copy-start.3
  119.4 1.4 %collective-permute-done.7.next_ref = f32[32,1,128]{2,1,0:T(1,128)S(1)} collective-permute-done((f32[32,1,128]{2,1,0:T(1,128)S(1)}, f32[32,1,128]{2,1,0:T(1,128)S(1)}, u32[]{:S(2)}, u32[]{:S(2)}) %collective-permute-start.7) | collective-permute-done | bytes 16416 | tf_op jit(solution)/shard_map/ppermute | solution.py:251
  120.8 0.0 copy-start.4
  120.8 0.0 collective-permute-done.6.swap_ref
  120.8 0.0 copy-done.2
  120.8 0.0 copy-done.3
  120.8 0.6 copy-done.4
  121.4 0.0 copy-start.5
  121.4 0.6 copy-done.5
  122.0 1.7 %finish.1 = f32[1,512]{1,0:T(1,128)} custom-call(f32[32,1,128]{2,1,0:T(1,128)} %copy-done.2, f32[32,1,128]{2,1,0:T(1,128)} %copy-done.5, f32[32,1,128]{2,1,0:T(1,128)} %copy-done.4, f32[32,1,128]{2,1,0:T(1,128)} %copy-done.3, s32[1,512]{1,0:T(1,128)} %get-tuple-element.10.pos_ref), custom_call_target="tpu_custom_call" | custom-call | bytes 67584 | tf_op jit(solution)/shard_map/finish/pallas_call | solution.py:98
Async XLA Ops:
  3.5 34.0 %all-to-all-start = ((bf16[32,112,128]{2,1,0:T(8,128)(2,1)}), bf16[32,112,128]{2,1,0:T(8,128)(2,1)S(1)}, u32[]{:S(2)}, u32[]{:S(2)}) async-start(bf16[32,112,128]{2,1,0:T(8,128)(2,1)} %get-tuple-element.8), calls=%async_computation | async-start | bytes 1835008 | tf_op jit(solution)/shard_map/all_to_all | solution.py:255
  37.5 35.6 %copy-start = (bf16[32,112,128]{2,1,0:T(8,128)(2,1)}, bf16[32,112,128]{2,1,0:T(8,128)(2,1)S(1)}, u32[]{:S(2)}) copy-start(bf16[32,112,128]{2,1,0:T(8,128)(2,1)S(1)} %all-to-all-done.refs_1_.refs_2_) | copy-start | bytes 2752516
  37.5 28.3 %all-to-all-start.1 = ((bf16[32,96,128]{2,1,0:T(8,128)(2,1)}), bf16[32,96,128]{2,1,0:T(8,128)(2,1)S(1)}, u32[]{:S(2)}, u32[]{:S(2)}) async-start(bf16[32,96,128]{2,1,0:T(8,128)(2,1)} %pack_second.1), calls=%async_computation.1 | async-start | bytes 1572864 | tf_op jit(solution)/shard_map/all_to_all | solution.py:255
  45.9 25.5 %collective-permute-start.4 = (bf16[32,112,128]{2,1,0:T(8,128)(2,1)S(1)}, bf16[32,112,128]{2,1,0:T(8,128)(2,1)S(1)}, u32[]{:S(2)}, u32[]{:S(2)}) collective-permute-start(bf16[32,112,128]{2,1,0:T(8,128)(2,1)S(1)} %all-to-all-done.refs_1_.refs_2_), channel_id=1, source_target_pairs={{192,0},{200,8},{0,64},{8,72},{64,128},{72,136},{128,192},{136,200... | collective-permute-start | bytes 2752520 | tf_op jit(solution)/shard_map/ppermute | solution.py:251
  47.2 25.9 %collective-permute-start.2 = (bf16[32,112,128]{2,1,0:T(8,128)(2,1)S(1)}, bf16[32,112,128]{2,1,0:T(8,128)(2,1)S(1)}, u32[]{:S(2)}, u32[]{:S(2)}) collective-permute-start(bf16[32,112,128]{2,1,0:T(8,128)(2,1)S(1)} %all-to-all-done.refs_1_.refs_2_), channel_id=1, source_target_pairs={{8,0},{0,8},{72,64},{64,72},{136,128},{128,136},{200,192},{192,200... | collective-permute-start | bytes 2752520 | tf_op jit(solution)/shard_map/ppermute | solution.py:251
  49.0 24.1 %collective-permute-start = (bf16[32,112,128]{2,1,0:T(8,128)(2,1)S(1)}, bf16[32,112,128]{2,1,0:T(8,128)(2,1)}, u32[]{:S(2)}, u32[]{:S(2)}) collective-permute-start(bf16[32,112,128]{2,1,0:T(8,128)(2,1)S(1)} %all-to-all-done.refs_1_.refs_2_), channel_id=1, source_target_pairs={{64,0},{72,8},{128,64},{136,72},{200,128},{192,136},{8,192},{0,200... | collective-permute-start | bytes 2752520 | tf_op jit(solution)/shard_map/ppermute | solution.py:251
  65.7 13.6 %copy-start.1 = (bf16[32,96,128]{2,1,0:T(8,128)(2,1)}, bf16[32,96,128]{2,1,0:T(8,128)(2,1)S(1)}, u32[]{:S(2)}) copy-start(bf16[32,96,128]{2,1,0:T(8,128)(2,1)S(1)} %all-to-all-done.1.refs_2_.refs_3_) | copy-start | bytes 2359300
  65.7 13.6 %collective-permute-start.3 = (bf16[32,96,128]{2,1,0:T(8,128)(2,1)S(1)}, bf16[32,96,128]{2,1,0:T(8,128)(2,1)}, u32[]{:S(2)}, u32[]{:S(2)}) collective-permute-start(bf16[32,96,128]{2,1,0:T(8,128)(2,1)S(1)} %all-to-all-done.1.refs_2_.refs_3_), channel_id=1, source_target_pairs={{8,0},{0,8},{72,64},{64,72},{136,128},{128,136},{200,192},{192,200... | collective-permute-start | bytes 2359304 | tf_op jit(solution)/shard_map/ppermute | solution.py:251
  70.2 20.5 %collective-permute-start.5 = (bf16[32,96,128]{2,1,0:T(8,128)(2,1)S(1)}, bf16[32,96,128]{2,1,0:T(8,128)(2,1)}, u32[]{:S(2)}, u32[]{:S(2)}) collective-permute-start(bf16[32,96,128]{2,1,0:T(8,128)(2,1)S(1)} %all-to-all-done.1.refs_2_.refs_3_), channel_id=1, source_target_pairs={{192,0},{200,8},{0,64},{8,72},{64,128},{72,136},{128,192},{136,200... | collective-permute-start | bytes 2359304 | tf_op jit(solution)/shard_map/ppermute | solution.py:251
  71.4 1.7 %copy-start.6 = (bf16[32,112,128]{2,1,0:T(8,128)(2,1)}, bf16[32,112,128]{2,1,0:T(8,128)(2,1)S(1)}, u32[]{:S(2)}) copy-start(bf16[32,112,128]{2,1,0:T(8,128)(2,1)S(1)} %collective-permute-done.4.refs_3_.refs_6_) | copy-start | bytes 2752516
  71.4 19.3 %collective-permute-start.1 = (bf16[32,96,128]{2,1,0:T(8,128)(2,1)S(1)}, bf16[32,96,128]{2,1,0:T(8,128)(2,1)}, u32[]{:S(2)}, u32[]{:S(2)}) collective-permute-start(bf16[32,96,128]{2,1,0:T(8,128)(2,1)S(1)} %all-to-all-done.1.refs_2_.refs_3_), channel_id=1, source_target_pairs={{64,0},{72,8},{128,64},{136,72},{200,128},{192,136},{8,192},{0,200... | collective-permute-start | bytes 2359304 | tf_op jit(solution)/shard_map/ppermute | solution.py:251
  73.1 0.9 copy-start.7
  113.8 7.0 %copy-start.2 = (f32[32,1,128]{2,1,0:T(1,128)}, f32[32,1,128]{2,1,0:T(1,128)S(1)}, u32[]{:S(2)}) copy-start(f32[32,1,128]{2,1,0:T(1,128)S(1)} %all_to_all.15.own_ref) | copy-start | bytes 49156
  113.8 5.6 %collective-permute-start.8 = (f32[32,1,128]{2,1,0:T(1,128)S(1)}, f32[32,1,128]{2,1,0:T(1,128)S(1)}, u32[]{:S(2)}, u32[]{:S(2)}) collective-permute-start(f32[32,1,128]{2,1,0:T(1,128)S(1)} %all_to_all.15.own_ref), channel_id=1, source_target_pairs={{0,192},{8,200},{64,0},{72,8},{128,64},{136,72},{192,128},{200,136... | collective-permute-start | bytes 49160 | tf_op jit(solution)/shard_map/ppermute | solution.py:251
  116.4 4.4 %collective-permute-start.7 = (f32[32,1,128]{2,1,0:T(1,128)S(1)}, f32[32,1,128]{2,1,0:T(1,128)S(1)}, u32[]{:S(2)}, u32[]{:S(2)}) collective-permute-start(f32[32,1,128]{2,1,0:T(1,128)S(1)} %all_to_all.15.own_ref), channel_id=1, source_target_pairs={{0,64},{8,72},{64,128},{72,136},{128,200},{136,192},{192,8},{200,0... | collective-permute-start | bytes 49160 | tf_op jit(solution)/shard_map/ppermute | solution.py:251
  116.4 4.4 %collective-permute-start.6 = (f32[32,1,128]{2,1,0:T(1,128)S(1)}, f32[32,1,128]{2,1,0:T(1,128)S(1)}, u32[]{:S(2)}, u32[]{:S(2)}) collective-permute-start(f32[32,1,128]{2,1,0:T(1,128)S(1)} %all_to_all.15.own_ref), channel_id=1, source_target_pairs={{0,8},{8,0},{64,72},{72,64},{128,136},{136,128},{192,200},{200,192... | collective-permute-start | bytes 49160 | tf_op jit(solution)/shard_map/ppermute | solution.py:251
  119.4 1.4 %copy-start.3 = (f32[32,1,128]{2,1,0:T(1,128)}, f32[32,1,128]{2,1,0:T(1,128)S(1)}, u32[]{:S(2)}) copy-start(f32[32,1,128]{2,1,0:T(1,128)S(1)} %collective-permute-done.8.last_ref) | copy-start | bytes 49156
  120.8 0.6 copy-start.4
  121.4 0.6 copy-start.5

commit v3 on v2

--- a/solution.py
+++ b/solution.py
@@ -15,7 +15,8 @@
 PART = GROUPS * HALF
 PARTS = D // 128
 SIZE = {"x": 4, "y": 4, "c": 2, "z": 8}
-LIMIT = 60 * 1024 * 1024
+EARLY = 1
+LIMIT = 24 * 1024 * 1024
 NT = (((1,), (1,)), ((), ()))
 NN = (((1,), (0,)), ((), ()))
 TN = (((0,), (0,)), ((), ()))
@@ -44,16 +45,19 @@
     return parts
 
 
-def place_rows(unit, slot_at, half, out_ref):
-    slot, at = slot_at & (SLOTS - 1), slot_at // SLOTS
-    row = jnp.where(slot // HALF == half, at * HALF + slot % HALF, -1)
-    chosen = bits(iota((PART, ROWS), 0) == row)
-    moved = dot(chosen, unit, NN).astype(jnp.bfloat16)
-    for part in range(PARTS):
-        out_ref[:, part * HALF : (part + 1) * HALF, :] = moved[
-            :, part * 128 : (part + 1) * 128
-        ].reshape(GROUPS, HALF, 128)
-    return chosen
+def chosen_rows(position, half):
+    slot, group = position & (SLOTS - 1), position // SLOTS
+    row = jnp.where(slot // HALF == half, group * HALF + slot % HALF, -1)
+    return bits(iota((PART, ROWS), 0) == row)
+
+
+def put(moved, out_ref, start):
+    moved = moved.astype(jnp.bfloat16)
+    for part in range(moved.shape[1] // 128):
+        rows = start + part * HALF
+        out_ref[:, rows : rows + HALF, :] = moved[:, part * 128 : (part + 1) * 128].reshape(
+            GROUPS, HALF, 128
+        )
 
 
 def pack_first(emb_ref, ids_ref, rank_ref, out_ref, unit_ref, pos_ref):
@@ -70,10 +74,9 @@
     position = target * SLOTS + slot
     pos_ref[...] = position
 
-    first = place_rows(unit, position, 0, out_ref)
-    second = bits(
-        iota((PART, ROWS), 0) == jnp.where(slot >= HALF, target * HALF + slot - HALF, -1)
-    )
+    first, second = chosen_rows(position, 0), chosen_rows(position, 1)
+    put(dot(first, unit, NN), out_ref, 0)
+    put(dot(second, unit[:, : EARLY * 128], NN), out_ref, D // 8 + HALF)
     rank = rank_ref[...]
     line = iota((128, ROWS), 0)
     ranks = jnp.zeros((PART, 128), jnp.float32)
@@ -82,11 +85,11 @@
         for index, part in enumerate(((rank >> 14) - 128, (rank >> 7) & 127, rank & 127)):
             parts = jnp.where(line == 3 * half + index, part, parts)
         ranks += dot(chosen, parts.astype(jnp.float32).astype(jnp.bfloat16), NT)
-    out_ref[:, D // 8 :, :] = ranks.astype(jnp.bfloat16).reshape(GROUPS, HALF, 128)
+    put(ranks, out_ref, D // 8)
 
 
 def pack_second(unit_ref, pos_ref, out_ref):
-    place_rows(unit_ref[...], pos_ref[...], 1, out_ref)
+    put(dot(chosen_rows(pos_ref[...], 1), unit_ref[:, EARLY * 128 :], NN), out_ref, 0)
 
 
 def vmem(count):
@@ -111,10 +114,17 @@
     return out[0] if len(shapes) == 1 else out
 
 
-def keys_of(ref):
-    wide = [
-        ref[:, part * HALF : (part + 1) * HALF, :].reshape(PART, 128) for part in range(PARTS)
-    ]
+def tile(ref, index):
+    return ref[:, index * HALF : (index + 1) * HALF, :].reshape(PART, 128)
+
+
+def keys_of(data, name):
+    first = data[name[0] + "0"]
+    if name[1] == "0":
+        wide = [tile(first, part) for part in range(PARTS)]
+    else:
+        wide = [tile(first, PARTS + 1 + part) for part in range(EARLY)]
+        wide += [tile(data[name], part) for part in range(PARTS - EARLY)]
     return jnp.concatenate(wide, axis=1)
 
 
@@ -141,13 +151,13 @@
     carried = None if len(refs) == len(names) + 1 else refs[len(names)]
     out_ref = refs[-1]
     used = sorted({name for pair in pairs for name in pair[:2]})
-    keys = {name: keys_of(data[name]) for name in used}
+    keys = {name: keys_of(data, name) for name in used}
     by_row, by_lane = {}, {}
     for name in used:
-        tile = data[name[0] + "0"][:, D // 8 :, :].reshape(PART, 128)
+        ranks = tile(data[name[0] + "0"], PARTS)
         start = 3 * int(name[1])
-        by_row[name] = dot(tile, rank_weights((128, 128), 0, start), NN)
-        by_lane[name] = dot(rank_weights((8, 128), 1, start), tile, NT)[0:1]
+        by_row[name] = dot(ranks, rank_weights((128, 128), 0, start), NN)
+        by_lane[name] = dot(rank_weights((8, 128), 1, start), ranks, NT)[0:1]
     best_row, best_lane = {}, {}
     for rows, columns, forward, backward in pairs:
         scores = dot(keys[rows], keys[columns], NT)
@@ -207,11 +217,11 @@
     ("o1", "s1", True, False),
     ("o0", "s1", True, True),
     ("s1", "b0", True, True),
+    ("o1", "z0", True, True),
+    ("s1", "z0", True, True),
 )
 THIRD = (
-    ("o0", "b1", True, True),
     ("o1", "b1", True, True),
-    ("s0", "b1", True, True),
     ("s1", "b1", True, True),
     ("z0", "b1", True, True),
     ("z1", "b0", True, True),
@@ -260,7 +270,7 @@
     first, unit, position = call(
         pack_first,
         "pack_first",
-        [((GROUPS, D // 8 + HALF, 128), bf16), ((ROWS, D), bf16), ((1, ROWS), jnp.int32)],
+        [((GROUPS, D // 8 + (1 + EARLY) * HALF, 128), bf16), ((ROWS, D), bf16), ((1, ROWS), jnp.int32)],
         embeddings,
         cluster_ids.reshape(1, ROWS),
         ranks.reshape(1, ROWS),
@@ -269,7 +279,7 @@
     second = call(
         pack_second,
         "pack_second",
-        [((GROUPS, D // 8, 128), bf16)],
+        [((GROUPS, D // 8 - EARLY * HALF, 128), bf16)],
         unit,
         position,
         flops=2 * PART * ROWS * D,

time: 125 us -> 125 us (level)
  Pallas kernels: 26.8 us -> 19.2 us
  blocking collectives: 15.2 us -> 19.1 us
  starting transfers between devices: 37.8 us -> 40.9 us
    pallas_call x6, Pallas kernels: 26.8 us -> 19.2 us  [call(): pl.pallas_call(kernel, out_shape=shapes, in_specs=vmem(len(operands)), ou...]
    all_to_all x1, blocking collectives: 15.2 us -> 19.1 us  [to_home(): lax.all_to_all(array, ('y', 'z'), split_axis=0, concat_axis=0, tiled=True)]
    ppermute x9, starting transfers between devices: 17.3 us -> 20.3 us  [send(): return lax.ppermute(array, ('x', 'c'), pairs)]
    unnamed x16 -> x6, local copies, waits for them, and re-layouts: 2.11 us -> 2.77 us
  transfers between devices with their start and end apart: 11 -> 11, of which waited for: 4 -> 6; matrix products, arithmetic and copies ran while one was open for 0% -> 0% of each run, Pallas kernels for 11% -> 9%
where the time goes in v3:
time: 125 us; the launch traced here: 124 us
  waiting for transfers between devices  42.4 us (34%)
  starting transfers between devices  40.9 us (33%)
  Pallas kernels  19.2 us (15%)
  blocking collectives  19.1 us (15%)
  local copies, waits for them, and re-layouts  2.77 us (2%)
    all_to_all x2, waiting for transfers between devices, to_home(): lax.all_to_all(array, ('y', 'z'), split_axis=0, concat_axis=0, tiled=True)  35.6 us
    all_to_all x2, starting transfers between devices, to_home(): lax.all_to_all(array, ('y', 'z'), split_axis=0, concat_axis=0, tiled=True)  20.6 us
    ppermute x9, starting transfers between devices, send(): return lax.ppermute(array, ('x', 'c'), pairs)  20.3 us
    pallas_call x6, Pallas kernels, call(): pl.pallas_call(kernel, out_shape=shapes, in_specs=vmem(len(operands)), ou...  19.2 us
    all_to_all x1, blocking collectives, to_home(): lax.all_to_all(array, ('y', 'z'), split_axis=0, concat_axis=0, tiled=True)  19.1 us
    ppermute x9, waiting for transfers between devices, send(): return lax.ppermute(array, ('x', 'c'), pairs)  6.79 us
    unnamed x6, local copies, waits for them, and re-layouts  2.77 us
  transfers between devices with their start and end apart: 11, of which 6 were waited for; matrix products, arithmetic and copies ran while one was open for 0% of the time, Pallas kernels for 9%

profile of v3, /device:TPU:1, one launch (start us, length us, event | category | flops | bytes accessed | tf_op | source)
XLA Modules:
  0.0 124.4 jit_solution(2036522871820565714)
XLA Ops:
  0.0 0.0 copy-start
  0.0 1.4 %copy-done = f32[512,768]{1,0:T(8,128)S(1)} copy-done((f32[512,768]{1,0:T(8,128)S(1)}, f32[512,768]{1,0:T(8,128)}, u32[]{:S(2)}) %copy-start) | copy-done | bytes 1572888
  1.4 0.0 copy-start.1
  1.4 0.7 copy-done.1
  2.1 0.0 copy-start.2
  2.1 0.7 copy-done.2
  2.8 2.2 %pack_first.1 = (bf16[32,128,128]{2,1,0:T(8,128)(2,1)}, bf16[512,768]{1,0:T(8,128)(2,1)S(1)}, s32[1,512]{1,0:T(1,128)S(1)}) custom-call(f32[512,768]{1,0:T(8,128)S(1)} %copy-done, s32[1,512]{1,0:T(1,128)S(1)} %bitcast.3, s32[1,512]{1,0:T(1,128)S(1)} %bitcast.4), custom_call_target="tpu_custom_call" | custom-call | flops 402653184 | bytes 1576960 | tf_op jit(solution)/shard_map/pack_first/pallas_call | solution.py:101
  5.0 12.0 %all-to-all-start = ((bf16[32,128,128]{2,1,0:T(8,128)(2,1)}), bf16[32,128,128]{2,1,0:T(8,128)(2,1)S(1)}, u32[]{:S(2)}, u32[]{:S(2)}) async-start(bf16[32,128,128]{2,1,0:T(8,128)(2,1)} %get-tuple-element.8), calls=%async_computation | async-start | bytes 2097152 | tf_op jit(solution)/shard_map/all_to_all | solution.py:265
  17.0 1.4 %pack_second.1 = bf16[32,80,128]{2,1,0:T(8,128)(2,1)} custom-call(bf16[512,768]{1,0:T(8,128)(2,1)S(1)} %get-tuple-element.9.unit_ref, s32[1,512]{1,0:T(1,128)S(1)} %get-tuple-element.10.pos_ref), custom_call_target="tpu_custom_call" | custom-call | flops 402653184 | bytes 788480 | tf_op jit(solution)/shard_map/pack_second/pallas_call | solution.py:101
  18.4 23.2 %all-to-all-done.refs_1_.refs_2_ = bf16[32,128,128]{2,1,0:T(8,128)(2,1)S(1)} async-done(((bf16[32,128,128]{2,1,0:T(8,128)(2,1)}), bf16[32,128,128]{2,1,0:T(8,128)(2,1)S(1)}, u32[]{:S(2)}, u32[]{:S(2)}) %all-to-all-start) | async-done | bytes 1048608 | tf_op jit(solution)/shard_map/all_to_all | solution.py:265
  41.6 8.6 %all-to-all-start.1 = ((bf16[32,80,128]{2,1,0:T(8,128)(2,1)}), bf16[32,80,128]{2,1,0:T(8,128)(2,1)S(1)}, u32[]{:S(2)}, u32[]{:S(2)}) async-start(bf16[32,80,128]{2,1,0:T(8,128)(2,1)} %pack_second.1), calls=%async_computation.1 | async-start | bytes 1310720 | tf_op jit(solution)/shard_map/all_to_all | solution.py:265
  50.2 1.3 %collective-permute-start.4 = (bf16[32,128,128]{2,1,0:T(8,128)(2,1)S(1)}, bf16[32,128,128]{2,1,0:T(8,128)(2,1)S(1)}, u32[]{:S(2)}, u32[]{:S(2)}) collective-permute-start(bf16[32,128,128]{2,1,0:T(8,128)(2,1)S(1)} %all-to-all-done.refs_1_.refs_2_), channel_id=1, source_target_pairs={{192,0},{200,8},{0,64},{8,72},{64,128},{72,136},{128,192},{136,200... | collective-permute-start | bytes 3145736 | tf_op jit(solution)/shard_map/ppermute | solution.py:261
  51.5 1.7 %collective-permute-start.2 = (bf16[32,128,128]{2,1,0:T(8,128)(2,1)S(1)}, bf16[32,128,128]{2,1,0:T(8,128)(2,1)}, u32[]{:S(2)}, u32[]{:S(2)}) collective-permute-start(bf16[32,128,128]{2,1,0:T(8,128)(2,1)S(1)} %all-to-all-done.refs_1_.refs_2_), channel_id=1, source_target_pairs={{8,0},{0,8},{72,64},{64,72},{136,128},{128,136},{200,192},{192,200... | collective-permute-start | bytes 3145736 | tf_op jit(solution)/shard_map/ppermute | solution.py:261
  53.3 1.4 %collective-permute-start = (bf16[32,128,128]{2,1,0:T(8,128)(2,1)S(1)}, bf16[32,128,128]{2,1,0:T(8,128)(2,1)}, u32[]{:S(2)}, u32[]{:S(2)}) collective-permute-start(bf16[32,128,128]{2,1,0:T(8,128)(2,1)S(1)} %all-to-all-done.refs_1_.refs_2_), channel_id=1, source_target_pairs={{64,0},{72,8},{128,64},{136,72},{200,128},{192,136},{8,192},{0,200... | collective-permute-start | bytes 3145736 | tf_op jit(solution)/shard_map/ppermute | solution.py:261
  54.6 12.4 %all-to-all-done.1.refs_2_.refs_3_ = bf16[32,80,128]{2,1,0:T(8,128)(2,1)S(1)} async-done(((bf16[32,80,128]{2,1,0:T(8,128)(2,1)}), bf16[32,80,128]{2,1,0:T(8,128)(2,1)S(1)}, u32[]{:S(2)}, u32[]{:S(2)}) %all-to-all-start.1) | async-done | bytes 655392 | tf_op jit(solution)/shard_map/all_to_all | solution.py:265
  67.0 4.8 %collective-permute-start.3 = (bf16[32,80,128]{2,1,0:T(8,128)(2,1)S(1)}, bf16[32,80,128]{2,1,0:T(8,128)(2,1)S(1)}, u32[]{:S(2)}, u32[]{:S(2)}) collective-permute-start(bf16[32,80,128]{2,1,0:T(8,128)(2,1)S(1)} %all-to-all-done.1.refs_2_.refs_3_), channel_id=1, source_target_pairs={{8,0},{0,8},{72,64},{64,72},{136,128},{128,136},{200,192},{192,200... | collective-permute-start | bytes 1966088 | tf_op jit(solution)/shard_map/ppermute | solution.py:261
  71.9 1.2 collective-permute-start.5
  73.1 1.6 %collective-permute-done.4.refs_3_.refs_5_.refs_6_ = bf16[32,128,128]{2,1,0:T(8,128)(2,1)S(1)} collective-permute-done((bf16[32,128,128]{2,1,0:T(8,128)(2,1)S(1)}, bf16[32,128,128]{2,1,0:T(8,128)(2,1)S(1)}, u32[]{:S(2)}, u32[]{:S(2)}) %collective-permute-start.4) | collective-permute-done | bytes 1048608 | tf_op jit(solution)/shard_map/ppermute | solution.py:261
  74.7 4.4 %collective-permute-start.1 = (bf16[32,80,128]{2,1,0:T(8,128)(2,1)S(1)}, bf16[32,80,128]{2,1,0:T(8,128)(2,1)S(1)}, u32[]{:S(2)}, u32[]{:S(2)}) collective-permute-start(bf16[32,80,128]{2,1,0:T(8,128)(2,1)S(1)} %all-to-all-done.1.refs_2_.refs_3_), channel_id=1, source_target_pairs={{64,0},{72,8},{128,64},{136,72},{200,128},{192,136},{8,192},{0,200... | collective-permute-start | bytes 1966088 | tf_op jit(solution)/shard_map/ppermute | solution.py:261
  79.1 0.0 collective-permute-done.2.refs_2_.refs_3_.refs_4_
  79.1 0.0 collective-permute-done.refs_0_
  79.1 4.2 %score_first.1.refs_6_ = f32[8,512]{1,0:T(8,128)S(1)} custom-call(bf16[32,128,128]{2,1,0:T(8,128)(2,1)} %collective-permute-done.refs_0_, bf16[32,128,128]{2,1,0:T(8,128)(2,1)S(1)} %all-to-all-done.refs_1_.refs_2_, bf16[32,128,128]{2,1,0:T(8,128)(2,1)} %collective-permute-done.2.refs_2_.refs_3_.refs_4_, ...), custom_call_target="tpu_custom_call" | custom-call | flops 2013265920 | bytes 4194304 | tf_op jit(solution)/shard_map/score_first/pallas_call | solution.py:101
  83.3 0.0 collective-permute-done.3.refs_4_.refs_5_
  83.3 5.6 %score_second.1.refs_8_ = f32[8,512]{1,0:T(8,128)S(1)} custom-call(bf16[32,128,128]{2,1,0:T(8,128)(2,1)} %collective-permute-done.refs_0_, bf16[32,128,128]{2,1,0:T(8,128)(2,1)S(1)} %all-to-all-done.refs_1_.refs_2_, bf16[32,80,128]{2,1,0:T(8,128)(2,1)S(1)} %all-to-all-done.1.refs_2_.refs_3_, ...), custom_call_target="tpu_custom_call" | custom-call | flops 3221225472 | bytes 5521408 | tf_op jit(solution)/shard_map/score_second/pallas_call | solution.py:101
  88.9 1.0 collective-permute-done.5.refs_7_
  89.9 2.8 %collective-permute-done.1.refs_1_ = bf16[32,80,128]{2,1,0:T(8,128)(2,1)S(1)} collective-permute-done((bf16[32,80,128]{2,1,0:T(8,128)(2,1)S(1)}, bf16[32,80,128]{2,1,0:T(8,128)(2,1)S(1)}, u32[]{:S(2)}, u32[]{:S(2)}) %collective-permute-start.1) | collective-permute-done | bytes 655392 | tf_op jit(solution)/shard_map/ppermute | solution.py:261
  92.7 4.9 %score_third.1 = f32[32,1,128]{2,1,0:T(1,128)S(1)} custom-call(bf16[32,128,128]{2,1,0:T(8,128)(2,1)} %collective-permute-done.refs_0_, bf16[32,80,128]{2,1,0:T(8,128)(2,1)S(1)} %collective-permute-done.1.refs_1_, bf16[32,128,128]{2,1,0:T(8,128)(2,1)S(1)} %all-to-all-done.refs_1_.refs_2_, bf16[32,80,128]{2,1,0:T(8,128)(2,1)S(1)} %all-to-all-done.1.refs_2_.refs_3_, ...), custom_call_target="tpu_custom_call" | custom-call | flops 2013265920 | bytes 6832128 | tf_op jit(solution)/shard_map/score_third/pallas_call | solution.py:101
  97.6 19.1 %all_to_all.15.own_ref = f32[32,1,128]{2,1,0:T(1,128)S(1)} all-to-all(f32[32,1,128]{2,1,0:T(1,128)S(1)} %score_third.1), channel_id=1, replica_groups=mesh['x'=4,'y'=4,'c'=2,'z'=8] {'y','z'}, dimensions={0} | all-to-all | bytes 32768 | tf_op jit(solution)/shard_map/all_to_all | solution.py:265
  116.6 2.5 %collective-permute-start.8 = (f32[32,1,128]{2,1,0:T(1,128)S(1)}, f32[32,1,128]{2,1,0:T(1,128)S(1)}, u32[]{:S(2)}, u32[]{:S(2)}) collective-permute-start(f32[32,1,128]{2,1,0:T(1,128)S(1)} %all_to_all.15.own_ref), channel_id=1, source_target_pairs={{0,192},{8,200},{64,0},{72,8},{128,64},{136,72},{192,128},{200,136... | collective-permute-start | bytes 49160 | tf_op jit(solution)/shard_map/ppermute | solution.py:261
  119.1 0.0 collective-permute-start.7
  119.1 3.1 %collective-permute-start.6 = (f32[32,1,128]{2,1,0:T(1,128)S(1)}, f32[32,1,128]{2,1,0:T(1,128)S(1)}, u32[]{:S(2)}, u32[]{:S(2)}) collective-permute-start(f32[32,1,128]{2,1,0:T(1,128)S(1)} %all_to_all.15.own_ref), channel_id=1, source_target_pairs={{0,8},{8,0},{64,72},{72,64},{128,136},{136,128},{192,200},{200,192... | collective-permute-start | bytes 49160 | tf_op jit(solution)/shard_map/ppermute | solution.py:261
  122.1 0.0 collective-permute-done.8.last_ref
  122.1 1.4 %collective-permute-done.7.next_ref = f32[32,1,128]{2,1,0:T(1,128)S(1)} collective-permute-done((f32[32,1,128]{2,1,0:T(1,128)S(1)}, f32[32,1,128]{2,1,0:T(1,128)S(1)}, u32[]{:S(2)}, u32[]{:S(2)}) %collective-permute-start.7) | collective-permute-done | bytes 16416 | tf_op jit(solution)/shard_map/ppermute | solution.py:261
  123.5 0.0 collective-permute-done.6.swap_ref
  123.5 0.9 finish.1
Async XLA Ops:
  0.0 1.4 %copy-start = (f32[512,768]{1,0:T(8,128)S(1)}, f32[512,768]{1,0:T(8,128)}, u32[]{:S(2)}) copy-start(f32[512,768]{1,0:T(8,128)} %emb_ref.1) | copy-start | bytes 4718596
  1.4 0.7 copy-start.1
  2.1 0.7 copy-start.2
  5.0 36.7 %all-to-all-start = ((bf16[32,128,128]{2,1,0:T(8,128)(2,1)}), bf16[32,128,128]{2,1,0:T(8,128)(2,1)S(1)}, u32[]{:S(2)}, u32[]{:S(2)}) async-start(bf16[32,128,128]{2,1,0:T(8,128)(2,1)} %get-tuple-element.8), calls=%async_computation | async-start | bytes 2097152 | tf_op jit(solution)/shard_map/all_to_all | solution.py:265
  41.6 25.4 %all-to-all-start.1 = ((bf16[32,80,128]{2,1,0:T(8,128)(2,1)}), bf16[32,80,128]{2,1,0:T(8,128)(2,1)S(1)}, u32[]{:S(2)}, u32[]{:S(2)}) async-start(bf16[32,80,128]{2,1,0:T(8,128)(2,1)} %pack_second.1), calls=%async_computation.1 | async-start | bytes 1310720 | tf_op jit(solution)/shard_map/all_to_all | solution.py:265
  50.2 24.5 %collective-permute-start.4 = (bf16[32,128,128]{2,1,0:T(8,128)(2,1)S(1)}, bf16[32,128,128]{2,1,0:T(8,128)(2,1)S(1)}, u32[]{:S(2)}, u32[]{:S(2)}) collective-permute-start(bf16[32,128,128]{2,1,0:T(8,128)(2,1)S(1)} %all-to-all-done.refs_1_.refs_2_), channel_id=1, source_target_pairs={{192,0},{200,8},{0,64},{8,72},{64,128},{72,136},{128,192},{136,200... | collective-permute-start | bytes 3145736 | tf_op jit(solution)/shard_map/ppermute | solution.py:261
  51.5 27.6 %collective-permute-start.2 = (bf16[32,128,128]{2,1,0:T(8,128)(2,1)S(1)}, bf16[32,128,128]{2,1,0:T(8,128)(2,1)}, u32[]{:S(2)}, u32[]{:S(2)}) collective-permute-start(bf16[32,128,128]{2,1,0:T(8,128)(2,1)S(1)} %all-to-all-done.refs_1_.refs_2_), channel_id=1, source_target_pairs={{8,0},{0,8},{72,64},{64,72},{136,128},{128,136},{200,192},{192,200... | collective-permute-start | bytes 3145736 | tf_op jit(solution)/shard_map/ppermute | solution.py:261
  53.3 25.9 %collective-permute-start = (bf16[32,128,128]{2,1,0:T(8,128)(2,1)S(1)}, bf16[32,128,128]{2,1,0:T(8,128)(2,1)}, u32[]{:S(2)}, u32[]{:S(2)}) collective-permute-start(bf16[32,128,128]{2,1,0:T(8,128)(2,1)S(1)} %all-to-all-done.refs_1_.refs_2_), channel_id=1, source_target_pairs={{64,0},{72,8},{128,64},{136,72},{200,128},{192,136},{8,192},{0,200... | collective-permute-start | bytes 3145736 | tf_op jit(solution)/shard_map/ppermute | solution.py:261
  67.0 16.3 %collective-permute-start.3 = (bf16[32,80,128]{2,1,0:T(8,128)(2,1)S(1)}, bf16[32,80,128]{2,1,0:T(8,128)(2,1)S(1)}, u32[]{:S(2)}, u32[]{:S(2)}) collective-permute-start(bf16[32,80,128]{2,1,0:T(8,128)(2,1)S(1)} %all-to-all-done.1.refs_2_.refs_3_), channel_id=1, source_target_pairs={{8,0},{0,8},{72,64},{64,72},{136,128},{128,136},{200,192},{192,200... | collective-permute-start | bytes 1966088 | tf_op jit(solution)/shard_map/ppermute | solution.py:261
  71.9 18.0 %collective-permute-start.5 = (bf16[32,80,128]{2,1,0:T(8,128)(2,1)S(1)}, bf16[32,80,128]{2,1,0:T(8,128)(2,1)S(1)}, u32[]{:S(2)}, u32[]{:S(2)}) collective-permute-start(bf16[32,80,128]{2,1,0:T(8,128)(2,1)S(1)} %all-to-all-done.1.refs_2_.refs_3_), channel_id=1, source_target_pairs={{192,0},{200,8},{0,64},{8,72},{64,128},{72,136},{128,192},{136,200... | collective-permute-start | bytes 1966088 | tf_op jit(solution)/shard_map/ppermute | solution.py:261
  74.7 18.0 %collective-permute-start.1 = (bf16[32,80,128]{2,1,0:T(8,128)(2,1)S(1)}, bf16[32,80,128]{2,1,0:T(8,128)(2,1)S(1)}, u32[]{:S(2)}, u32[]{:S(2)}) collective-permute-start(bf16[32,80,128]{2,1,0:T(8,128)(2,1)S(1)} %all-to-all-done.1.refs_2_.refs_3_), channel_id=1, source_target_pairs={{64,0},{72,8},{128,64},{136,72},{200,128},{192,136},{8,192},{0,200... | collective-permute-start | bytes 1966088 | tf_op jit(solution)/shard_map/ppermute | solution.py:261
  116.6 5.5 %collective-permute-start.8 = (f32[32,1,128]{2,1,0:T(1,128)S(1)}, f32[32,1,128]{2,1,0:T(1,128)S(1)}, u32[]{:S(2)}, u32[]{:S(2)}) collective-permute-start(f32[32,1,128]{2,1,0:T(1,128)S(1)} %all_to_all.15.own_ref), channel_id=1, source_target_pairs={{0,192},{8,200},{64,0},{72,8},{128,64},{136,72},{192,128},{200,136... | collective-permute-start | bytes 49160 | tf_op jit(solution)/shard_map/ppermute | solution.py:261
  119.1 4.4 %collective-permute-start.7 = (f32[32,1,128]{2,1,0:T(1,128)S(1)}, f32[32,1,128]{2,1,0:T(1,128)S(1)}, u32[]{:S(2)}, u32[]{:S(2)}) collective-permute-start(f32[32,1,128]{2,1,0:T(1,128)S(1)} %all_to_all.15.own_ref), channel_id=1, source_target_pairs={{0,64},{8,72},{64,128},{72,136},{128,200},{136,192},{192,8},{200,0... | collective-permute-start | bytes 49160 | tf_op jit(solution)/shard_map/ppermute | solution.py:261
  119.1 4.4 %collective-permute-start.6 = (f32[32,1,128]{2,1,0:T(1,128)S(1)}, f32[32,1,128]{2,1,0:T(1,128)S(1)}, u32[]{:S(2)}, u32[]{:S(2)}) collective-permute-start(f32[32,1,128]{2,1,0:T(1,128)S(1)} %all_to_all.15.own_ref), channel_id=1, source_target_pairs={{0,8},{8,0},{64,72},{72,64},{128,136},{136,128},{192,200},{200,192... | collective-permute-start | bytes 49160 | tf_op jit(solution)/shard_map/ppermute | solution.py:261

commit v4 on v3

--- a/solution.py
+++ b/solution.py
@@ -15,7 +15,8 @@
 PART = GROUPS * HALF
 PARTS = D // 128
 SIZE = {"x": 4, "y": 4, "c": 2, "z": 8}
-EARLY = 1
+EARLY = 0
+CUTS = 4
 LIMIT = 24 * 1024 * 1024
 NT = (((1,), (1,)), ((), ()))
 NN = (((1,), (0,)), ((), ()))
@@ -60,11 +61,19 @@
         )
 
 
-def pack_first(emb_ref, ids_ref, rank_ref, out_ref, unit_ref, pos_ref):
-    rows = emb_ref[...]
-    norms = jnp.sum(rows * rows, axis=1, keepdims=True)
-    unit = (rows * lax.rsqrt(norms + 1e-06)).astype(jnp.bfloat16)
-    unit_ref[...] = unit
+def pack_first(emb_hbm, ids_hbm, rank_hbm, out_ref, unit_ref, pos_ref, emb_ref, ids_ref, rank_ref, sems):
+    pieces = [pl.ds(start, ROWS // CUTS) for start in range(0, ROWS, ROWS // CUTS)]
+    copies = [
+        pltpu.make_async_copy(ids_hbm, ids_ref, sems.at[CUTS]),
+        pltpu.make_async_copy(rank_hbm, rank_ref, sems.at[CUTS + 1]),
+    ] + [
+        pltpu.make_async_copy(emb_hbm.at[piece], emb_ref.at[piece], sems.at[index])
+        for index, piece in enumerate(pieces)
+    ]
+    for copy in copies:
+        copy.start()
+    for copy in copies[:2]:
+        copy.wait()
 
     target = ids_ref[...]
     member = (iota((GROUPS, ROWS), 0) == target).astype(jnp.float32)
@@ -75,8 +84,15 @@
     pos_ref[...] = position
 
     first, second = chosen_rows(position, 0), chosen_rows(position, 1)
+    for copy, piece in zip(copies[2:], pieces):
+        copy.wait()
+        rows = emb_ref[piece, :]
+        norms = jnp.sum(rows * rows, axis=1, keepdims=True)
+        unit_ref[piece, :] = (rows * lax.rsqrt(norms + 1e-06)).astype(jnp.bfloat16)
+    unit = unit_ref[...]
     put(dot(first, unit, NN), out_ref, 0)
-    put(dot(second, unit[:, : EARLY * 128], NN), out_ref, D // 8 + HALF)
+    if EARLY:
+        put(dot(second, unit[:, : EARLY * 128], NN), out_ref, D // 8 + HALF)
     rank = rank_ref[...]
     line = iota((128, ROWS), 0)
     ranks = jnp.zeros((PART, 128), jnp.float32)
@@ -96,14 +112,15 @@
     return [pl.BlockSpec(memory_space=pltpu.VMEM)] * count
 
 
-def call(kernel, name, shapes, *operands, flops=0):
+def call(kernel, name, shapes, *operands, flops=0, scratch=None, limit=LIMIT):
     shapes = tuple(jax.ShapeDtypeStruct(shape, dtype) for shape, dtype in shapes)
     out = pl.pallas_call(
         kernel,
         out_shape=shapes,
-        in_specs=vmem(len(operands)),
+        in_specs=[pl.BlockSpec(memory_space=pltpu.HBM)] * len(operands) if scratch else vmem(len(operands)),
         out_specs=tuple(vmem(len(shapes))),
-        compiler_params=pltpu.CompilerParams(vmem_limit_bytes=LIMIT),
+        scratch_shapes=scratch or [],
+        compiler_params=pltpu.CompilerParams(vmem_limit_bytes=limit),
         cost_estimate=pl.CostEstimate(
             flops=flops,
             bytes_accessed=sum(array.size * array.dtype.itemsize for array in operands),
@@ -275,6 +292,13 @@
         cluster_ids.reshape(1, ROWS),
         ranks.reshape(1, ROWS),
         flops=2 * PART * ROWS * D,
+        scratch=[
+            pltpu.VMEM((ROWS, D), jnp.float32),
+            pltpu.VMEM((1, ROWS), jnp.int32),
+            pltpu.VMEM((1, ROWS), jnp.int32),
+            pltpu.SemaphoreType.DMA((CUTS + 2,)),
+        ],
+        limit=60 * 1024 * 1024,
     )
     second = call(
         pack_second,

time: 125 us -> 119 us (0.952)
  blocking collectives: 19.1 us -> 15.1 us
  waiting for transfers between devices: 42.4 us -> 45.6 us
  starting transfers between devices: 40.9 us -> 37.9 us
  local copies, waits for them, and re-layouts: 2.77 us -> 0.01 us
    all_to_all x1, blocking collectives: 19.1 us -> 15.1 us  [to_home(): lax.all_to_all(array, ('y', 'z'), split_axis=0, concat_axis=0, tiled=True)]
    ppermute x9, starting transfers between devices: 20.3 us -> 17.2 us  [send(): return lax.ppermute(array, ('x', 'c'), pairs)]
    ppermute x9, waiting for transfers between devices: 6.79 us -> 9.73 us  [send(): return lax.ppermute(array, ('x', 'c'), pairs)]
    unnamed x6 -> x4, local copies, waits for them, and re-layouts: 2.77 us -> 0.01 us
  transfers between devices with their start and end apart: 11 -> 11, of which waited for: 6 -> 4; matrix products, arithmetic and copies ran while one was open for 0% -> 0% of each run, Pallas kernels for 9% -> 9%
where the time goes in v4:
time: 119 us; the launch traced here: 118 us
  waiting for transfers between devices  45.6 us (38%)
  starting transfers between devices  37.9 us (32%)
  Pallas kernels  19.5 us (16%)
  blocking collectives  15.1 us (13%)
    all_to_all x2, waiting for transfers between devices, to_home(): lax.all_to_all(array, ('y', 'z'), split_axis=0, concat_axis=0, tiled=True)  35.8 us
    all_to_all x2, starting transfers between devices, to_home(): lax.all_to_all(array, ('y', 'z'), split_axis=0, concat_axis=0, tiled=True)  20.6 us
    pallas_call x6, Pallas kernels, call(): pl.pallas_call(kernel, out_shape=shapes, in_specs=[pl.BlockSpec(memory_sp...  19.5 us
    ppermute x9, starting transfers between devices, send(): return lax.ppermute(array, ('x', 'c'), pairs)  17.2 us
    all_to_all x1, blocking collectives, to_home(): lax.all_to_all(array, ('y', 'z'), split_axis=0, concat_axis=0, tiled=True)  15.1 us
    ppermute x9, waiting for transfers between devices, send(): return lax.ppermute(array, ('x', 'c'), pairs)  9.73 us
  transfers between devices with their start and end apart: 11, of which 4 were waited for; matrix products, arithmetic and copies ran while one was open for 0% of the time, Pallas kernels for 9%

profile of v4, /device:TPU:1, one launch (start us, length us, event | category | flops | bytes accessed | tf_op | source)
XLA Modules:
  0.0 118.1 jit_solution(14000804844126962390)
XLA Ops:
  0.0 3.4 %pack_first.1 = (bf16[32,112,128]{2,1,0:T(8,128)(2,1)}, bf16[512,768]{1,0:T(8,128)(2,1)}, s32[1,512]{1,0:T(1,128)}) custom-call(f32[512,768]{1,0:T(8,128)} %emb_hbm.1, s32[1,512]{1,0:T(1,128)} %bitcast.3, s32[1,512]{1,0:T(1,128)} %bitcast.4), custom_call_target="tpu_custom_call" | custom-call | flops 402653184 | bytes 1576960 | tf_op jit(solution)/shard_map/pack_first/pallas_call | solution.py:117
  3.4 0.0 copy-start
  3.4 0.0 copy-start.1
  3.5 12.2 %all-to-all-start = ((bf16[32,112,128]{2,1,0:T(8,128)(2,1)}), bf16[32,112,128]{2,1,0:T(8,128)(2,1)S(1)}, u32[]{:S(2)}, u32[]{:S(2)}) async-start(bf16[32,112,128]{2,1,0:T(8,128)(2,1)} %get-tuple-element.8), calls=%async_computation | async-start | bytes 1835008 | tf_op jit(solution)/shard_map/all_to_all | solution.py:282
  15.6 0.0 copy-done
  15.7 0.0 copy-done.1
  15.7 1.5 %pack_second.1 = bf16[32,96,128]{2,1,0:T(8,128)(2,1)} custom-call(bf16[512,768]{1,0:T(8,128)(2,1)S(1)} %copy-done, s32[1,512]{1,0:T(1,128)S(1)} %copy-done.1), custom_call_target="tpu_custom_call" | custom-call | flops 402653184 | bytes 788480 | tf_op jit(solution)/shard_map/pack_second/pallas_call | solution.py:117
  17.2 20.4 %all-to-all-done.refs_1_.refs_2_ = bf16[32,112,128]{2,1,0:T(8,128)(2,1)S(1)} async-done(((bf16[32,112,128]{2,1,0:T(8,128)(2,1)}), bf16[32,112,128]{2,1,0:T(8,128)(2,1)S(1)}, u32[]{:S(2)}, u32[]{:S(2)}) %all-to-all-start) | async-done | bytes 917536 | tf_op jit(solution)/shard_map/all_to_all | solution.py:282
  37.6 8.5 %all-to-all-start.1 = ((bf16[32,96,128]{2,1,0:T(8,128)(2,1)}), bf16[32,96,128]{2,1,0:T(8,128)(2,1)S(1)}, u32[]{:S(2)}, u32[]{:S(2)}) async-start(bf16[32,96,128]{2,1,0:T(8,128)(2,1)} %pack_second.1), calls=%async_computation.1 | async-start | bytes 1572864 | tf_op jit(solution)/shard_map/all_to_all | solution.py:282
  46.1 1.3 %collective-permute-start.4 = (bf16[32,112,128]{2,1,0:T(8,128)(2,1)S(1)}, bf16[32,112,128]{2,1,0:T(8,128)(2,1)S(1)}, u32[]{:S(2)}, u32[]{:S(2)}) collective-permute-start(bf16[32,112,128]{2,1,0:T(8,128)(2,1)S(1)} %all-to-all-done.refs_1_.refs_2_), channel_id=1, source_target_pairs={{192,0},{200,8},{0,64},{8,72},{64,128},{72,136},{128,192},{136,200... | collective-permute-start | bytes 2752520 | tf_op jit(solution)/shard_map/ppermute | solution.py:278
  47.4 1.7 %collective-permute-start.2 = (bf16[32,112,128]{2,1,0:T(8,128)(2,1)S(1)}, bf16[32,112,128]{2,1,0:T(8,128)(2,1)S(1)}, u32[]{:S(2)}, u32[]{:S(2)}) collective-permute-start(bf16[32,112,128]{2,1,0:T(8,128)(2,1)S(1)} %all-to-all-done.refs_1_.refs_2_), channel_id=1, source_target_pairs={{8,0},{0,8},{72,64},{64,72},{136,128},{128,136},{200,192},{192,200... | collective-permute-start | bytes 2752520 | tf_op jit(solution)/shard_map/ppermute | solution.py:278
  49.1 1.4 %collective-permute-start = (bf16[32,112,128]{2,1,0:T(8,128)(2,1)S(1)}, bf16[32,112,128]{2,1,0:T(8,128)(2,1)}, u32[]{:S(2)}, u32[]{:S(2)}) collective-permute-start(bf16[32,112,128]{2,1,0:T(8,128)(2,1)S(1)} %all-to-all-done.refs_1_.refs_2_), channel_id=1, source_target_pairs={{64,0},{72,8},{128,64},{136,72},{200,128},{192,136},{8,192},{0,200... | collective-permute-start | bytes 2752520 | tf_op jit(solution)/shard_map/ppermute | solution.py:278
  50.4 15.4 %all-to-all-done.1.refs_2_.refs_3_ = bf16[32,96,128]{2,1,0:T(8,128)(2,1)S(1)} async-done(((bf16[32,96,128]{2,1,0:T(8,128)(2,1)}), bf16[32,96,128]{2,1,0:T(8,128)(2,1)S(1)}, u32[]{:S(2)}, u32[]{:S(2)}) %all-to-all-start.1) | async-done | bytes 786464 | tf_op jit(solution)/shard_map/all_to_all | solution.py:282
  65.9 4.5 %collective-permute-start.3 = (bf16[32,96,128]{2,1,0:T(8,128)(2,1)S(1)}, bf16[32,96,128]{2,1,0:T(8,128)(2,1)S(1)}, u32[]{:S(2)}, u32[]{:S(2)}) collective-permute-start(bf16[32,96,128]{2,1,0:T(8,128)(2,1)S(1)} %all-to-all-done.1.refs_2_.refs_3_), channel_id=1, source_target_pairs={{8,0},{0,8},{72,64},{64,72},{136,128},{128,136},{200,192},{192,200... | collective-permute-start | bytes 2359304 | tf_op jit(solution)/shard_map/ppermute | solution.py:278
  70.4 1.2 %collective-permute-start.5 = (bf16[32,96,128]{2,1,0:T(8,128)(2,1)S(1)}, bf16[32,96,128]{2,1,0:T(8,128)(2,1)S(1)}, u32[]{:S(2)}, u32[]{:S(2)}) collective-permute-start(bf16[32,96,128]{2,1,0:T(8,128)(2,1)S(1)} %all-to-all-done.1.refs_2_.refs_3_), channel_id=1, source_target_pairs={{192,0},{200,8},{0,64},{8,72},{64,128},{72,136},{128,192},{136,200... | collective-permute-start | bytes 2359304 | tf_op jit(solution)/shard_map/ppermute | solution.py:278
  71.6 0.0 collective-permute-done.4.refs_3_.refs_5_.refs_6_
  71.6 1.6 %collective-permute-start.1 = (bf16[32,96,128]{2,1,0:T(8,128)(2,1)S(1)}, bf16[32,96,128]{2,1,0:T(8,128)(2,1)S(1)}, u32[]{:S(2)}, u32[]{:S(2)}) collective-permute-start(bf16[32,96,128]{2,1,0:T(8,128)(2,1)S(1)} %all-to-all-done.1.refs_2_.refs_3_), channel_id=1, source_target_pairs={{64,0},{72,8},{128,64},{136,72},{200,128},{192,136},{8,192},{0,200... | collective-permute-start | bytes 2359304 | tf_op jit(solution)/shard_map/ppermute | solution.py:278
  73.2 0.0 collective-permute-done.2.refs_2_.refs_3_.refs_4_
  73.2 0.0 collective-permute-done.refs_0_
  73.2 3.8 %score_first.1.refs_6_ = f32[8,512]{1,0:T(8,128)S(1)} custom-call(bf16[32,112,128]{2,1,0:T(8,128)(2,1)} %collective-permute-done.refs_0_, bf16[32,112,128]{2,1,0:T(8,128)(2,1)S(1)} %all-to-all-done.refs_1_.refs_2_, bf16[32,112,128]{2,1,0:T(8,128)(2,1)S(1)} %collective-permute-done.2.refs_2_.refs_3_.refs_4_, ...), custom_call_target="tpu_custom_call" | custom-call | flops 2013265920 | bytes 3670016 | tf_op jit(solution)/shard_map/score_first/pallas_call | solution.py:117
  77.1 0.0 collective-permute-done.3.refs_4_.refs_5_
  77.1 5.3 %score_second.1.refs_8_ = f32[8,512]{1,0:T(8,128)S(1)} custom-call(bf16[32,112,128]{2,1,0:T(8,128)(2,1)} %collective-permute-done.refs_0_, bf16[32,112,128]{2,1,0:T(8,128)(2,1)S(1)} %all-to-all-done.refs_1_.refs_2_, bf16[32,96,128]{2,1,0:T(8,128)(2,1)S(1)} %all-to-all-done.1.refs_2_.refs_3_, ...), custom_call_target="tpu_custom_call" | custom-call | flops 3221225472 | bytes 5259264 | tf_op jit(solution)/shard_map/score_second/pallas_call | solution.py:117
  82.4 8.4 %collective-permute-done.5.refs_7_ = bf16[32,96,128]{2,1,0:T(8,128)(2,1)S(1)} collective-permute-done((bf16[32,96,128]{2,1,0:T(8,128)(2,1)S(1)}, bf16[32,96,128]{2,1,0:T(8,128)(2,1)S(1)}, u32[]{:S(2)}, u32[]{:S(2)}) %collective-permute-start.5) | collective-permute-done | bytes 786464 | tf_op jit(solution)/shard_map/ppermute | solution.py:278
  90.7 0.0 collective-permute-done.1.refs_1_
  90.7 4.5 %score_third.1 = f32[32,1,128]{2,1,0:T(1,128)S(1)} custom-call(bf16[32,112,128]{2,1,0:T(8,128)(2,1)} %collective-permute-done.refs_0_, bf16[32,96,128]{2,1,0:T(8,128)(2,1)S(1)} %collective-permute-done.1.refs_1_, bf16[32,112,128]{2,1,0:T(8,128)(2,1)S(1)} %all-to-all-done.refs_1_.refs_2_, bf16[32,96,128]{2,1,0:T(8,128)(2,1)S(1)} %all-to-all-done.1.refs_2_.refs_3_, ...), custom_call_target="tpu_custom_call" | custom-call | flops 2013265920 | bytes 6832128 | tf_op jit(solution)/shard_map/score_third/pallas_call | solution.py:117
  95.2 15.1 %all_to_all.15.own_ref = f32[32,1,128]{2,1,0:T(1,128)S(1)} all-to-all(f32[32,1,128]{2,1,0:T(1,128)S(1)} %score_third.1), channel_id=1, replica_groups=mesh['x'=4,'y'=4,'c'=2,'z'=8] {'y','z'}, dimensions={0} | all-to-all | bytes 32768 | tf_op jit(solution)/shard_map/all_to_all | solution.py:282
  110.4 2.4 %collective-permute-start.8 = (f32[32,1,128]{2,1,0:T(1,128)S(1)}, f32[32,1,128]{2,1,0:T(1,128)S(1)}, u32[]{:S(2)}, u32[]{:S(2)}) collective-permute-start(f32[32,1,128]{2,1,0:T(1,128)S(1)} %all_to_all.15.own_ref), channel_id=1, source_target_pairs={{0,192},{8,200},{64,0},{72,8},{128,64},{136,72},{192,128},{200,136... | collective-permute-start | bytes 49160 | tf_op jit(solution)/shard_map/ppermute | solution.py:278
  112.8 0.0 collective-permute-start.7
  112.8 3.1 %collective-permute-start.6 = (f32[32,1,128]{2,1,0:T(1,128)S(1)}, f32[32,1,128]{2,1,0:T(1,128)S(1)}, u32[]{:S(2)}, u32[]{:S(2)}) collective-permute-start(f32[32,1,128]{2,1,0:T(1,128)S(1)} %all_to_all.15.own_ref), channel_id=1, source_target_pairs={{0,8},{8,0},{64,72},{72,64},{128,136},{136,128},{192,200},{200,192... | collective-permute-start | bytes 49160 | tf_op jit(solution)/shard_map/ppermute | solution.py:278
  115.9 0.0 collective-permute-done.8.last_ref
  115.9 1.4 %collective-permute-done.7.next_ref = f32[32,1,128]{2,1,0:T(1,128)S(1)} collective-permute-done((f32[32,1,128]{2,1,0:T(1,128)S(1)}, f32[32,1,128]{2,1,0:T(1,128)S(1)}, u32[]{:S(2)}, u32[]{:S(2)}) %collective-permute-start.7) | collective-permute-done | bytes 16416 | tf_op jit(solution)/shard_map/ppermute | solution.py:278
  117.2 0.0 collective-permute-done.6.swap_ref
  117.2 0.9 finish.1
Async XLA Ops:
  3.4 12.2 %copy-start = (bf16[512,768]{1,0:T(8,128)(2,1)S(1)}, bf16[512,768]{1,0:T(8,128)(2,1)}, u32[]{:S(2)}) copy-start(bf16[512,768]{1,0:T(8,128)(2,1)} %get-tuple-element.9.unit_ref) | copy-start | bytes 2359300
  3.4 12.2 %copy-start.1 = (s32[1,512]{1,0:T(1,128)S(1)}, s32[1,512]{1,0:T(1,128)}, u32[]{:S(2)}) copy-start(s32[1,512]{1,0:T(1,128)} %get-tuple-element.10.pos_ref) | copy-start | bytes 6148
  3.5 34.1 %all-to-all-start = ((bf16[32,112,128]{2,1,0:T(8,128)(2,1)}), bf16[32,112,128]{2,1,0:T(8,128)(2,1)S(1)}, u32[]{:S(2)}, u32[]{:S(2)}) async-start(bf16[32,112,128]{2,1,0:T(8,128)(2,1)} %get-tuple-element.8), calls=%async_computation | async-start | bytes 1835008 | tf_op jit(solution)/shard_map/all_to_all | solution.py:282
  37.6 28.3 %all-to-all-start.1 = ((bf16[32,96,128]{2,1,0:T(8,128)(2,1)}), bf16[32,96,128]{2,1,0:T(8,128)(2,1)S(1)}, u32[]{:S(2)}, u32[]{:S(2)}) async-start(bf16[32,96,128]{2,1,0:T(8,128)(2,1)} %pack_second.1), calls=%async_computation.1 | async-start | bytes 1572864 | tf_op jit(solution)/shard_map/all_to_all | solution.py:282
  46.1 25.5 %collective-permute-start.4 = (bf16[32,112,128]{2,1,0:T(8,128)(2,1)S(1)}, bf16[32,112,128]{2,1,0:T(8,128)(2,1)S(1)}, u32[]{:S(2)}, u32[]{:S(2)}) collective-permute-start(bf16[32,112,128]{2,1,0:T(8,128)(2,1)S(1)} %all-to-all-done.refs_1_.refs_2_), channel_id=1, source_target_pairs={{192,0},{200,8},{0,64},{8,72},{64,128},{72,136},{128,192},{136,200... | collective-permute-start | bytes 2752520 | tf_op jit(solution)/shard_map/ppermute | solution.py:278
  47.4 25.9 %collective-permute-start.2 = (bf16[32,112,128]{2,1,0:T(8,128)(2,1)S(1)}, bf16[32,112,128]{2,1,0:T(8,128)(2,1)S(1)}, u32[]{:S(2)}, u32[]{:S(2)}) collective-permute-start(bf16[32,112,128]{2,1,0:T(8,128)(2,1)S(1)} %all-to-all-done.refs_1_.refs_2_), channel_id=1, source_target_pairs={{8,0},{0,8},{72,64},{64,72},{136,128},{128,136},{200,192},{192,200... | collective-permute-start | bytes 2752520 | tf_op jit(solution)/shard_map/ppermute | solution.py:278
  49.1 24.1 %collective-permute-start = (bf16[32,112,128]{2,1,0:T(8,128)(2,1)S(1)}, bf16[32,112,128]{2,1,0:T(8,128)(2,1)}, u32[]{:S(2)}, u32[]{:S(2)}) collective-permute-start(bf16[32,112,128]{2,1,0:T(8,128)(2,1)S(1)} %all-to-all-done.refs_1_.refs_2_), channel_id=1, source_target_pairs={{64,0},{72,8},{128,64},{136,72},{200,128},{192,136},{8,192},{0,200... | collective-permute-start | bytes 2752520 | tf_op jit(solution)/shard_map/ppermute | solution.py:278
  65.9 11.2 %collective-permute-start.3 = (bf16[32,96,128]{2,1,0:T(8,128)(2,1)S(1)}, bf16[32,96,128]{2,1,0:T(8,128)(2,1)S(1)}, u32[]{:S(2)}, u32[]{:S(2)}) collective-permute-start(bf16[32,96,128]{2,1,0:T(8,128)(2,1)S(1)} %all-to-all-done.1.refs_2_.refs_3_), channel_id=1, source_target_pairs={{8,0},{0,8},{72,64},{64,72},{136,128},{128,136},{200,192},{192,200... | collective-permute-start | bytes 2359304 | tf_op jit(solution)/shard_map/ppermute | solution.py:278
  70.4 20.4 %collective-permute-start.5 = (bf16[32,96,128]{2,1,0:T(8,128)(2,1)S(1)}, bf16[32,96,128]{2,1,0:T(8,128)(2,1)S(1)}, u32[]{:S(2)}, u32[]{:S(2)}) collective-permute-start(bf16[32,96,128]{2,1,0:T(8,128)(2,1)S(1)} %all-to-all-done.1.refs_2_.refs_3_), channel_id=1, source_target_pairs={{192,0},{200,8},{0,64},{8,72},{64,128},{72,136},{128,192},{136,200... | collective-permute-start | bytes 2359304 | tf_op jit(solution)/shard_map/ppermute | solution.py:278
  71.6 19.2 %collective-permute-start.1 = (bf16[32,96,128]{2,1,0:T(8,128)(2,1)S(1)}, bf16[32,96,128]{2,1,0:T(8,128)(2,1)S(1)}, u32[]{:S(2)}, u32[]{:S(2)}) collective-permute-start(bf16[32,96,128]{2,1,0:T(8,128)(2,1)S(1)} %all-to-all-done.1.refs_2_.refs_3_), channel_id=1, source_target_pairs={{64,0},{72,8},{128,64},{136,72},{200,128},{192,136},{8,192},{0,200... | collective-permute-start | bytes 2359304 | tf_op jit(solution)/shard_map/ppermute | solution.py:278
  110.4 5.5 %collective-permute-start.8 = (f32[32,1,128]{2,1,0:T(1,128)S(1)}, f32[32,1,128]{2,1,0:T(1,128)S(1)}, u32[]{:S(2)}, u32[]{:S(2)}) collective-permute-start(f32[32,1,128]{2,1,0:T(1,128)S(1)} %all_to_all.15.own_ref), channel_id=1, source_target_pairs={{0,192},{8,200},{64,0},{72,8},{128,64},{136,72},{192,128},{200,136... | collective-permute-start | bytes 49160 | tf_op jit(solution)/shard_map/ppermute | solution.py:278
  112.8 4.4 %collective-permute-start.7 = (f32[32,1,128]{2,1,0:T(1,128)S(1)}, f32[32,1,128]{2,1,0:T(1,128)S(1)}, u32[]{:S(2)}, u32[]{:S(2)}) collective-permute-start(f32[32,1,128]{2,1,0:T(1,128)S(1)} %all_to_all.15.own_ref), channel_id=1, source_target_pairs={{0,64},{8,72},{64,128},{72,136},{128,200},{136,192},{192,8},{200,0... | collective-permute-start | bytes 49160 | tf_op jit(solution)/shard_map/ppermute | solution.py:278
  112.8 4.4 %collective-permute-start.6 = (f32[32,1,128]{2,1,0:T(1,128)S(1)}, f32[32,1,128]{2,1,0:T(1,128)S(1)}, u32[]{:S(2)}, u32[]{:S(2)}) collective-permute-start(f32[32,1,128]{2,1,0:T(1,128)S(1)} %all_to_all.15.own_ref), channel_id=1, source_target_pairs={{0,8},{8,0},{64,72},{72,64},{128,136},{136,128},{192,200},{200,192... | collective-permute-start | bytes 49160 | tf_op jit(solution)/shard_map/ppermute | solution.py:278

commit v5 on v4

--- a/solution.py
+++ b/solution.py
@@ -165,8 +165,12 @@
 
 def score_kernel(names, pairs, last, *refs):
     data = dict(zip(names, refs))
-    carried = None if len(refs) == len(names) + 1 else refs[len(names)]
-    out_ref = refs[-1]
+    refs = refs[len(names) :]
+    if pairs is FIRST:
+        carried, (out_ref, keep_ref) = None, refs
+        keep_ref[...] = data["b0"][...]
+    else:
+        carried, out_ref = refs
     used = sorted({name for pair in pairs for name in pair[:2]})
     keys = {name: keys_of(data, name) for name in used}
     by_row, by_lane = {}, {}
@@ -210,11 +214,14 @@
     used = {half for pair in pairs for half in pair[:2]}
     names = tuple(sorted(used | {half[0] + "0" for half in used}))
     shape = ((GROUPS, 1, 128) if last else (8, PART), jnp.float32)
+    shapes = [shape]
+    if pairs is FIRST:
+        shapes.append((blocks["b0"].shape, blocks["b0"].dtype))
     operands = [blocks[half] for half in names] + ([] if carried is None else [carried])
     return call(
         functools.partial(score_kernel, names, pairs, last),
         name,
-        [shape],
+        shapes,
         *operands,
         flops=2 * len(pairs) * PART * PART * D,
     )
@@ -314,7 +321,7 @@
         blocks["s" + half] = send(home, SWAP)
         blocks["b" + half] = send(home, FROM_NEXT)
         blocks["z" + half] = send(home, FROM_LAST)
-    best = score(blocks, FIRST, None, False, "score_first")
+    best, blocks["b0"] = score(blocks, FIRST, None, False, "score_first")
     best = score(blocks, SECOND, best, False, "score_second")
     own = to_home(score(blocks, THIRD, best, True, "score_third"))
     nearest = call(

time: 119 us -> 117 us (0.983)
  waiting for transfers between devices: 45.6 us -> 49.3 us
  Pallas kernels: 19.5 us -> 17.2 us
  blocking collectives: 15.1 us -> 12.9 us
    ppermute x9, waiting for transfers between devices: 9.73 us -> 13.5 us  [send(): return lax.ppermute(array, ('x', 'c'), pairs)]
    pallas_call x6, Pallas kernels: 19.5 us -> 17.2 us  [call(): pl.pallas_call(kernel, out_shape=shapes, in_specs=[pl.BlockSpec(memory_sp...]
    all_to_all x1, blocking collectives: 15.1 us -> 12.9 us  [to_home(): lax.all_to_all(array, ('y', 'z'), split_axis=0, concat_axis=0, tiled=True)]
  transfers between devices with their start and end apart: 11 -> 11, of which waited for: 4 -> 5; matrix products, arithmetic and copies ran while one was open for 0% -> 0% of each run, Pallas kernels for 9% -> 8%
where the time goes in v5:
time: 117 us
  waiting for transfers between devices  49.3 us (42%)
  starting transfers between devices  37.3 us (32%)
  Pallas kernels  17.2 us (15%)
  blocking collectives  12.9 us (11%)
    all_to_all x2, waiting for transfers between devices, to_home(): lax.all_to_all(array, ('y', 'z'), split_axis=0, concat_axis=0, tiled=True)  35.8 us
    all_to_all x2, starting transfers between devices, to_home(): lax.all_to_all(array, ('y', 'z'), split_axis=0, concat_axis=0, tiled=True)  20.6 us
    pallas_call x6, Pallas kernels, call(): pl.pallas_call(kernel, out_shape=shapes, in_specs=[pl.BlockSpec(memory_sp...  17.2 us
    ppermute x9, starting transfers between devices, send(): return lax.ppermute(array, ('x', 'c'), pairs)  16.7 us
    ppermute x9, waiting for transfers between devices, send(): return lax.ppermute(array, ('x', 'c'), pairs)  13.5 us
    all_to_all x1, blocking collectives, to_home(): lax.all_to_all(array, ('y', 'z'), split_axis=0, concat_axis=0, tiled=True)  12.9 us
  transfers between devices with their start and end apart: 11, of which 5 were waited for; matrix products, arithmetic and copies ran while one was open for 0% of the time, Pallas kernels for 8%

profile of v5, /device:TPU:1, one launch (start us, length us, event | category | flops | bytes accessed | tf_op | source)
XLA Modules:
  0.0 116.9 jit_solution(13860116530546260956)
XLA Ops:
  0.0 3.4 %pack_first.1 = (bf16[32,112,128]{2,1,0:T(8,128)(2,1)}, bf16[512,768]{1,0:T(8,128)(2,1)}, s32[1,512]{1,0:T(1,128)}) custom-call(f32[512,768]{1,0:T(8,128)} %emb_hbm.1, s32[1,512]{1,0:T(1,128)} %bitcast.3, s32[1,512]{1,0:T(1,128)} %bitcast.4), custom_call_target="tpu_custom_call" | custom-call | flops 402653184 | bytes 1576960 | tf_op jit(solution)/shard_map/pack_first/pallas_call | solution.py:117
  3.4 0.0 copy-start
  3.4 0.0 copy-start.1
  3.5 12.2 %all-to-all-start = ((bf16[32,112,128]{2,1,0:T(8,128)(2,1)}), bf16[32,112,128]{2,1,0:T(8,128)(2,1)S(1)}, u32[]{:S(2)}, u32[]{:S(2)}) async-start(bf16[32,112,128]{2,1,0:T(8,128)(2,1)} %get-tuple-element.10), calls=%async_computation | async-start | bytes 1835008 | tf_op jit(solution)/shard_map/all_to_all | solution.py:289
  15.6 0.0 copy-done
  15.7 0.0 copy-done.1
  15.7 1.5 %pack_second.1 = bf16[32,96,128]{2,1,0:T(8,128)(2,1)} custom-call(bf16[512,768]{1,0:T(8,128)(2,1)S(1)} %copy-done, s32[1,512]{1,0:T(1,128)S(1)} %copy-done.1), custom_call_target="tpu_custom_call" | custom-call | flops 402653184 | bytes 788480 | tf_op jit(solution)/shard_map/pack_second/pallas_call | solution.py:117
  17.2 20.4 %all-to-all-done.refs_1_.refs_2_ = bf16[32,112,128]{2,1,0:T(8,128)(2,1)S(1)} async-done(((bf16[32,112,128]{2,1,0:T(8,128)(2,1)}), bf16[32,112,128]{2,1,0:T(8,128)(2,1)S(1)}, u32[]{:S(2)}, u32[]{:S(2)}) %all-to-all-start) | async-done | bytes 917536 | tf_op jit(solution)/shard_map/all_to_all | solution.py:289
  37.6 8.5 %all-to-all-start.1 = ((bf16[32,96,128]{2,1,0:T(8,128)(2,1)}), bf16[32,96,128]{2,1,0:T(8,128)(2,1)S(1)}, u32[]{:S(2)}, u32[]{:S(2)}) async-start(bf16[32,96,128]{2,1,0:T(8,128)(2,1)} %pack_second.1), calls=%async_computation.1 | async-start | bytes 1572864 | tf_op jit(solution)/shard_map/all_to_all | solution.py:289
  46.1 1.5 %collective-permute-start.1 = (bf16[32,112,128]{2,1,0:T(8,128)(2,1)S(1)}, bf16[32,112,128]{2,1,0:T(8,128)(2,1)S(1)}, u32[]{:S(2)}, u32[]{:S(2)}) collective-permute-start(bf16[32,112,128]{2,1,0:T(8,128)(2,1)S(1)} %all-to-all-done.refs_1_.refs_2_), channel_id=1, source_target_pairs={{8,0},{0,8},{72,64},{64,72},{136,128},{128,136},{200,192},{192,200... | collective-permute-start | bytes 2752520 | tf_op jit(solution)/shard_map/ppermute | solution.py:285
  47.6 1.2 %collective-permute-start.2 = (bf16[32,112,128]{2,1,0:T(8,128)(2,1)S(1)}, bf16[32,112,128]{2,1,0:T(8,128)(2,1)S(1)}, u32[]{:S(2)}, u32[]{:S(2)}) collective-permute-start(bf16[32,112,128]{2,1,0:T(8,128)(2,1)S(1)} %all-to-all-done.refs_1_.refs_2_), channel_id=1, source_target_pairs={{192,0},{200,8},{0,64},{8,72},{64,128},{72,136},{128,192},{136,200... | collective-permute-start | bytes 2752520 | tf_op jit(solution)/shard_map/ppermute | solution.py:285
  48.8 1.7 %collective-permute-start = (bf16[32,112,128]{2,1,0:T(8,128)(2,1)S(1)}, bf16[32,112,128]{2,1,0:T(8,128)(2,1)}, u32[]{:S(2)}, u32[]{:S(2)}) collective-permute-start(bf16[32,112,128]{2,1,0:T(8,128)(2,1)S(1)} %all-to-all-done.refs_1_.refs_2_), channel_id=1, source_target_pairs={{64,0},{72,8},{128,64},{136,72},{200,128},{192,136},{8,192},{0,200... | collective-permute-start | bytes 2752520 | tf_op jit(solution)/shard_map/ppermute | solution.py:285
  50.5 15.3 %all-to-all-done.1.refs_2_.refs_3_ = bf16[32,96,128]{2,1,0:T(8,128)(2,1)S(1)} async-done(((bf16[32,96,128]{2,1,0:T(8,128)(2,1)}), bf16[32,96,128]{2,1,0:T(8,128)(2,1)S(1)}, u32[]{:S(2)}, u32[]{:S(2)}) %all-to-all-start.1) | async-done | bytes 786464 | tf_op jit(solution)/shard_map/all_to_all | solution.py:289
  65.9 4.5 %collective-permute-start.4 = (bf16[32,96,128]{2,1,0:T(8,128)(2,1)S(1)}, bf16[32,96,128]{2,1,0:T(8,128)(2,1)S(1)}, u32[]{:S(2)}, u32[]{:S(2)}) collective-permute-start(bf16[32,96,128]{2,1,0:T(8,128)(2,1)S(1)} %all-to-all-done.1.refs_2_.refs_3_), channel_id=1, source_target_pairs={{8,0},{0,8},{72,64},{64,72},{136,128},{128,136},{200,192},{192,200... | collective-permute-start | bytes 2359304 | tf_op jit(solution)/shard_map/ppermute | solution.py:285
  70.4 2.4 %collective-permute-start.3 = (bf16[32,96,128]{2,1,0:T(8,128)(2,1)S(1)}, bf16[32,96,128]{2,1,0:T(8,128)(2,1)S(1)}, u32[]{:S(2)}, u32[]{:S(2)}) collective-permute-start(bf16[32,96,128]{2,1,0:T(8,128)(2,1)S(1)} %all-to-all-done.1.refs_2_.refs_3_), channel_id=1, source_target_pairs={{64,0},{72,8},{128,64},{136,72},{200,128},{192,136},{8,192},{0,200... | collective-permute-start | bytes 2359304 | tf_op jit(solution)/shard_map/ppermute | solution.py:285
  72.7 0.0 collective-permute-done.1.refs_2_.refs_3_.refs_4_
  72.7 0.0 collective-permute-start.5
  72.7 0.0 collective-permute-done.2.refs_3_.refs_5_.refs_6_
  72.7 0.0 collective-permute-done.refs_0_
  72.7 3.9 %score_first.1 = (f32[8,512]{1,0:T(8,128)S(1)}, bf16[32,112,128]{2,1,0:T(8,128)(2,1)S(1)}) custom-call(bf16[32,112,128]{2,1,0:T(8,128)(2,1)} %collective-permute-done.refs_0_, bf16[32,112,128]{2,1,0:T(8,128)(2,1)S(1)} %all-to-all-done.refs_1_.refs_2_, bf16[32,112,128]{2,1,0:T(8,128)(2,1)S(1)} %collective-permute-done.1.refs_2_.refs_3_.refs_4_, ...), custom_call_target="tpu_custom_call" | custom-call | flops 2013265920 | bytes 3670016 | tf_op jit(solution)/shard_map/score_first/pallas_call | solution.py:117
  76.7 0.0 collective-permute-done.4.refs_4_.refs_5_
  76.7 4.2 %score_second.1.refs_8_ = f32[8,512]{1,0:T(8,128)S(1)} custom-call(bf16[32,112,128]{2,1,0:T(8,128)(2,1)S(1)} %get-tuple-element.11.refs_0_, bf16[32,112,128]{2,1,0:T(8,128)(2,1)S(1)} %all-to-all-done.refs_1_.refs_2_, bf16[32,96,128]{2,1,0:T(8,128)(2,1)S(1)} %all-to-all-done.1.refs_2_.refs_3_, ...), custom_call_target="tpu_custom_call" | custom-call | flops 3221225472 | bytes 5259264 | tf_op jit(solution)/shard_map/score_second/pallas_call | solution.py:117
  80.8 8.7 %collective-permute-done.3.refs_1_ = bf16[32,96,128]{2,1,0:T(8,128)(2,1)S(1)} collective-permute-done((bf16[32,96,128]{2,1,0:T(8,128)(2,1)S(1)}, bf16[32,96,128]{2,1,0:T(8,128)(2,1)S(1)}, u32[]{:S(2)}, u32[]{:S(2)}) %collective-permute-start.3) | collective-permute-done | bytes 786464 | tf_op jit(solution)/shard_map/ppermute | solution.py:285
  89.5 3.0 %collective-permute-done.5.refs_7_ = bf16[32,96,128]{2,1,0:T(8,128)(2,1)S(1)} collective-permute-done((bf16[32,96,128]{2,1,0:T(8,128)(2,1)S(1)}, bf16[32,96,128]{2,1,0:T(8,128)(2,1)S(1)}, u32[]{:S(2)}, u32[]{:S(2)}) %collective-permute-start.5) | collective-permute-done | bytes 786464 | tf_op jit(solution)/shard_map/ppermute | solution.py:285
  92.5 3.3 %score_third.1 = f32[32,1,128]{2,1,0:T(1,128)S(1)} custom-call(bf16[32,112,128]{2,1,0:T(8,128)(2,1)S(1)} %get-tuple-element.11.refs_0_, bf16[32,96,128]{2,1,0:T(8,128)(2,1)S(1)} %collective-permute-done.3.refs_1_, bf16[32,112,128]{2,1,0:T(8,128)(2,1)S(1)} %all-to-all-done.refs_1_.refs_2_, bf16[32,96,128]{2,1,0:T(8,128)(2,1)S(1)} %all-to-all-done.1.refs_2_.refs_3_, ...), custom_call_target="tpu_custom_call" | custom-call | flops 2013265920 | bytes 6832128 | tf_op jit(solution)/shard_map/score_third/pallas_call | solution.py:117
  95.9 12.9 %all_to_all.15.own_ref = f32[32,1,128]{2,1,0:T(1,128)S(1)} all-to-all(f32[32,1,128]{2,1,0:T(1,128)S(1)} %score_third.1), channel_id=1, replica_groups=mesh['x'=4,'y'=4,'c'=2,'z'=8] {'y','z'}, dimensions={0} | all-to-all | bytes 32768 | tf_op jit(solution)/shard_map/all_to_all | solution.py:289
  108.8 2.8 %collective-permute-start.6 = (f32[32,1,128]{2,1,0:T(1,128)S(1)}, f32[32,1,128]{2,1,0:T(1,128)S(1)}, u32[]{:S(2)}, u32[]{:S(2)}) collective-permute-start(f32[32,1,128]{2,1,0:T(1,128)S(1)} %all_to_all.15.own_ref), channel_id=1, source_target_pairs={{0,8},{8,0},{64,72},{72,64},{128,136},{136,128},{192,200},{200,192... | collective-permute-start | bytes 49160 | tf_op jit(solution)/shard_map/ppermute | solution.py:285
  111.6 0.8 collective-permute-start.7
  112.4 1.8 %collective-permute-start.8 = (f32[32,1,128]{2,1,0:T(1,128)S(1)}, f32[32,1,128]{2,1,0:T(1,128)S(1)}, u32[]{:S(2)}, u32[]{:S(2)}) collective-permute-start(f32[32,1,128]{2,1,0:T(1,128)S(1)} %all_to_all.15.own_ref), channel_id=1, source_target_pairs={{0,192},{8,200},{64,0},{72,8},{128,64},{136,72},{192,128},{200,136... | collective-permute-start | bytes 49160 | tf_op jit(solution)/shard_map/ppermute | solution.py:285
  114.1 0.0 collective-permute-done.6.swap_ref
  114.1 1.8 %collective-permute-done.7.next_ref = f32[32,1,128]{2,1,0:T(1,128)S(1)} collective-permute-done((f32[32,1,128]{2,1,0:T(1,128)S(1)}, f32[32,1,128]{2,1,0:T(1,128)S(1)}, u32[]{:S(2)}, u32[]{:S(2)}) %collective-permute-start.7) | collective-permute-done | bytes 16416 | tf_op jit(solution)/shard_map/ppermute | solution.py:285
  115.9 0.0 collective-permute-done.8.last_ref
  115.9 0.9 finish.1
Async XLA Ops:
  3.4 12.2 %copy-start = (bf16[512,768]{1,0:T(8,128)(2,1)S(1)}, bf16[512,768]{1,0:T(8,128)(2,1)}, u32[]{:S(2)}) copy-start(bf16[512,768]{1,0:T(8,128)(2,1)} %get-tuple-element.12.unit_ref) | copy-start | bytes 2359300
  3.4 12.2 %copy-start.1 = (s32[1,512]{1,0:T(1,128)S(1)}, s32[1,512]{1,0:T(1,128)}, u32[]{:S(2)}) copy-start(s32[1,512]{1,0:T(1,128)} %get-tuple-element.13.pos_ref) | copy-start | bytes 6148
  3.5 34.1 %all-to-all-start = ((bf16[32,112,128]{2,1,0:T(8,128)(2,1)}), bf16[32,112,128]{2,1,0:T(8,128)(2,1)S(1)}, u32[]{:S(2)}, u32[]{:S(2)}) async-start(bf16[32,112,128]{2,1,0:T(8,128)(2,1)} %get-tuple-element.10), calls=%async_computation | async-start | bytes 1835008 | tf_op jit(solution)/shard_map/all_to_all | solution.py:289
  37.6 28.3 %all-to-all-start.1 = ((bf16[32,96,128]{2,1,0:T(8,128)(2,1)}), bf16[32,96,128]{2,1,0:T(8,128)(2,1)S(1)}, u32[]{:S(2)}, u32[]{:S(2)}) async-start(bf16[32,96,128]{2,1,0:T(8,128)(2,1)} %pack_second.1), calls=%async_computation.1 | async-start | bytes 1572864 | tf_op jit(solution)/shard_map/all_to_all | solution.py:289
  46.1 26.7 %collective-permute-start.1 = (bf16[32,112,128]{2,1,0:T(8,128)(2,1)S(1)}, bf16[32,112,128]{2,1,0:T(8,128)(2,1)S(1)}, u32[]{:S(2)}, u32[]{:S(2)}) collective-permute-start(bf16[32,112,128]{2,1,0:T(8,128)(2,1)S(1)} %all-to-all-done.refs_1_.refs_2_), channel_id=1, source_target_pairs={{8,0},{0,8},{72,64},{64,72},{136,128},{128,136},{200,192},{192,200... | collective-permute-start | bytes 2752520 | tf_op jit(solution)/shard_map/ppermute | solution.py:285
  47.6 25.1 %collective-permute-start.2 = (bf16[32,112,128]{2,1,0:T(8,128)(2,1)S(1)}, bf16[32,112,128]{2,1,0:T(8,128)(2,1)S(1)}, u32[]{:S(2)}, u32[]{:S(2)}) collective-permute-start(bf16[32,112,128]{2,1,0:T(8,128)(2,1)S(1)} %all-to-all-done.refs_1_.refs_2_), channel_id=1, source_target_pairs={{192,0},{200,8},{0,64},{8,72},{64,128},{72,136},{128,192},{136,200... | collective-permute-start | bytes 2752520 | tf_op jit(solution)/shard_map/ppermute | solution.py:285
  48.8 23.9 %collective-permute-start = (bf16[32,112,128]{2,1,0:T(8,128)(2,1)S(1)}, bf16[32,112,128]{2,1,0:T(8,128)(2,1)}, u32[]{:S(2)}, u32[]{:S(2)}) collective-permute-start(bf16[32,112,128]{2,1,0:T(8,128)(2,1)S(1)} %all-to-all-done.refs_1_.refs_2_), channel_id=1, source_target_pairs={{64,0},{72,8},{128,64},{136,72},{200,128},{192,136},{8,192},{0,200... | collective-permute-start | bytes 2752520 | tf_op jit(solution)/shard_map/ppermute | solution.py:285
  65.9 10.8 %collective-permute-start.4 = (bf16[32,96,128]{2,1,0:T(8,128)(2,1)S(1)}, bf16[32,96,128]{2,1,0:T(8,128)(2,1)S(1)}, u32[]{:S(2)}, u32[]{:S(2)}) collective-permute-start(bf16[32,96,128]{2,1,0:T(8,128)(2,1)S(1)} %all-to-all-done.1.refs_2_.refs_3_), channel_id=1, source_target_pairs={{8,0},{0,8},{72,64},{64,72},{136,128},{128,136},{200,192},{192,200... | collective-permute-start | bytes 2359304 | tf_op jit(solution)/shard_map/ppermute | solution.py:285
  70.4 19.2 %collective-permute-start.3 = (bf16[32,96,128]{2,1,0:T(8,128)(2,1)S(1)}, bf16[32,96,128]{2,1,0:T(8,128)(2,1)S(1)}, u32[]{:S(2)}, u32[]{:S(2)}) collective-permute-start(bf16[32,96,128]{2,1,0:T(8,128)(2,1)S(1)} %all-to-all-done.1.refs_2_.refs_3_), channel_id=1, source_target_pairs={{64,0},{72,8},{128,64},{136,72},{200,128},{192,136},{8,192},{0,200... | collective-permute-start | bytes 2359304 | tf_op jit(solution)/shard_map/ppermute | solution.py:285
  72.7 19.8 %collective-permute-start.5 = (bf16[32,96,128]{2,1,0:T(8,128)(2,1)S(1)}, bf16[32,96,128]{2,1,0:T(8,128)(2,1)S(1)}, u32[]{:S(2)}, u32[]{:S(2)}) collective-permute-start(bf16[32,96,128]{2,1,0:T(8,128)(2,1)S(1)} %all-to-all-done.1.refs_2_.refs_3_), channel_id=1, source_target_pairs={{192,0},{200,8},{0,64},{8,72},{64,128},{72,136},{128,192},{136,200... | collective-permute-start | bytes 2359304 | tf_op jit(solution)/shard_map/ppermute | solution.py:285
  108.8 5.4 %collective-permute-start.6 = (f32[32,1,128]{2,1,0:T(1,128)S(1)}, f32[32,1,128]{2,1,0:T(1,128)S(1)}, u32[]{:S(2)}, u32[]{:S(2)}) collective-permute-start(f32[32,1,128]{2,1,0:T(1,128)S(1)} %all_to_all.15.own_ref), channel_id=1, source_target_pairs={{0,8},{8,0},{64,72},{72,64},{128,136},{136,128},{192,200},{200,192... | collective-permute-start | bytes 49160 | tf_op jit(solution)/shard_map/ppermute | solution.py:285
  111.6 4.4 %collective-permute-start.7 = (f32[32,1,128]{2,1,0:T(1,128)S(1)}, f32[32,1,128]{2,1,0:T(1,128)S(1)}, u32[]{:S(2)}, u32[]{:S(2)}) collective-permute-start(f32[32,1,128]{2,1,0:T(1,128)S(1)} %all_to_all.15.own_ref), channel_id=1, source_target_pairs={{0,64},{8,72},{64,128},{72,136},{128,200},{136,192},{192,8},{200,0... | collective-permute-start | bytes 49160 | tf_op jit(solution)/shard_map/ppermute | solution.py:285
  112.4 3.6 %collective-permute-start.8 = (f32[32,1,128]{2,1,0:T(1,128)S(1)}, f32[32,1,128]{2,1,0:T(1,128)S(1)}, u32[]{:S(2)}, u32[]{:S(2)}) collective-permute-start(f32[32,1,128]{2,1,0:T(1,128)S(1)} %all_to_all.15.own_ref), channel_id=1, source_target_pairs={{0,192},{8,200},{64,0},{72,8},{128,64},{136,72},{192,128},{200,136... | collective-permute-start | bytes 49160 | tf_op jit(solution)/shard_map/ppermute | solution.py:285

commit v6 on v5

--- a/solution.py
+++ b/solution.py
@@ -15,13 +15,14 @@
 PART = GROUPS * HALF
 PARTS = D // 128
 SIZE = {"x": 4, "y": 4, "c": 2, "z": 8}
-EARLY = 0
+EARLY = 1
 CUTS = 4
 LIMIT = 24 * 1024 * 1024
 NT = (((1,), (1,)), ((), ()))
 NN = (((1,), (0,)), ((), ()))
 TN = (((0,), (0,)), ((), ()))
 BLOCKS = ("o", "s", "b", "z")
+KEPT = ("b0", "z0")
 FINALS = tuple(block + half for block in BLOCKS for half in "01")
 
 
@@ -61,7 +62,9 @@
         )
 
 
-def pack_first(emb_hbm, ids_hbm, rank_hbm, out_ref, unit_ref, pos_ref, emb_ref, ids_ref, rank_ref, sems):
+def pack_first(
+    emb_hbm, ids_hbm, rank_hbm, out_ref, table_ref, unit_ref, pos_ref, emb_ref, ids_ref, rank_ref, sems
+):
     pieces = [pl.ds(start, ROWS // CUTS) for start in range(0, ROWS, ROWS // CUTS)]
     copies = [
         pltpu.make_async_copy(ids_hbm, ids_ref, sems.at[CUTS]),
@@ -92,7 +95,7 @@
     unit = unit_ref[...]
     put(dot(first, unit, NN), out_ref, 0)
     if EARLY:
-        put(dot(second, unit[:, : EARLY * 128], NN), out_ref, D // 8 + HALF)
+        put(dot(second, unit[:, : EARLY * 128], NN), out_ref, D // 8)
     rank = rank_ref[...]
     line = iota((128, ROWS), 0)
     ranks = jnp.zeros((PART, 128), jnp.float32)
@@ -101,11 +104,18 @@
         for index, part in enumerate(((rank >> 14) - 128, (rank >> 7) & 127, rank & 127)):
             parts = jnp.where(line == 3 * half + index, part, parts)
         ranks += dot(chosen, parts.astype(jnp.float32).astype(jnp.bfloat16), NT)
-    put(ranks, out_ref, D // 8)
-
-
-def pack_second(unit_ref, pos_ref, out_ref):
+    put(ranks, table_ref, 0)
+
+
+def pack_second(unit_ref, pos_ref, *refs):
+    out_ref = refs[-1]
     put(dot(chosen_rows(pos_ref[...], 1), unit_ref[:, EARLY * 128 :], NN), out_ref, 0)
+    ranks = jnp.zeros((PART, 128), jnp.float32)
+    lane, other = iota((128, 128), 0), iota((128, 128), 1)
+    for index, table_ref in enumerate(refs[:-1]):
+        moved = bits((lane < 6) & (other == lane + 6 * index))
+        ranks += dot(tile(table_ref, 0), moved, NN)
+    put(ranks, out_ref, D // 8 - EARLY * HALF)
 
 
 def vmem(count):
@@ -136,11 +146,10 @@
 
 
 def keys_of(data, name):
-    first = data[name[0] + "0"]
     if name[1] == "0":
-        wide = [tile(first, part) for part in range(PARTS)]
+        wide = [tile(data[name], part) for part in range(PARTS)]
     else:
-        wide = [tile(first, PARTS + 1 + part) for part in range(EARLY)]
+        wide = [tile(data[name[0] + "0"], PARTS + part) for part in range(EARLY)]
         wide += [tile(data[name], part) for part in range(PARTS - EARLY)]
     return jnp.concatenate(wide, axis=1)
 
@@ -149,6 +158,11 @@
     place = iota(shape, axis) - start
     weights = jnp.where(place == 0, 16384.0, jnp.where(place == 1, 128.0, 1.0))
     return jnp.where((place >= 0) & (place < 3), weights, 0.0).astype(jnp.bfloat16)
+
+
+def cut_kernel(home_ref, body_ref, ranks_ref):
+    body_ref[...] = home_ref[:, : D // 8 - EARLY * HALF, :]
+    ranks_ref[...] = home_ref[:, D // 8 - EARLY * HALF :, :]
 
 
 def homeward(best):
@@ -165,18 +179,19 @@
 
 def score_kernel(names, pairs, last, *refs):
     data = dict(zip(names, refs))
-    refs = refs[len(names) :]
+    ranks = tile(refs[len(names)], 0)
+    refs = refs[len(names) + 1 :]
     if pairs is FIRST:
-        carried, (out_ref, keep_ref) = None, refs
-        keep_ref[...] = data["b0"][...]
+        carried, (out_ref, *kept) = None, refs
+        for name, ref in zip(KEPT, kept):
+            ref[...] = data[name][...]
     else:
         carried, out_ref = refs
     used = sorted({name for pair in pairs for name in pair[:2]})
     keys = {name: keys_of(data, name) for name in used}
     by_row, by_lane = {}, {}
     for name in used:
-        ranks = tile(data[name[0] + "0"], PARTS)
-        start = 3 * int(name[1])
+        start = 3 * FINALS.index(name)
         by_row[name] = dot(ranks, rank_weights((128, 128), 0, start), NN)
         by_lane[name] = dot(rank_weights((8, 128), 1, start), ranks, NT)[0:1]
     best_row, best_lane = {}, {}
@@ -212,12 +227,12 @@
 
 def score(blocks, pairs, carried, last, name):
     used = {half for pair in pairs for half in pair[:2]}
-    names = tuple(sorted(used | {half[0] + "0" for half in used}))
+    names = tuple(sorted(used | {half[0] + "0" for half in used if EARLY}))
     shape = ((GROUPS, 1, 128) if last else (8, PART), jnp.float32)
     shapes = [shape]
     if pairs is FIRST:
-        shapes.append((blocks["b0"].shape, blocks["b0"].dtype))
-    operands = [blocks[half] for half in names] + ([] if carried is None else [carried])
+        shapes += [(blocks[half].shape, blocks[half].dtype) for half in KEPT]
+    operands = [blocks[half] for half in names + ("ranks",)] + ([] if carried is None else [carried])
     return call(
         functools.partial(score_kernel, names, pairs, last),
         name,
@@ -285,16 +300,25 @@
     return lax.ppermute(array, ("x", "c"), pairs)
 
 
+def spread(array):
+    return send(array, SWAP), send(array, FROM_NEXT), send(array, FROM_LAST)
+
+
 def to_home(array):
     return lax.all_to_all(array, ("y", "z"), split_axis=0, concat_axis=0, tiled=True)
 
 
 def on_device(embeddings, cluster_ids, ranks):
     bf16 = jnp.bfloat16
-    first, unit, position = call(
+    first, table, unit, position = call(
         pack_first,
         "pack_first",
-        [((GROUPS, D // 8 + (1 + EARLY) * HALF, 128), bf16), ((ROWS, D), bf16), ((1, ROWS), jnp.int32)],
+        [
+            ((GROUPS, D // 8 + EARLY * HALF, 128), bf16),
+            ((GROUPS, HALF, 128), bf16),
+            ((ROWS, D), bf16),
+            ((1, ROWS), jnp.int32),
+        ],
         embeddings,
         cluster_ids.reshape(1, ROWS),
         ranks.reshape(1, ROWS),
@@ -310,18 +334,28 @@
     second = call(
         pack_second,
         "pack_second",
-        [((GROUPS, D // 8 - EARLY * HALF, 128), bf16)],
+        [((GROUPS, D // 8 + (1 - EARLY) * HALF, 128), bf16)],
         unit,
         position,
+        table,
+        *spread(table),
         flops=2 * PART * ROWS * D,
     )
     blocks = {}
-    for half, packed in zip("01", (first, second)):
-        blocks["o" + half] = home = to_home(packed)
-        blocks["s" + half] = send(home, SWAP)
-        blocks["b" + half] = send(home, FROM_NEXT)
-        blocks["z" + half] = send(home, FROM_LAST)
-    best, blocks["b0"] = score(blocks, FIRST, None, False, "score_first")
+    home = to_home(first)
+    for half in "01":
+        if half == "1":
+            home, blocks["ranks"] = call(
+                cut_kernel,
+                "cut",
+                [((GROUPS, D // 8 - EARLY * HALF, 128), bf16), ((GROUPS, HALF, 128), bf16)],
+                to_home(second),
+            )
+        blocks["o" + half] = home
+        for block, moved in zip("sbz", spread(home)):
+            blocks[block + half] = moved
+    best, *kept = score(blocks, FIRST, None, False, "score_first")
+    blocks.update(zip(KEPT, kept))
     best = score(blocks, SECOND, best, False, "score_second")
     own = to_home(score(blocks, THIRD, best, True, "score_third"))
     nearest = call(

time: 117 us -> 116 us (level)
  waiting for transfers between devices: 49.3 us -> 42.5 us
  starting transfers between devices: 37.3 us -> 40.5 us
  blocking collectives: 12.9 us -> 14.7 us
    all_to_all x2, waiting for transfers between devices: 35.8 us -> 26.8 us  [to_home(): lax.all_to_all(array, ('y', 'z'), split_axis=0, concat_axis=0, tiled=True)]
    ppermute x9 -> x12, starting transfers between devices: 16.7 us -> 19.8 us  [send(): return lax.ppermute(array, ('x', 'c'), pairs)]
    ppermute x9 -> x12, waiting for transfers between devices: 13.5 us -> 15.7 us  [send(): return lax.ppermute(array, ('x', 'c'), pairs)]
    all_to_all x1, blocking collectives: 12.9 us -> 14.7 us  [to_home(): lax.all_to_all(array, ('y', 'z'), split_axis=0, concat_axis=0, tiled=True)]
    pallas_call x6 -> x7, Pallas kernels: 17.2 us -> 18.1 us  [call(): pl.pallas_call(kernel, out_shape=shapes, in_specs=[pl.BlockSpec(memory_sp...]
  transfers between devices with their start and end apart: 11 -> 14, of which waited for: 5 -> 8; matrix products, arithmetic and copies ran while one was open for 0% -> 0% of each run, Pallas kernels for 8% -> 9%
where the time goes in v6:
time: 116 us
  waiting for transfers between devices  42.5 us (37%)
  starting transfers between devices  40.5 us (35%)
  Pallas kernels  18.1 us (16%)
  blocking collectives  14.7 us (13%)
    all_to_all x2, waiting for transfers between devices, to_home(): lax.all_to_all(array, ('y', 'z'), split_axis=0, concat_axis=0, tiled=True)  26.8 us
    all_to_all x2, starting transfers between devices, to_home(): lax.all_to_all(array, ('y', 'z'), split_axis=0, concat_axis=0, tiled=True)  20.6 us
    ppermute x12, starting transfers between devices, send(): return lax.ppermute(array, ('x', 'c'), pairs)  19.8 us
    pallas_call x7, Pallas kernels, call(): pl.pallas_call(kernel, out_shape=shapes, in_specs=[pl.BlockSpec(memory_sp...  18.1 us
    ppermute x12, waiting for transfers between devices, send(): return lax.ppermute(array, ('x', 'c'), pairs)  15.7 us
    all_to_all x1, blocking collectives, to_home(): lax.all_to_all(array, ('y', 'z'), split_axis=0, concat_axis=0, tiled=True)  14.7 us
  transfers between devices with their start and end apart: 14, of which 8 were waited for; matrix products, arithmetic and copies ran while one was open for 0% of the time, Pallas kernels for 9%

profile of v6, /device:TPU:1, one launch (start us, length us, event | category | flops | bytes accessed | tf_op | source)
XLA Modules:
  0.0 115.9 jit_solution(6472031466769229033)
XLA Ops:
  0.0 3.8 %pack_first.1 = (bf16[32,112,128]{2,1,0:T(8,128)(2,1)}, bf16[32,16,128]{2,1,0:T(8,128)(2,1)}, bf16[512,768]{1,0:T(8,128)(2,1)}, s32[1,512]{1,0:T(1,128)}) custom-call(f32[512,768]{1,0:T(8,128)} %emb_hbm.1, s32[1,512]{1,0:T(1,128)} %bitcast.3, s32[1,512]{1,0:T(1,128)} %bitcast.4), custom_call_target="tpu_custom_call" | custom-call | flops 402653184 | bytes 1576960 | tf_op jit(solution)/shard_map/pack_first/pallas_call | solution.py:127
  3.8 0.0 copy-start.1
  3.8 0.0 copy-start
  3.9 0.0 copy-start.2
  3.9 12.2 %all-to-all-start = ((bf16[32,112,128]{2,1,0:T(8,128)(2,1)}), bf16[32,112,128]{2,1,0:T(8,128)(2,1)S(1)}, u32[]{:S(2)}, u32[]{:S(2)}) async-start(bf16[32,112,128]{2,1,0:T(8,128)(2,1)} %get-tuple-element.14), calls=%async_computation | async-start | bytes 1835008 | tf_op jit(solution)/shard_map/all_to_all | solution.py:308
  16.1 0.0 copy-done.1
  16.1 1.0 collective-permute-start.3
  17.1 2.5 %collective-permute-start.4 = (bf16[32,16,128]{2,1,0:T(8,128)(2,1)S(1)}, bf16[32,16,128]{2,1,0:T(8,128)(2,1)S(1)}, u32[]{:S(2)}, u32[]{:S(2)}) collective-permute-start(bf16[32,16,128]{2,1,0:T(8,128)(2,1)S(1)} %copy-done.1), channel_id=1, source_target_pairs={{64,0},{72,8},{128,64},{136,72},{200,128},{192,136},{8,192},{0,200... | collective-permute-start | bytes 393224 | tf_op jit(solution)/shard_map/ppermute | solution.py:300
  19.6 0.0 collective-permute-start.5
  19.6 0.0 collective-permute-done.3.refs_1_
  19.6 2.8 %collective-permute-done.4.refs_2_ = bf16[32,16,128]{2,1,0:T(8,128)(2,1)S(1)} collective-permute-done((bf16[32,16,128]{2,1,0:T(8,128)(2,1)S(1)}, bf16[32,16,128]{2,1,0:T(8,128)(2,1)S(1)}, u32[]{:S(2)}, u32[]{:S(2)}) %collective-permute-start.4) | collective-permute-done | bytes 131104 | tf_op jit(solution)/shard_map/ppermute | solution.py:300
  22.3 3.1 %collective-permute-done.5.refs_3_ = bf16[32,16,128]{2,1,0:T(8,128)(2,1)S(1)} collective-permute-done((bf16[32,16,128]{2,1,0:T(8,128)(2,1)S(1)}, bf16[32,16,128]{2,1,0:T(8,128)(2,1)S(1)}, u32[]{:S(2)}, u32[]{:S(2)}) %collective-permute-start.5) | collective-permute-done | bytes 131104 | tf_op jit(solution)/shard_map/ppermute | solution.py:300
  25.4 0.0 copy-done
  25.4 0.0 copy-done.2
  25.4 1.6 %pack_second.1 = bf16[32,96,128]{2,1,0:T(8,128)(2,1)} custom-call(bf16[512,768]{1,0:T(8,128)(2,1)S(1)} %copy-done, s32[1,512]{1,0:T(1,128)S(1)} %copy-done.2, bf16[32,16,128]{2,1,0:T(8,128)(2,1)S(1)} %copy-done.1, bf16[32,16,128]{2,1,0:T(8,128)(2,1)S(1)} %collective-permute-done.3.refs_1_, bf16[32,16,128]{2,1,0:T(8,128)(2,1)S(1)} %collective-permute-done.4.refs_2_, ...), custom_call_target="tpu_custom_call" | custom-call | flops 402653184 | bytes 1312768 | tf_op jit(solution)/shard_map/pack_second/pallas_call | solution.py:127
  27.0 11.0 %all-to-all-done.refs_1_.refs_2_ = bf16[32,112,128]{2,1,0:T(8,128)(2,1)S(1)} async-done(((bf16[32,112,128]{2,1,0:T(8,128)(2,1)}), bf16[32,112,128]{2,1,0:T(8,128)(2,1)S(1)}, u32[]{:S(2)}, u32[]{:S(2)}) %all-to-all-start) | async-done | bytes 917536 | tf_op jit(solution)/shard_map/all_to_all | solution.py:308
  38.0 8.5 %all-to-all-start.1 = ((bf16[32,96,128]{2,1,0:T(8,128)(2,1)}), bf16[32,96,128]{2,1,0:T(8,128)(2,1)S(1)}, u32[]{:S(2)}, u32[]{:S(2)}) async-start(bf16[32,96,128]{2,1,0:T(8,128)(2,1)} %pack_second.1), calls=%async_computation.1 | async-start | bytes 1572864 | tf_op jit(solution)/shard_map/all_to_all | solution.py:308
  46.5 1.5 %collective-permute-start.1 = (bf16[32,112,128]{2,1,0:T(8,128)(2,1)S(1)}, bf16[32,112,128]{2,1,0:T(8,128)(2,1)S(1)}, u32[]{:S(2)}, u32[]{:S(2)}) collective-permute-start(bf16[32,112,128]{2,1,0:T(8,128)(2,1)S(1)} %all-to-all-done.refs_1_.refs_2_), channel_id=1, source_target_pairs={{8,0},{0,8},{72,64},{64,72},{136,128},{128,136},{200,192},{192,200... | collective-permute-start | bytes 2752520 | tf_op jit(solution)/shard_map/ppermute | solution.py:300
  48.0 2.5 %collective-permute-start = (bf16[32,112,128]{2,1,0:T(8,128)(2,1)S(1)}, bf16[32,112,128]{2,1,0:T(8,128)(2,1)}, u32[]{:S(2)}, u32[]{:S(2)}) collective-permute-start(bf16[32,112,128]{2,1,0:T(8,128)(2,1)S(1)} %all-to-all-done.refs_1_.refs_2_), channel_id=1, source_target_pairs={{64,0},{72,8},{128,64},{136,72},{200,128},{192,136},{8,192},{0,200... | collective-permute-start | bytes 2752520 | tf_op jit(solution)/shard_map/ppermute | solution.py:300
  50.5 0.0 collective-permute-start.2
  50.5 15.8 %all-to-all-done.1.home_ref = bf16[32,96,128]{2,1,0:T(8,128)(2,1)S(1)} async-done(((bf16[32,96,128]{2,1,0:T(8,128)(2,1)}), bf16[32,96,128]{2,1,0:T(8,128)(2,1)S(1)}, u32[]{:S(2)}, u32[]{:S(2)}) %all-to-all-start.1) | async-done | bytes 786464 | tf_op jit(solution)/shard_map/all_to_all | solution.py:308
  66.3 0.1 cut.1
  66.3 4.6 %collective-permute-start.7 = (bf16[32,80,128]{2,1,0:T(8,128)(2,1)S(1)}, bf16[32,80,128]{2,1,0:T(8,128)(2,1)S(1)}, u32[]{:S(2)}, u32[]{:S(2)}) collective-permute-start(bf16[32,80,128]{2,1,0:T(8,128)(2,1)S(1)} %get-tuple-element.20.refs_2_.refs_3_), channel_id=1, source_target_pairs={{8,0},{0,8},{72,64},{64,72},{136,128},{128,136},{200,192},{192,200... | collective-permute-start | bytes 1966088 | tf_op jit(solution)/shard_map/ppermute | solution.py:300
  70.9 2.5 %collective-permute-start.6 = (bf16[32,80,128]{2,1,0:T(8,128)(2,1)S(1)}, bf16[32,80,128]{2,1,0:T(8,128)(2,1)S(1)}, u32[]{:S(2)}, u32[]{:S(2)}) collective-permute-start(bf16[32,80,128]{2,1,0:T(8,128)(2,1)S(1)} %get-tuple-element.20.refs_2_.refs_3_), channel_id=1, source_target_pairs={{64,0},{72,8},{128,64},{136,72},{200,128},{192,136},{8,192},{0,200... | collective-permute-start | bytes 1966088 | tf_op jit(solution)/shard_map/ppermute | solution.py:300
  73.4 0.0 collective-permute-done.1.refs_2_.refs_3_.refs_4_
  73.4 0.0 collective-permute-start.8
  73.4 0.0 collective-permute-done.refs_0_
  73.4 0.0 collective-permute-done.2.refs_3_
  73.4 4.3 %score_first.1 = (f32[8,512]{1,0:T(8,128)S(1)}, bf16[32,112,128]{2,1,0:T(8,128)(2,1)S(1)}, bf16[32,112,128]{2,1,0:T(8,128)(2,1)S(1)}) custom-call(bf16[32,112,128]{2,1,0:T(8,128)(2,1)} %collective-permute-done.refs_0_, bf16[32,112,128]{2,1,0:T(8,128)(2,1)S(1)} %all-to-all-done.refs_1_.refs_2_, ...), custom_call_target="tpu_custom_call" | custom-call | flops 2013265920 | bytes 3801088 | tf_op jit(solution)/shard_map/score_first/pallas_call | solution.py:127
  77.6 0.0 collective-permute-done.7.refs_4_.refs_5_
  77.7 4.1 %score_second.1.refs_9_ = f32[8,512]{1,0:T(8,128)S(1)} custom-call(bf16[32,112,128]{2,1,0:T(8,128)(2,1)S(1)} %get-tuple-element.19.refs_0_, bf16[32,112,128]{2,1,0:T(8,128)(2,1)S(1)} %all-to-all-done.refs_1_.refs_2_, bf16[32,80,128]{2,1,0:T(8,128)(2,1)S(1)} %get-tuple-element.20.refs_2_.refs_3_, ...), custom_call_target="tpu_custom_call" | custom-call | flops 3221225472 | bytes 5128192 | tf_op jit(solution)/shard_map/score_second/pallas_call | solution.py:127
  81.8 5.6 %collective-permute-done.6.refs_1_ = bf16[32,80,128]{2,1,0:T(8,128)(2,1)S(1)} collective-permute-done((bf16[32,80,128]{2,1,0:T(8,128)(2,1)S(1)}, bf16[32,80,128]{2,1,0:T(8,128)(2,1)S(1)}, u32[]{:S(2)}, u32[]{:S(2)}) %collective-permute-start.6) | collective-permute-done | bytes 655392 | tf_op jit(solution)/shard_map/ppermute | solution.py:300
  87.4 3.1 %collective-permute-done.8.refs_7_ = bf16[32,80,128]{2,1,0:T(8,128)(2,1)S(1)} collective-permute-done((bf16[32,80,128]{2,1,0:T(8,128)(2,1)S(1)}, bf16[32,80,128]{2,1,0:T(8,128)(2,1)S(1)}, u32[]{:S(2)}, u32[]{:S(2)}) %collective-permute-start.8) | collective-permute-done | bytes 655392 | tf_op jit(solution)/shard_map/ppermute | solution.py:300
  90.5 3.3 %score_third.1 = f32[32,1,128]{2,1,0:T(1,128)S(1)} custom-call(bf16[32,112,128]{2,1,0:T(8,128)(2,1)S(1)} %get-tuple-element.19.refs_0_, bf16[32,80,128]{2,1,0:T(8,128)(2,1)S(1)} %collective-permute-done.6.refs_1_, bf16[32,112,128]{2,1,0:T(8,128)(2,1)S(1)} %all-to-all-done.refs_1_.refs_2_, bf16[32,80,128]{2,1,0:T(8,128)(2,1)S(1)} %get-tuple-element.20.refs_2_.refs_3_, ...), custom_call_target="tpu_custom_call" | custom-call | flops 2013265920 | bytes 6438912 | tf_op jit(solution)/shard_map/score_third/pallas_call | solution.py:127
  93.8 14.7 %all_to_all.15.own_ref = f32[32,1,128]{2,1,0:T(1,128)S(1)} all-to-all(f32[32,1,128]{2,1,0:T(1,128)S(1)} %score_third.1), channel_id=1, replica_groups=mesh['x'=4,'y'=4,'c'=2,'z'=8] {'y','z'}, dimensions={0} | all-to-all | bytes 32768 | tf_op jit(solution)/shard_map/all_to_all | solution.py:308
  108.5 0.0 collective-permute-start.10
  108.5 5.3 %collective-permute-start.11 = (f32[32,1,128]{2,1,0:T(1,128)S(1)}, f32[32,1,128]{2,1,0:T(1,128)S(1)}, u32[]{:S(2)}, u32[]{:S(2)}) collective-permute-start(f32[32,1,128]{2,1,0:T(1,128)S(1)} %all_to_all.15.own_ref), channel_id=1, source_target_pairs={{0,192},{8,200},{64,0},{72,8},{128,64},{136,72},{192,128},{200,136... | collective-permute-start | bytes 49160 | tf_op jit(solution)/shard_map/ppermute | solution.py:300
  113.8 0.0 collective-permute-start.9
  113.8 0.0 collective-permute-done.10.next_ref
  113.8 0.9 collective-permute-done.11.last_ref
  114.6 0.3 collective-permute-done.9.swap_ref
  114.9 0.9 finish.1
Async XLA Ops:
  3.8 12.2 %copy-start.1 = (bf16[32,16,128]{2,1,0:T(8,128)(2,1)S(1)}, bf16[32,16,128]{2,1,0:T(8,128)(2,1)}, u32[]{:S(2)}) copy-start(bf16[32,16,128]{2,1,0:T(8,128)(2,1)} %get-tuple-element.17.refs_0_) | copy-start | bytes 393220
  3.8 21.6 %copy-start = (bf16[512,768]{1,0:T(8,128)(2,1)S(1)}, bf16[512,768]{1,0:T(8,128)(2,1)}, u32[]{:S(2)}) copy-start(bf16[512,768]{1,0:T(8,128)(2,1)} %get-tuple-element.15.unit_ref) | copy-start | bytes 2359300
  3.9 21.6 %copy-start.2 = (s32[1,512]{1,0:T(1,128)S(1)}, s32[1,512]{1,0:T(1,128)}, u32[]{:S(2)}) copy-start(s32[1,512]{1,0:T(1,128)} %get-tuple-element.16.pos_ref) | copy-start | bytes 6148
  3.9 34.1 %all-to-all-start = ((bf16[32,112,128]{2,1,0:T(8,128)(2,1)}), bf16[32,112,128]{2,1,0:T(8,128)(2,1)S(1)}, u32[]{:S(2)}, u32[]{:S(2)}) async-start(bf16[32,112,128]{2,1,0:T(8,128)(2,1)} %get-tuple-element.14), calls=%async_computation | async-start | bytes 1835008 | tf_op jit(solution)/shard_map/all_to_all | solution.py:308
  16.1 3.5 %collective-permute-start.3 = (bf16[32,16,128]{2,1,0:T(8,128)(2,1)S(1)}, bf16[32,16,128]{2,1,0:T(8,128)(2,1)S(1)}, u32[]{:S(2)}, u32[]{:S(2)}) collective-permute-start(bf16[32,16,128]{2,1,0:T(8,128)(2,1)S(1)} %copy-done.1), channel_id=1, source_target_pairs={{8,0},{0,8},{72,64},{64,72},{136,128},{128,136},{200,192},{192,200... | collective-permute-start | bytes 393224 | tf_op jit(solution)/shard_map/ppermute | solution.py:300
  17.1 5.2 %collective-permute-start.4 = (bf16[32,16,128]{2,1,0:T(8,128)(2,1)S(1)}, bf16[32,16,128]{2,1,0:T(8,128)(2,1)S(1)}, u32[]{:S(2)}, u32[]{:S(2)}) collective-permute-start(bf16[32,16,128]{2,1,0:T(8,128)(2,1)S(1)} %copy-done.1), channel_id=1, source_target_pairs={{64,0},{72,8},{128,64},{136,72},{200,128},{192,136},{8,192},{0,200... | collective-permute-start | bytes 393224 | tf_op jit(solution)/shard_map/ppermute | solution.py:300
  19.6 5.9 %collective-permute-start.5 = (bf16[32,16,128]{2,1,0:T(8,128)(2,1)S(1)}, bf16[32,16,128]{2,1,0:T(8,128)(2,1)S(1)}, u32[]{:S(2)}, u32[]{:S(2)}) collective-permute-start(bf16[32,16,128]{2,1,0:T(8,128)(2,1)S(1)} %copy-done.1), channel_id=1, source_target_pairs={{192,0},{200,8},{0,64},{8,72},{64,128},{72,136},{128,192},{136,200... | collective-permute-start | bytes 393224 | tf_op jit(solution)/shard_map/ppermute | solution.py:300
  38.0 28.3 %all-to-all-start.1 = ((bf16[32,96,128]{2,1,0:T(8,128)(2,1)}), bf16[32,96,128]{2,1,0:T(8,128)(2,1)S(1)}, u32[]{:S(2)}, u32[]{:S(2)}) async-start(bf16[32,96,128]{2,1,0:T(8,128)(2,1)} %pack_second.1), calls=%async_computation.1 | async-start | bytes 1572864 | tf_op jit(solution)/shard_map/all_to_all | solution.py:308
  46.5 26.9 %collective-permute-start.1 = (bf16[32,112,128]{2,1,0:T(8,128)(2,1)S(1)}, bf16[32,112,128]{2,1,0:T(8,128)(2,1)S(1)}, u32[]{:S(2)}, u32[]{:S(2)}) collective-permute-start(bf16[32,112,128]{2,1,0:T(8,128)(2,1)S(1)} %all-to-all-done.refs_1_.refs_2_), channel_id=1, source_target_pairs={{8,0},{0,8},{72,64},{64,72},{136,128},{128,136},{200,192},{192,200... | collective-permute-start | bytes 2752520 | tf_op jit(solution)/shard_map/ppermute | solution.py:300
  48.0 25.4 %collective-permute-start = (bf16[32,112,128]{2,1,0:T(8,128)(2,1)S(1)}, bf16[32,112,128]{2,1,0:T(8,128)(2,1)}, u32[]{:S(2)}, u32[]{:S(2)}) collective-permute-start(bf16[32,112,128]{2,1,0:T(8,128)(2,1)S(1)} %all-to-all-done.refs_1_.refs_2_), channel_id=1, source_target_pairs={{64,0},{72,8},{128,64},{136,72},{200,128},{192,136},{8,192},{0,200... | collective-permute-start | bytes 2752520 | tf_op jit(solution)/shard_map/ppermute | solution.py:300
  50.5 22.9 %collective-permute-start.2 = (bf16[32,112,128]{2,1,0:T(8,128)(2,1)S(1)}, bf16[32,112,128]{2,1,0:T(8,128)(2,1)}, u32[]{:S(2)}, u32[]{:S(2)}) collective-permute-start(bf16[32,112,128]{2,1,0:T(8,128)(2,1)S(1)} %all-to-all-done.refs_1_.refs_2_), channel_id=1, source_target_pairs={{192,0},{200,8},{0,64},{8,72},{64,128},{72,136},{128,192},{136,200... | collective-permute-start | bytes 2752520 | tf_op jit(solution)/shard_map/ppermute | solution.py:300
  66.3 11.3 %collective-permute-start.7 = (bf16[32,80,128]{2,1,0:T(8,128)(2,1)S(1)}, bf16[32,80,128]{2,1,0:T(8,128)(2,1)S(1)}, u32[]{:S(2)}, u32[]{:S(2)}) collective-permute-start(bf16[32,80,128]{2,1,0:T(8,128)(2,1)S(1)} %get-tuple-element.20.refs_2_.refs_3_), channel_id=1, source_target_pairs={{8,0},{0,8},{72,64},{64,72},{136,128},{128,136},{200,192},{192,200... | collective-permute-start | bytes 1966088 | tf_op jit(solution)/shard_map/ppermute | solution.py:300
  70.9 16.5 %collective-permute-start.6 = (bf16[32,80,128]{2,1,0:T(8,128)(2,1)S(1)}, bf16[32,80,128]{2,1,0:T(8,128)(2,1)S(1)}, u32[]{:S(2)}, u32[]{:S(2)}) collective-permute-start(bf16[32,80,128]{2,1,0:T(8,128)(2,1)S(1)} %get-tuple-element.20.refs_2_.refs_3_), channel_id=1, source_target_pairs={{64,0},{72,8},{128,64},{136,72},{200,128},{192,136},{8,192},{0,200... | collective-permute-start | bytes 1966088 | tf_op jit(solution)/shard_map/ppermute | solution.py:300
  73.4 17.1 %collective-permute-start.8 = (bf16[32,80,128]{2,1,0:T(8,128)(2,1)S(1)}, bf16[32,80,128]{2,1,0:T(8,128)(2,1)S(1)}, u32[]{:S(2)}, u32[]{:S(2)}) collective-permute-start(bf16[32,80,128]{2,1,0:T(8,128)(2,1)S(1)} %get-tuple-element.20.refs_2_.refs_3_), channel_id=1, source_target_pairs={{192,0},{200,8},{0,64},{8,72},{64,128},{72,136},{128,192},{136,200... | collective-permute-start | bytes 1966088 | tf_op jit(solution)/shard_map/ppermute | solution.py:300
  108.5 5.3 %collective-permute-start.10 = (f32[32,1,128]{2,1,0:T(1,128)S(1)}, f32[32,1,128]{2,1,0:T(1,128)S(1)}, u32[]{:S(2)}, u32[]{:S(2)}) collective-permute-start(f32[32,1,128]{2,1,0:T(1,128)S(1)} %all_to_all.15.own_ref), channel_id=1, source_target_pairs={{0,64},{8,72},{64,128},{72,136},{128,200},{136,192},{192,8},{200,0... | collective-permute-start | bytes 49160 | tf_op jit(solution)/shard_map/ppermute | solution.py:300
  108.5 6.1 %collective-permute-start.11 = (f32[32,1,128]{2,1,0:T(1,128)S(1)}, f32[32,1,128]{2,1,0:T(1,128)S(1)}, u32[]{:S(2)}, u32[]{:S(2)}) collective-permute-start(f32[32,1,128]{2,1,0:T(1,128)S(1)} %all_to_all.15.own_ref), channel_id=1, source_target_pairs={{0,192},{8,200},{64,0},{72,8},{128,64},{136,72},{192,128},{200,136... | collective-permute-start | bytes 49160 | tf_op jit(solution)/shard_map/ppermute | solution.py:300
  113.8 1.2 %collective-permute-start.9 = (f32[32,1,128]{2,1,0:T(1,128)S(1)}, f32[32,1,128]{2,1,0:T(1,128)S(1)}, u32[]{:S(2)}, u32[]{:S(2)}) collective-permute-start(f32[32,1,128]{2,1,0:T(1,128)S(1)} %all_to_all.15.own_ref), channel_id=1, source_target_pairs={{0,8},{8,0},{64,72},{72,64},{128,136},{136,128},{192,200},{200,192... | collective-permute-start | bytes 49160 | tf_op jit(solution)/shard_map/ppermute | solution.py:300

commit v7 on v6

--- a/solution.py
+++ b/solution.py
@@ -263,6 +263,8 @@
     ("o1", "b1", True, True),
     ("s1", "b1", True, True),
     ("z0", "b1", True, True),
+)
+FOURTH = (
     ("z1", "b0", True, True),
     ("z1", "b1", True, True),
 )
@@ -357,7 +359,8 @@
     best, *kept = score(blocks, FIRST, None, False, "score_first")
     blocks.update(zip(KEPT, kept))
     best = score(blocks, SECOND, best, False, "score_second")
-    own = to_home(score(blocks, THIRD, best, True, "score_third"))
+    best = score(blocks, THIRD, best, False, "score_third")
+    own = to_home(score(blocks, FOURTH, best, True, "score_fourth"))
     nearest = call(
         finish_kernel,
         "finish",

time: 116 us -> 115 us (level)
  waiting for transfers between devices: 42.5 us -> 41 us
    ppermute x12, waiting for transfers between devices: 15.7 us -> 14.2 us  [send(): return lax.ppermute(array, ('x', 'c'), pairs)]
    pallas_call x7 -> x8, Pallas kernels: 18.1 us -> 18.1 us  [call(): pl.pallas_call(kernel, out_shape=shapes, in_specs=[pl.BlockSpec(memory_sp...]
  transfers between devices with their start and end apart: 14 -> 14, of which waited for: 8 -> 8; matrix products, arithmetic and copies ran while one was open for 0% -> 0% of each run, Pallas kernels for 9% -> 10%
where the time goes in v7:
time: 115 us; the launch traced here: 114 us
  waiting for transfers between devices  41 us (36%)
  starting transfers between devices  40.5 us (35%)
  Pallas kernels  18.1 us (16%)
  blocking collectives  14.7 us (13%)
    all_to_all x2, waiting for transfers between devices, to_home(): lax.all_to_all(array, ('y', 'z'), split_axis=0, concat_axis=0, tiled=True)  26.7 us
    all_to_all x2, starting transfers between devices, to_home(): lax.all_to_all(array, ('y', 'z'), split_axis=0, concat_axis=0, tiled=True)  20.6 us
    ppermute x12, starting transfers between devices, send(): return lax.ppermute(array, ('x', 'c'), pairs)  19.8 us
    pallas_call x8, Pallas kernels, call(): pl.pallas_call(kernel, out_shape=shapes, in_specs=[pl.BlockSpec(memory_sp...  18.1 us
    all_to_all x1, blocking collectives, to_home(): lax.all_to_all(array, ('y', 'z'), split_axis=0, concat_axis=0, tiled=True)  14.7 us
    ppermute x12, waiting for transfers between devices, send(): return lax.ppermute(array, ('x', 'c'), pairs)  14.2 us
  transfers between devices with their start and end apart: 14, of which 8 were waited for; matrix products, arithmetic and copies ran while one was open for 0% of the time, Pallas kernels for 10%

profile of v7, /device:TPU:1, one launch (start us, length us, event | category | flops | bytes accessed | tf_op | source)
XLA Modules:
  0.0 114.4 jit_solution(8493475206908172378)
XLA Ops:
  0.0 3.8 %pack_first.1 = (bf16[32,112,128]{2,1,0:T(8,128)(2,1)}, bf16[32,16,128]{2,1,0:T(8,128)(2,1)}, bf16[512,768]{1,0:T(8,128)(2,1)}, s32[1,512]{1,0:T(1,128)}) custom-call(f32[512,768]{1,0:T(8,128)} %emb_hbm.1, s32[1,512]{1,0:T(1,128)} %bitcast.3, s32[1,512]{1,0:T(1,128)} %bitcast.4), custom_call_target="tpu_custom_call" | custom-call | flops 402653184 | bytes 1576960 | tf_op jit(solution)/shard_map/pack_first/pallas_call | solution.py:127
  3.8 0.0 copy-start.1
  3.8 0.0 copy-start
  3.9 0.0 copy-start.2
  3.9 12.2 %all-to-all-start = ((bf16[32,112,128]{2,1,0:T(8,128)(2,1)}), bf16[32,112,128]{2,1,0:T(8,128)(2,1)S(1)}, u32[]{:S(2)}, u32[]{:S(2)}) async-start(bf16[32,112,128]{2,1,0:T(8,128)(2,1)} %get-tuple-element.14), calls=%async_computation | async-start | bytes 1835008 | tf_op jit(solution)/shard_map/all_to_all | solution.py:310
  16.1 0.0 copy-done.1
  16.1 1.0 collective-permute-start.3
  17.1 2.5 %collective-permute-start.4 = (bf16[32,16,128]{2,1,0:T(8,128)(2,1)S(1)}, bf16[32,16,128]{2,1,0:T(8,128)(2,1)S(1)}, u32[]{:S(2)}, u32[]{:S(2)}) collective-permute-start(bf16[32,16,128]{2,1,0:T(8,128)(2,1)S(1)} %copy-done.1), channel_id=1, source_target_pairs={{64,0},{72,8},{128,64},{136,72},{200,128},{192,136},{8,192},{0,200... | collective-permute-start | bytes 393224 | tf_op jit(solution)/shard_map/ppermute | solution.py:302
  19.6 0.0 collective-permute-start.5
  19.6 0.0 collective-permute-done.3.refs_1_
  19.6 2.8 %collective-permute-done.4.refs_2_ = bf16[32,16,128]{2,1,0:T(8,128)(2,1)S(1)} collective-permute-done((bf16[32,16,128]{2,1,0:T(8,128)(2,1)S(1)}, bf16[32,16,128]{2,1,0:T(8,128)(2,1)S(1)}, u32[]{:S(2)}, u32[]{:S(2)}) %collective-permute-start.4) | collective-permute-done | bytes 131104 | tf_op jit(solution)/shard_map/ppermute | solution.py:302
  22.3 3.1 %collective-permute-done.5.refs_3_ = bf16[32,16,128]{2,1,0:T(8,128)(2,1)S(1)} collective-permute-done((bf16[32,16,128]{2,1,0:T(8,128)(2,1)S(1)}, bf16[32,16,128]{2,1,0:T(8,128)(2,1)S(1)}, u32[]{:S(2)}, u32[]{:S(2)}) %collective-permute-start.5) | collective-permute-done | bytes 131104 | tf_op jit(solution)/shard_map/ppermute | solution.py:302
  25.4 0.0 copy-done
  25.4 0.0 copy-done.2
  25.4 1.7 %pack_second.1 = bf16[32,96,128]{2,1,0:T(8,128)(2,1)} custom-call(bf16[512,768]{1,0:T(8,128)(2,1)S(1)} %copy-done, s32[1,512]{1,0:T(1,128)S(1)} %copy-done.2, bf16[32,16,128]{2,1,0:T(8,128)(2,1)S(1)} %copy-done.1, bf16[32,16,128]{2,1,0:T(8,128)(2,1)S(1)} %collective-permute-done.3.refs_1_, bf16[32,16,128]{2,1,0:T(8,128)(2,1)S(1)} %collective-permute-done.4.refs_2_, ...), custom_call_target="tpu_custom_call" | custom-call | flops 402653184 | bytes 1312768 | tf_op jit(solution)/shard_map/pack_second/pallas_call | solution.py:127
  27.1 10.9 %all-to-all-done.refs_1_.refs_2_ = bf16[32,112,128]{2,1,0:T(8,128)(2,1)S(1)} async-done(((bf16[32,112,128]{2,1,0:T(8,128)(2,1)}), bf16[32,112,128]{2,1,0:T(8,128)(2,1)S(1)}, u32[]{:S(2)}, u32[]{:S(2)}) %all-to-all-start) | async-done | bytes 917536 | tf_op jit(solution)/shard_map/all_to_all | solution.py:310
  38.0 8.5 %all-to-all-start.1 = ((bf16[32,96,128]{2,1,0:T(8,128)(2,1)}), bf16[32,96,128]{2,1,0:T(8,128)(2,1)S(1)}, u32[]{:S(2)}, u32[]{:S(2)}) async-start(bf16[32,96,128]{2,1,0:T(8,128)(2,1)} %pack_second.1), calls=%async_computation.1 | async-start | bytes 1572864 | tf_op jit(solution)/shard_map/all_to_all | solution.py:310
  46.5 1.5 %collective-permute-start.1 = (bf16[32,112,128]{2,1,0:T(8,128)(2,1)S(1)}, bf16[32,112,128]{2,1,0:T(8,128)(2,1)S(1)}, u32[]{:S(2)}, u32[]{:S(2)}) collective-permute-start(bf16[32,112,128]{2,1,0:T(8,128)(2,1)S(1)} %all-to-all-done.refs_1_.refs_2_), channel_id=1, source_target_pairs={{8,0},{0,8},{72,64},{64,72},{136,128},{128,136},{200,192},{192,200... | collective-permute-start | bytes 2752520 | tf_op jit(solution)/shard_map/ppermute | solution.py:302
  48.0 2.5 %collective-permute-start = (bf16[32,112,128]{2,1,0:T(8,128)(2,1)S(1)}, bf16[32,112,128]{2,1,0:T(8,128)(2,1)S(1)}, u32[]{:S(2)}, u32[]{:S(2)}) collective-permute-start(bf16[32,112,128]{2,1,0:T(8,128)(2,1)S(1)} %all-to-all-done.refs_1_.refs_2_), channel_id=1, source_target_pairs={{64,0},{72,8},{128,64},{136,72},{200,128},{192,136},{8,192},{0,200... | collective-permute-start | bytes 2752520 | tf_op jit(solution)/shard_map/ppermute | solution.py:302
  50.5 0.0 collective-permute-start.2
  50.5 15.8 %all-to-all-done.1.home_ref = bf16[32,96,128]{2,1,0:T(8,128)(2,1)S(1)} async-done(((bf16[32,96,128]{2,1,0:T(8,128)(2,1)}), bf16[32,96,128]{2,1,0:T(8,128)(2,1)S(1)}, u32[]{:S(2)}, u32[]{:S(2)}) %all-to-all-start.1) | async-done | bytes 786464 | tf_op jit(solution)/shard_map/all_to_all | solution.py:310
  66.3 0.1 cut.1
  66.3 4.6 %collective-permute-start.8 = (bf16[32,80,128]{2,1,0:T(8,128)(2,1)S(1)}, bf16[32,80,128]{2,1,0:T(8,128)(2,1)S(1)}, u32[]{:S(2)}, u32[]{:S(2)}) collective-permute-start(bf16[32,80,128]{2,1,0:T(8,128)(2,1)S(1)} %get-tuple-element.20.refs_2_.refs_3_), channel_id=1, source_target_pairs={{8,0},{0,8},{72,64},{64,72},{136,128},{128,136},{200,192},{192,200... | collective-permute-start | bytes 1966088 | tf_op jit(solution)/shard_map/ppermute | solution.py:302
  70.9 2.5 %collective-permute-start.6 = (bf16[32,80,128]{2,1,0:T(8,128)(2,1)S(1)}, bf16[32,80,128]{2,1,0:T(8,128)(2,1)S(1)}, u32[]{:S(2)}, u32[]{:S(2)}) collective-permute-start(bf16[32,80,128]{2,1,0:T(8,128)(2,1)S(1)} %get-tuple-element.20.refs_2_.refs_3_), channel_id=1, source_target_pairs={{64,0},{72,8},{128,64},{136,72},{200,128},{192,136},{8,192},{0,200... | collective-permute-start | bytes 1966088 | tf_op jit(solution)/shard_map/ppermute | solution.py:302
  73.4 0.0 collective-permute-done.1.refs_2_.refs_3_.refs_4_
  73.4 0.0 collective-permute-start.7
  73.4 0.0 collective-permute-done.refs_0_
  73.4 0.0 collective-permute-done.2.refs_3_
  73.4 4.0 %score_first.1 = (f32[8,512]{1,0:T(8,128)S(1)}, bf16[32,112,128]{2,1,0:T(8,128)(2,1)S(1)}, bf16[32,112,128]{2,1,0:T(8,128)(2,1)S(1)}) custom-call(bf16[32,112,128]{2,1,0:T(8,128)(2,1)S(1)} %collective-permute-done.refs_0_, bf16[32,112,128]{2,1,0:T(8,128)(2,1)S(1)} %all-to-all-done.refs_1_.refs_2_, ...), custom_call_target="tpu_custom_call" | custom-call | flops 2013265920 | bytes 3801088 | tf_op jit(solution)/shard_map/score_first/pallas_call | solution.py:127
  77.4 0.0 collective-permute-done.8.refs_4_.refs_5_
  77.4 4.1 %score_second.1.refs_8_ = f32[8,512]{1,0:T(8,128)S(1)} custom-call(bf16[32,112,128]{2,1,0:T(8,128)(2,1)S(1)} %get-tuple-element.19.refs_0_, bf16[32,112,128]{2,1,0:T(8,128)(2,1)S(1)} %all-to-all-done.refs_1_.refs_2_, bf16[32,80,128]{2,1,0:T(8,128)(2,1)S(1)} %get-tuple-element.20.refs_2_.refs_3_, ...), custom_call_target="tpu_custom_call" | custom-call | flops 3221225472 | bytes 5128192 | tf_op jit(solution)/shard_map/score_second/pallas_call | solution.py:127
  81.5 5.9 %collective-permute-done.6.refs_1_ = bf16[32,80,128]{2,1,0:T(8,128)(2,1)S(1)} collective-permute-done((bf16[32,80,128]{2,1,0:T(8,128)(2,1)S(1)}, bf16[32,80,128]{2,1,0:T(8,128)(2,1)S(1)}, u32[]{:S(2)}, u32[]{:S(2)}) %collective-permute-start.6) | collective-permute-done | bytes 655392 | tf_op jit(solution)/shard_map/ppermute | solution.py:302
  87.4 1.7 %score_third.1.refs_5_ = f32[8,512]{1,0:T(8,128)S(1)} custom-call(bf16[32,112,128]{2,1,0:T(8,128)(2,1)S(1)} %get-tuple-element.19.refs_0_, bf16[32,80,128]{2,1,0:T(8,128)(2,1)S(1)} %collective-permute-done.6.refs_1_, bf16[32,112,128]{2,1,0:T(8,128)(2,1)S(1)} %all-to-all-done.refs_1_.refs_2_, bf16[32,80,128]{2,1,0:T(8,128)(2,1)S(1)} %get-tuple-element.20.refs_2_.refs_3_, ...), custom_call_target="tpu_custom_call" | custom-call | flops 1207959552 | bytes 5783552 | tf_op jit(solution)/shard_map/score_third/pallas_call | solution.py:127
  89.1 1.4 %collective-permute-done.7.refs_3_ = bf16[32,80,128]{2,1,0:T(8,128)(2,1)S(1)} collective-permute-done((bf16[32,80,128]{2,1,0:T(8,128)(2,1)S(1)}, bf16[32,80,128]{2,1,0:T(8,128)(2,1)S(1)}, u32[]{:S(2)}, u32[]{:S(2)}) %collective-permute-start.7) | collective-permute-done | bytes 655392 | tf_op jit(solution)/shard_map/ppermute | solution.py:302
  90.5 1.9 %score_fourth.1 = f32[32,1,128]{2,1,0:T(1,128)S(1)} custom-call(bf16[32,112,128]{2,1,0:T(8,128)(2,1)S(1)} %get-tuple-element.19.refs_0_, bf16[32,80,128]{2,1,0:T(8,128)(2,1)S(1)} %collective-permute-done.6.refs_1_, bf16[32,112,128]{2,1,0:T(8,128)(2,1)S(1)} %get-tuple-element.21.refs_5_.refs_6_.refs_2_, ...), custom_call_target="tpu_custom_call" | custom-call | flops 805306368 | bytes 3293184 | tf_op jit(solution)/shard_map/score_fourth/pallas_call | solution.py:127
  92.3 14.7 %all_to_all.15.own_ref = f32[32,1,128]{2,1,0:T(1,128)S(1)} all-to-all(f32[32,1,128]{2,1,0:T(1,128)S(1)} %score_fourth.1), channel_id=1, replica_groups=mesh['x'=4,'y'=4,'c'=2,'z'=8] {'y','z'}, dimensions={0} | all-to-all | bytes 32768 | tf_op jit(solution)/shard_map/all_to_all | solution.py:310
  107.0 0.0 collective-permute-start.10
  107.0 5.3 %collective-permute-start.11 = (f32[32,1,128]{2,1,0:T(1,128)S(1)}, f32[32,1,128]{2,1,0:T(1,128)S(1)}, u32[]{:S(2)}, u32[]{:S(2)}) collective-permute-start(f32[32,1,128]{2,1,0:T(1,128)S(1)} %all_to_all.15.own_ref), channel_id=1, source_target_pairs={{0,192},{8,200},{64,0},{72,8},{128,64},{136,72},{192,128},{200,136... | collective-permute-start | bytes 49160 | tf_op jit(solution)/shard_map/ppermute | solution.py:302
  112.3 0.0 collective-permute-start.9
  112.3 0.0 collective-permute-done.10.next_ref
  112.3 0.9 collective-permute-done.11.last_ref
  113.2 0.3 collective-permute-done.9.swap_ref
  113.5 0.9 finish.1
Async XLA Ops:
  3.8 12.2 %copy-start.1 = (bf16[32,16,128]{2,1,0:T(8,128)(2,1)S(1)}, bf16[32,16,128]{2,1,0:T(8,128)(2,1)}, u32[]{:S(2)}) copy-start(bf16[32,16,128]{2,1,0:T(8,128)(2,1)} %get-tuple-element.17.refs_0_) | copy-start | bytes 393220
  3.8 21.6 %copy-start = (bf16[512,768]{1,0:T(8,128)(2,1)S(1)}, bf16[512,768]{1,0:T(8,128)(2,1)}, u32[]{:S(2)}) copy-start(bf16[512,768]{1,0:T(8,128)(2,1)} %get-tuple-element.15.unit_ref) | copy-start | bytes 2359300
  3.9 21.6 %copy-start.2 = (s32[1,512]{1,0:T(1,128)S(1)}, s32[1,512]{1,0:T(1,128)}, u32[]{:S(2)}) copy-start(s32[1,512]{1,0:T(1,128)} %get-tuple-element.16.pos_ref) | copy-start | bytes 6148
  3.9 34.1 %all-to-all-start = ((bf16[32,112,128]{2,1,0:T(8,128)(2,1)}), bf16[32,112,128]{2,1,0:T(8,128)(2,1)S(1)}, u32[]{:S(2)}, u32[]{:S(2)}) async-start(bf16[32,112,128]{2,1,0:T(8,128)(2,1)} %get-tuple-element.14), calls=%async_computation | async-start | bytes 1835008 | tf_op jit(solution)/shard_map/all_to_all | solution.py:310
  16.1 3.5 %collective-permute-start.3 = (bf16[32,16,128]{2,1,0:T(8,128)(2,1)S(1)}, bf16[32,16,128]{2,1,0:T(8,128)(2,1)S(1)}, u32[]{:S(2)}, u32[]{:S(2)}) collective-permute-start(bf16[32,16,128]{2,1,0:T(8,128)(2,1)S(1)} %copy-done.1), channel_id=1, source_target_pairs={{8,0},{0,8},{72,64},{64,72},{136,128},{128,136},{200,192},{192,200... | collective-permute-start | bytes 393224 | tf_op jit(solution)/shard_map/ppermute | solution.py:302
  17.1 5.2 %collective-permute-start.4 = (bf16[32,16,128]{2,1,0:T(8,128)(2,1)S(1)}, bf16[32,16,128]{2,1,0:T(8,128)(2,1)S(1)}, u32[]{:S(2)}, u32[]{:S(2)}) collective-permute-start(bf16[32,16,128]{2,1,0:T(8,128)(2,1)S(1)} %copy-done.1), channel_id=1, source_target_pairs={{64,0},{72,8},{128,64},{136,72},{200,128},{192,136},{8,192},{0,200... | collective-permute-start | bytes 393224 | tf_op jit(solution)/shard_map/ppermute | solution.py:302
  19.6 5.9 %collective-permute-start.5 = (bf16[32,16,128]{2,1,0:T(8,128)(2,1)S(1)}, bf16[32,16,128]{2,1,0:T(8,128)(2,1)S(1)}, u32[]{:S(2)}, u32[]{:S(2)}) collective-permute-start(bf16[32,16,128]{2,1,0:T(8,128)(2,1)S(1)} %copy-done.1), channel_id=1, source_target_pairs={{192,0},{200,8},{0,64},{8,72},{64,128},{72,136},{128,192},{136,200... | collective-permute-start | bytes 393224 | tf_op jit(solution)/shard_map/ppermute | solution.py:302
  38.0 28.3 %all-to-all-start.1 = ((bf16[32,96,128]{2,1,0:T(8,128)(2,1)}), bf16[32,96,128]{2,1,0:T(8,128)(2,1)S(1)}, u32[]{:S(2)}, u32[]{:S(2)}) async-start(bf16[32,96,128]{2,1,0:T(8,128)(2,1)} %pack_second.1), calls=%async_computation.1 | async-start | bytes 1572864 | tf_op jit(solution)/shard_map/all_to_all | solution.py:310
  46.5 26.9 %collective-permute-start.1 = (bf16[32,112,128]{2,1,0:T(8,128)(2,1)S(1)}, bf16[32,112,128]{2,1,0:T(8,128)(2,1)S(1)}, u32[]{:S(2)}, u32[]{:S(2)}) collective-permute-start(bf16[32,112,128]{2,1,0:T(8,128)(2,1)S(1)} %all-to-all-done.refs_1_.refs_2_), channel_id=1, source_target_pairs={{8,0},{0,8},{72,64},{64,72},{136,128},{128,136},{200,192},{192,200... | collective-permute-start | bytes 2752520 | tf_op jit(solution)/shard_map/ppermute | solution.py:302
  48.0 25.4 %collective-permute-start = (bf16[32,112,128]{2,1,0:T(8,128)(2,1)S(1)}, bf16[32,112,128]{2,1,0:T(8,128)(2,1)S(1)}, u32[]{:S(2)}, u32[]{:S(2)}) collective-permute-start(bf16[32,112,128]{2,1,0:T(8,128)(2,1)S(1)} %all-to-all-done.refs_1_.refs_2_), channel_id=1, source_target_pairs={{64,0},{72,8},{128,64},{136,72},{200,128},{192,136},{8,192},{0,200... | collective-permute-start | bytes 2752520 | tf_op jit(solution)/shard_map/ppermute | solution.py:302
  50.5 22.9 %collective-permute-start.2 = (bf16[32,112,128]{2,1,0:T(8,128)(2,1)S(1)}, bf16[32,112,128]{2,1,0:T(8,128)(2,1)}, u32[]{:S(2)}, u32[]{:S(2)}) collective-permute-start(bf16[32,112,128]{2,1,0:T(8,128)(2,1)S(1)} %all-to-all-done.refs_1_.refs_2_), channel_id=1, source_target_pairs={{192,0},{200,8},{0,64},{8,72},{64,128},{72,136},{128,192},{136,200... | collective-permute-start | bytes 2752520 | tf_op jit(solution)/shard_map/ppermute | solution.py:302
  66.3 11.0 %collective-permute-start.8 = (bf16[32,80,128]{2,1,0:T(8,128)(2,1)S(1)}, bf16[32,80,128]{2,1,0:T(8,128)(2,1)S(1)}, u32[]{:S(2)}, u32[]{:S(2)}) collective-permute-start(bf16[32,80,128]{2,1,0:T(8,128)(2,1)S(1)} %get-tuple-element.20.refs_2_.refs_3_), channel_id=1, source_target_pairs={{8,0},{0,8},{72,64},{64,72},{136,128},{128,136},{200,192},{192,200... | collective-permute-start | bytes 1966088 | tf_op jit(solution)/shard_map/ppermute | solution.py:302
  70.9 16.5 %collective-permute-start.6 = (bf16[32,80,128]{2,1,0:T(8,128)(2,1)S(1)}, bf16[32,80,128]{2,1,0:T(8,128)(2,1)S(1)}, u32[]{:S(2)}, u32[]{:S(2)}) collective-permute-start(bf16[32,80,128]{2,1,0:T(8,128)(2,1)S(1)} %get-tuple-element.20.refs_2_.refs_3_), channel_id=1, source_target_pairs={{64,0},{72,8},{128,64},{136,72},{200,128},{192,136},{8,192},{0,200... | collective-permute-start | bytes 1966088 | tf_op jit(solution)/shard_map/ppermute | solution.py:302
  73.4 17.1 %collective-permute-start.7 = (bf16[32,80,128]{2,1,0:T(8,128)(2,1)S(1)}, bf16[32,80,128]{2,1,0:T(8,128)(2,1)S(1)}, u32[]{:S(2)}, u32[]{:S(2)}) collective-permute-start(bf16[32,80,128]{2,1,0:T(8,128)(2,1)S(1)} %get-tuple-element.20.refs_2_.refs_3_), channel_id=1, source_target_pairs={{192,0},{200,8},{0,64},{8,72},{64,128},{72,136},{128,192},{136,200... | collective-permute-start | bytes 1966088 | tf_op jit(solution)/shard_map/ppermute | solution.py:302
  107.0 5.3 %collective-permute-start.10 = (f32[32,1,128]{2,1,0:T(1,128)S(1)}, f32[32,1,128]{2,1,0:T(1,128)S(1)}, u32[]{:S(2)}, u32[]{:S(2)}) collective-permute-start(f32[32,1,128]{2,1,0:T(1,128)S(1)} %all_to_all.15.own_ref), channel_id=1, source_target_pairs={{0,64},{8,72},{64,128},{72,136},{128,200},{136,192},{192,8},{200,0... | collective-permute-start | bytes 49160 | tf_op jit(solution)/shard_map/ppermute | solution.py:302
  107.0 6.1 %collective-permute-start.11 = (f32[32,1,128]{2,1,0:T(1,128)S(1)}, f32[32,1,128]{2,1,0:T(1,128)S(1)}, u32[]{:S(2)}, u32[]{:S(2)}) collective-permute-start(f32[32,1,128]{2,1,0:T(1,128)S(1)} %all_to_all.15.own_ref), channel_id=1, source_target_pairs={{0,192},{8,200},{64,0},{72,8},{128,64},{136,72},{192,128},{200,136... | collective-permute-start | bytes 49160 | tf_op jit(solution)/shard_map/ppermute | solution.py:302
  112.3 1.2 %collective-permute-start.9 = (f32[32,1,128]{2,1,0:T(1,128)S(1)}, f32[32,1,128]{2,1,0:T(1,128)S(1)}, u32[]{:S(2)}, u32[]{:S(2)}) collective-permute-start(f32[32,1,128]{2,1,0:T(1,128)S(1)} %all_to_all.15.own_ref), channel_id=1, source_target_pairs={{0,8},{8,0},{64,72},{72,64},{128,136},{136,128},{192,200},{200,192... | collective-permute-start | bytes 49160 | tf_op jit(solution)/shard_map/ppermute | solution.py:302

commit v8 on v7

--- a/solution.py
+++ b/solution.py
@@ -62,21 +62,21 @@
         )
 
 
-def pack_first(
-    emb_hbm, ids_hbm, rank_hbm, out_ref, table_ref, unit_ref, pos_ref, emb_ref, ids_ref, rank_ref, sems
-):
+def normalise(rows):
+    norms = jnp.sum(rows * rows, axis=1, keepdims=True)
+    return (rows * lax.rsqrt(norms + 1e-06)).astype(jnp.bfloat16)
+
+
+def pack_first(emb_hbm, ids_hbm, out_ref, pos_ref, emb_ref, ids_ref, unit_ref, sems):
     pieces = [pl.ds(start, ROWS // CUTS) for start in range(0, ROWS, ROWS // CUTS)]
+    small = pltpu.make_async_copy(ids_hbm, ids_ref, sems.at[CUTS])
     copies = [
-        pltpu.make_async_copy(ids_hbm, ids_ref, sems.at[CUTS]),
-        pltpu.make_async_copy(rank_hbm, rank_ref, sems.at[CUTS + 1]),
-    ] + [
         pltpu.make_async_copy(emb_hbm.at[piece], emb_ref.at[piece], sems.at[index])
         for index, piece in enumerate(pieces)
     ]
-    for copy in copies:
+    for copy in [small, *copies]:
         copy.start()
-    for copy in copies[:2]:
-        copy.wait()
+    small.wait()
 
     target = ids_ref[...]
     member = (iota((GROUPS, ROWS), 0) == target).astype(jnp.float32)
@@ -87,29 +87,32 @@
     pos_ref[...] = position
 
     first, second = chosen_rows(position, 0), chosen_rows(position, 1)
-    for copy, piece in zip(copies[2:], pieces):
+    for copy, piece in zip(copies, pieces):
         copy.wait()
-        rows = emb_ref[piece, :]
-        norms = jnp.sum(rows * rows, axis=1, keepdims=True)
-        unit_ref[piece, :] = (rows * lax.rsqrt(norms + 1e-06)).astype(jnp.bfloat16)
+        unit_ref[piece, :] = normalise(emb_ref[piece, :])
     unit = unit_ref[...]
     put(dot(first, unit, NN), out_ref, 0)
     if EARLY:
         put(dot(second, unit[:, : EARLY * 128], NN), out_ref, D // 8)
+
+
+def pack_table(pos_ref, rank_ref, table_ref):
     rank = rank_ref[...]
     line = iota((128, ROWS), 0)
     ranks = jnp.zeros((PART, 128), jnp.float32)
-    for half, chosen in enumerate((first, second)):
+    for half in range(2):
         parts = jnp.zeros((128, ROWS), jnp.int32)
         for index, part in enumerate(((rank >> 14) - 128, (rank >> 7) & 127, rank & 127)):
             parts = jnp.where(line == 3 * half + index, part, parts)
+        chosen = chosen_rows(pos_ref[...], half)
         ranks += dot(chosen, parts.astype(jnp.float32).astype(jnp.bfloat16), NT)
     put(ranks, table_ref, 0)
 
 
-def pack_second(unit_ref, pos_ref, *refs):
+def pack_second(emb_ref, pos_ref, *refs):
     out_ref = refs[-1]
-    put(dot(chosen_rows(pos_ref[...], 1), unit_ref[:, EARLY * 128 :], NN), out_ref, 0)
+    unit = normalise(emb_ref[...])
+    put(dot(chosen_rows(pos_ref[...], 1), unit[:, EARLY * 128 :], NN), out_ref, 0)
     ranks = jnp.zeros((PART, 128), jnp.float32)
     lane, other = iota((128, 128), 0), iota((128, 128), 1)
     for index, table_ref in enumerate(refs[:-1]):
@@ -312,32 +315,33 @@
 
 def on_device(embeddings, cluster_ids, ranks):
     bf16 = jnp.bfloat16
-    first, table, unit, position = call(
+    first, position = call(
         pack_first,
         "pack_first",
-        [
-            ((GROUPS, D // 8 + EARLY * HALF, 128), bf16),
-            ((GROUPS, HALF, 128), bf16),
-            ((ROWS, D), bf16),
-            ((1, ROWS), jnp.int32),
-        ],
+        [((GROUPS, D // 8 + EARLY * HALF, 128), bf16), ((1, ROWS), jnp.int32)],
         embeddings,
         cluster_ids.reshape(1, ROWS),
-        ranks.reshape(1, ROWS),
         flops=2 * PART * ROWS * D,
         scratch=[
             pltpu.VMEM((ROWS, D), jnp.float32),
             pltpu.VMEM((1, ROWS), jnp.int32),
-            pltpu.VMEM((1, ROWS), jnp.int32),
-            pltpu.SemaphoreType.DMA((CUTS + 2,)),
+            pltpu.VMEM((ROWS, D), bf16),
+            pltpu.SemaphoreType.DMA((CUTS + 1,)),
         ],
         limit=60 * 1024 * 1024,
+    )
+    table = call(
+        pack_table,
+        "pack_table",
+        [((GROUPS, HALF, 128), bf16)],
+        position,
+        ranks.reshape(1, ROWS),
     )
     second = call(
         pack_second,
         "pack_second",
         [((GROUPS, D // 8 + (1 - EARLY) * HALF, 128), bf16)],
-        unit,
+        embeddings,
         position,
         table,
         *spread(table),

time: 115 us -> 114 us (level)
    pallas_call x8 -> x9, Pallas kernels: 18.1 us -> 18.4 us  [call(): pl.pallas_call(kernel, out_shape=shapes, in_specs=[pl.BlockSpec(memory_sp...]
  transfers between devices with their start and end apart: 14 -> 14, of which waited for: 8 -> 8; matrix products, arithmetic and copies ran while one was open for 0% -> 0% of each run, Pallas kernels for 10% -> 11%
where the time goes in v8:
time: 114 us
  starting transfers between devices  40.3 us (35%)
  waiting for transfers between devices  40.2 us (35%)
  Pallas kernels  18.4 us (16%)
  blocking collectives  14.7 us (13%)
    all_to_all x2, waiting for transfers between devices, to_home(): lax.all_to_all(array, ('y', 'z'), split_axis=0, concat_axis=0, tiled=True)  26.2 us
    all_to_all x2, starting transfers between devices, to_home(): lax.all_to_all(array, ('y', 'z'), split_axis=0, concat_axis=0, tiled=True)  20.5 us
    ppermute x12, starting transfers between devices, send(): return lax.ppermute(array, ('x', 'c'), pairs)  19.8 us
    pallas_call x9, Pallas kernels, call(): pl.pallas_call(kernel, out_shape=shapes, in_specs=[pl.BlockSpec(memory_sp...  18.4 us
    all_to_all x1, blocking collectives, to_home(): lax.all_to_all(array, ('y', 'z'), split_axis=0, concat_axis=0, tiled=True)  14.7 us
    ppermute x12, waiting for transfers between devices, send(): return lax.ppermute(array, ('x', 'c'), pairs)  14 us
  transfers between devices with their start and end apart: 14, of which 8 were waited for; matrix products, arithmetic and copies ran while one was open for 0% of the time, Pallas kernels for 11%

profile of v8, /device:TPU:1, one launch (start us, length us, event | category | flops | bytes accessed | tf_op | source)
XLA Modules:
  0.0 113.8 jit_solution(2595196306201535276)
XLA Ops:
  0.0 0.0 copy-start.2
  0.0 0.0 copy-start
  0.0 3.3 %pack_first.1 = (bf16[32,112,128]{2,1,0:T(8,128)(2,1)}, s32[1,512]{1,0:T(1,128)}) custom-call(f32[512,768]{1,0:T(8,128)} %emb_ref.1, s32[1,512]{1,0:T(1,128)} %bitcast.4), custom_call_target="tpu_custom_call" | custom-call | flops 402653184 | bytes 1574912 | tf_op jit(solution)/shard_map/pack_first/pallas_call | solution.py:130
  3.3 0.0 copy-start.1
  3.4 12.0 %all-to-all-start = ((bf16[32,112,128]{2,1,0:T(8,128)(2,1)}), bf16[32,112,128]{2,1,0:T(8,128)(2,1)S(1)}, u32[]{:S(2)}, u32[]{:S(2)}) async-start(bf16[32,112,128]{2,1,0:T(8,128)(2,1)} %get-tuple-element.12), calls=%async_computation | async-start | bytes 1835008 | tf_op jit(solution)/shard_map/all_to_all | solution.py:313
  15.4 0.0 copy-done.2
  15.4 0.0 copy-done.1
  15.4 0.4 pack_table.1.refs_0_
  15.8 1.0 collective-permute-start.3
  16.9 2.5 %collective-permute-start.4 = (bf16[32,16,128]{2,1,0:T(8,128)(2,1)S(1)}, bf16[32,16,128]{2,1,0:T(8,128)(2,1)S(1)}, u32[]{:S(2)}, u32[]{:S(2)}) collective-permute-start(bf16[32,16,128]{2,1,0:T(8,128)(2,1)S(1)} %pack_table.1.refs_0_), channel_id=1, source_target_pairs={{64,0},{72,8},{128,64},{136,72},{200,128},{192,136},{8,192},{0,200... | collective-permute-start | bytes 393224 | tf_op jit(solution)/shard_map/ppermute | solution.py:305
  19.4 0.0 collective-permute-start.5
  19.4 0.0 collective-permute-done.3.refs_1_
  19.4 2.8 %collective-permute-done.4.refs_2_ = bf16[32,16,128]{2,1,0:T(8,128)(2,1)S(1)} collective-permute-done((bf16[32,16,128]{2,1,0:T(8,128)(2,1)S(1)}, bf16[32,16,128]{2,1,0:T(8,128)(2,1)S(1)}, u32[]{:S(2)}, u32[]{:S(2)}) %collective-permute-start.4) | collective-permute-done | bytes 131104 | tf_op jit(solution)/shard_map/ppermute | solution.py:305
  22.1 3.1 %collective-permute-done.5.refs_3_ = bf16[32,16,128]{2,1,0:T(8,128)(2,1)S(1)} collective-permute-done((bf16[32,16,128]{2,1,0:T(8,128)(2,1)S(1)}, bf16[32,16,128]{2,1,0:T(8,128)(2,1)S(1)}, u32[]{:S(2)}, u32[]{:S(2)}) %collective-permute-start.5) | collective-permute-done | bytes 131104 | tf_op jit(solution)/shard_map/ppermute | solution.py:305
  25.2 0.0 copy-done
  25.2 1.7 %pack_second.1 = bf16[32,96,128]{2,1,0:T(8,128)(2,1)} custom-call(f32[512,768]{1,0:T(8,128)S(1)} %copy-done, s32[1,512]{1,0:T(1,128)S(1)} %copy-done.1, bf16[32,16,128]{2,1,0:T(8,128)(2,1)S(1)} %pack_table.1.refs_0_, bf16[32,16,128]{2,1,0:T(8,128)(2,1)S(1)} %collective-permute-done.3.refs_1_, bf16[32,16,128]{2,1,0:T(8,128)(2,1)S(1)} %collective-permute-done.4.refs_2_, ...), custom_call_target="tpu_custom_call" | custom-call | flops 402653184 | bytes 2099200 | tf_op jit(solution)/shard_map/pack_second/pallas_call | solution.py:130
  26.9 10.4 %all-to-all-done.refs_1_.refs_2_ = bf16[32,112,128]{2,1,0:T(8,128)(2,1)S(1)} async-done(((bf16[32,112,128]{2,1,0:T(8,128)(2,1)}), bf16[32,112,128]{2,1,0:T(8,128)(2,1)S(1)}, u32[]{:S(2)}, u32[]{:S(2)}) %all-to-all-start) | async-done | bytes 917536 | tf_op jit(solution)/shard_map/all_to_all | solution.py:313
  37.4 8.5 %all-to-all-start.1 = ((bf16[32,96,128]{2,1,0:T(8,128)(2,1)}), bf16[32,96,128]{2,1,0:T(8,128)(2,1)S(1)}, u32[]{:S(2)}, u32[]{:S(2)}) async-start(bf16[32,96,128]{2,1,0:T(8,128)(2,1)} %pack_second.1), calls=%async_computation.1 | async-start | bytes 1572864 | tf_op jit(solution)/shard_map/all_to_all | solution.py:313
  45.8 1.5 %collective-permute-start.1 = (bf16[32,112,128]{2,1,0:T(8,128)(2,1)S(1)}, bf16[32,112,128]{2,1,0:T(8,128)(2,1)S(1)}, u32[]{:S(2)}, u32[]{:S(2)}) collective-permute-start(bf16[32,112,128]{2,1,0:T(8,128)(2,1)S(1)} %all-to-all-done.refs_1_.refs_2_), channel_id=1, source_target_pairs={{8,0},{0,8},{72,64},{64,72},{136,128},{128,136},{200,192},{192,200... | collective-permute-start | bytes 2752520 | tf_op jit(solution)/shard_map/ppermute | solution.py:305
  47.4 2.5 %collective-permute-start = (bf16[32,112,128]{2,1,0:T(8,128)(2,1)S(1)}, bf16[32,112,128]{2,1,0:T(8,128)(2,1)}, u32[]{:S(2)}, u32[]{:S(2)}) collective-permute-start(bf16[32,112,128]{2,1,0:T(8,128)(2,1)S(1)} %all-to-all-done.refs_1_.refs_2_), channel_id=1, source_target_pairs={{64,0},{72,8},{128,64},{136,72},{200,128},{192,136},{8,192},{0,200... | collective-permute-start | bytes 2752520 | tf_op jit(solution)/shard_map/ppermute | solution.py:305
  49.8 0.0 collective-permute-start.2
  49.8 15.8 %all-to-all-done.1.home_ref = bf16[32,96,128]{2,1,0:T(8,128)(2,1)S(1)} async-done(((bf16[32,96,128]{2,1,0:T(8,128)(2,1)}), bf16[32,96,128]{2,1,0:T(8,128)(2,1)S(1)}, u32[]{:S(2)}, u32[]{:S(2)}) %all-to-all-start.1) | async-done | bytes 786464 | tf_op jit(solution)/shard_map/all_to_all | solution.py:313
  65.6 0.1 cut.1
  65.7 4.6 %collective-permute-start.8 = (bf16[32,80,128]{2,1,0:T(8,128)(2,1)S(1)}, bf16[32,80,128]{2,1,0:T(8,128)(2,1)S(1)}, u32[]{:S(2)}, u32[]{:S(2)}) collective-permute-start(bf16[32,80,128]{2,1,0:T(8,128)(2,1)S(1)} %get-tuple-element.16.refs_2_.refs_3_), channel_id=1, source_target_pairs={{8,0},{0,8},{72,64},{64,72},{136,128},{128,136},{200,192},{192,200... | collective-permute-start | bytes 1966088 | tf_op jit(solution)/shard_map/ppermute | solution.py:305
  70.3 2.5 %collective-permute-start.6 = (bf16[32,80,128]{2,1,0:T(8,128)(2,1)S(1)}, bf16[32,80,128]{2,1,0:T(8,128)(2,1)S(1)}, u32[]{:S(2)}, u32[]{:S(2)}) collective-permute-start(bf16[32,80,128]{2,1,0:T(8,128)(2,1)S(1)} %get-tuple-element.16.refs_2_.refs_3_), channel_id=1, source_target_pairs={{64,0},{72,8},{128,64},{136,72},{200,128},{192,136},{8,192},{0,200... | collective-permute-start | bytes 1966088 | tf_op jit(solution)/shard_map/ppermute | solution.py:305
  72.7 0.0 collective-permute-done.1.refs_2_.refs_3_.refs_4_
  72.7 0.0 collective-permute-start.7
  72.7 0.0 collective-permute-done.refs_0_
  72.7 0.0 collective-permute-done.2.refs_3_
  72.8 4.2 %score_first.1 = (f32[8,512]{1,0:T(8,128)S(1)}, bf16[32,112,128]{2,1,0:T(8,128)(2,1)S(1)}, bf16[32,112,128]{2,1,0:T(8,128)(2,1)S(1)}) custom-call(bf16[32,112,128]{2,1,0:T(8,128)(2,1)} %collective-permute-done.refs_0_, bf16[32,112,128]{2,1,0:T(8,128)(2,1)S(1)} %all-to-all-done.refs_1_.refs_2_, ...), custom_call_target="tpu_custom_call" | custom-call | flops 2013265920 | bytes 3801088 | tf_op jit(solution)/shard_map/score_first/pallas_call | solution.py:130
  77.0 0.0 collective-permute-done.8.refs_4_.refs_5_
  77.0 4.1 %score_second.1.refs_8_ = f32[8,512]{1,0:T(8,128)S(1)} custom-call(bf16[32,112,128]{2,1,0:T(8,128)(2,1)S(1)} %get-tuple-element.15.refs_0_, bf16[32,112,128]{2,1,0:T(8,128)(2,1)S(1)} %all-to-all-done.refs_1_.refs_2_, bf16[32,80,128]{2,1,0:T(8,128)(2,1)S(1)} %get-tuple-element.16.refs_2_.refs_3_, ...), custom_call_target="tpu_custom_call" | custom-call | flops 3221225472 | bytes 5128192 | tf_op jit(solution)/shard_map/score_second/pallas_call | solution.py:130
  81.2 5.6 %collective-permute-done.6.refs_1_ = bf16[32,80,128]{2,1,0:T(8,128)(2,1)S(1)} collective-permute-done((bf16[32,80,128]{2,1,0:T(8,128)(2,1)S(1)}, bf16[32,80,128]{2,1,0:T(8,128)(2,1)S(1)}, u32[]{:S(2)}, u32[]{:S(2)}) %collective-permute-start.6) | collective-permute-done | bytes 655392 | tf_op jit(solution)/shard_map/ppermute | solution.py:305
  86.7 1.7 %score_third.1.refs_5_ = f32[8,512]{1,0:T(8,128)S(1)} custom-call(bf16[32,112,128]{2,1,0:T(8,128)(2,1)S(1)} %get-tuple-element.15.refs_0_, bf16[32,80,128]{2,1,0:T(8,128)(2,1)S(1)} %collective-permute-done.6.refs_1_, bf16[32,112,128]{2,1,0:T(8,128)(2,1)S(1)} %all-to-all-done.refs_1_.refs_2_, bf16[32,80,128]{2,1,0:T(8,128)(2,1)S(1)} %get-tuple-element.16.refs_2_.refs_3_, ...), custom_call_target="tpu_custom_call" | custom-call | flops 1207959552 | bytes 5783552 | tf_op jit(solution)/shard_map/score_third/pallas_call | solution.py:130
  88.5 1.4 %collective-permute-done.7.refs_3_ = bf16[32,80,128]{2,1,0:T(8,128)(2,1)S(1)} collective-permute-done((bf16[32,80,128]{2,1,0:T(8,128)(2,1)S(1)}, bf16[32,80,128]{2,1,0:T(8,128)(2,1)S(1)}, u32[]{:S(2)}, u32[]{:S(2)}) %collective-permute-start.7) | collective-permute-done | bytes 655392 | tf_op jit(solution)/shard_map/ppermute | solution.py:305
  89.8 1.9 %score_fourth.1 = f32[32,1,128]{2,1,0:T(1,128)S(1)} custom-call(bf16[32,112,128]{2,1,0:T(8,128)(2,1)S(1)} %get-tuple-element.15.refs_0_, bf16[32,80,128]{2,1,0:T(8,128)(2,1)S(1)} %collective-permute-done.6.refs_1_, bf16[32,112,128]{2,1,0:T(8,128)(2,1)S(1)} %get-tuple-element.17.refs_5_.refs_6_.refs_2_, ...), custom_call_target="tpu_custom_call" | custom-call | flops 805306368 | bytes 3293184 | tf_op jit(solution)/shard_map/score_fourth/pallas_call | solution.py:130
  91.7 14.7 %all_to_all.15.own_ref = f32[32,1,128]{2,1,0:T(1,128)S(1)} all-to-all(f32[32,1,128]{2,1,0:T(1,128)S(1)} %score_fourth.1), channel_id=1, replica_groups=mesh['x'=4,'y'=4,'c'=2,'z'=8] {'y','z'}, dimensions={0} | all-to-all | bytes 32768 | tf_op jit(solution)/shard_map/all_to_all | solution.py:313
  106.4 0.0 collective-permute-start.10
  106.4 5.2 %collective-permute-start.11 = (f32[32,1,128]{2,1,0:T(1,128)S(1)}, f32[32,1,128]{2,1,0:T(1,128)S(1)}, u32[]{:S(2)}, u32[]{:S(2)}) collective-permute-start(f32[32,1,128]{2,1,0:T(1,128)S(1)} %all_to_all.15.own_ref), channel_id=1, source_target_pairs={{0,192},{8,200},{64,0},{72,8},{128,64},{136,72},{192,128},{200,136... | collective-permute-start | bytes 49160 | tf_op jit(solution)/shard_map/ppermute | solution.py:305
  111.6 0.0 collective-permute-start.9
  111.7 0.0 collective-permute-done.10.next_ref
  111.7 0.9 collective-permute-done.11.last_ref
  112.5 0.3 collective-permute-done.9.swap_ref
  112.8 0.9 finish.1
Async XLA Ops:
  0.0 15.4 %copy-start.2 = (s32[512]{0:T(512)S(1)}, s32[512]{0:T(512)}, u32[]{:S(2)}) copy-start(s32[512]{0:T(512)} %param.5) | copy-start | bytes 6148
  0.0 25.2 %copy-start = (f32[512,768]{1,0:T(8,128)S(1)}, f32[512,768]{1,0:T(8,128)}, u32[]{:S(2)}) copy-start(f32[512,768]{1,0:T(8,128)} %emb_ref.1) | copy-start | bytes 4718596
  3.3 12.1 %copy-start.1 = (s32[1,512]{1,0:T(1,128)S(1)}, s32[1,512]{1,0:T(1,128)}, u32[]{:S(2)}) copy-start(s32[1,512]{1,0:T(1,128)} %get-tuple-element.13.pos_ref) | copy-start | bytes 6148
  3.4 34.0 %all-to-all-start = ((bf16[32,112,128]{2,1,0:T(8,128)(2,1)}), bf16[32,112,128]{2,1,0:T(8,128)(2,1)S(1)}, u32[]{:S(2)}, u32[]{:S(2)}) async-start(bf16[32,112,128]{2,1,0:T(8,128)(2,1)} %get-tuple-element.12), calls=%async_computation | async-start | bytes 1835008 | tf_op jit(solution)/shard_map/all_to_all | solution.py:313
  15.8 3.5 %collective-permute-start.3 = (bf16[32,16,128]{2,1,0:T(8,128)(2,1)S(1)}, bf16[32,16,128]{2,1,0:T(8,128)(2,1)S(1)}, u32[]{:S(2)}, u32[]{:S(2)}) collective-permute-start(bf16[32,16,128]{2,1,0:T(8,128)(2,1)S(1)} %pack_table.1.refs_0_), channel_id=1, source_target_pairs={{8,0},{0,8},{72,64},{64,72},{136,128},{128,136},{200,192},{192,200... | collective-permute-start | bytes 393224 | tf_op jit(solution)/shard_map/ppermute | solution.py:305
  16.9 5.2 %collective-permute-start.4 = (bf16[32,16,128]{2,1,0:T(8,128)(2,1)S(1)}, bf16[32,16,128]{2,1,0:T(8,128)(2,1)S(1)}, u32[]{:S(2)}, u32[]{:S(2)}) collective-permute-start(bf16[32,16,128]{2,1,0:T(8,128)(2,1)S(1)} %pack_table.1.refs_0_), channel_id=1, source_target_pairs={{64,0},{72,8},{128,64},{136,72},{200,128},{192,136},{8,192},{0,200... | collective-permute-start | bytes 393224 | tf_op jit(solution)/shard_map/ppermute | solution.py:305
  19.4 5.9 %collective-permute-start.5 = (bf16[32,16,128]{2,1,0:T(8,128)(2,1)S(1)}, bf16[32,16,128]{2,1,0:T(8,128)(2,1)S(1)}, u32[]{:S(2)}, u32[]{:S(2)}) collective-permute-start(bf16[32,16,128]{2,1,0:T(8,128)(2,1)S(1)} %pack_table.1.refs_0_), channel_id=1, source_target_pairs={{192,0},{200,8},{0,64},{8,72},{64,128},{72,136},{128,192},{136,200... | collective-permute-start | bytes 393224 | tf_op jit(solution)/shard_map/ppermute | solution.py:305
  37.4 28.3 %all-to-all-start.1 = ((bf16[32,96,128]{2,1,0:T(8,128)(2,1)}), bf16[32,96,128]{2,1,0:T(8,128)(2,1)S(1)}, u32[]{:S(2)}, u32[]{:S(2)}) async-start(bf16[32,96,128]{2,1,0:T(8,128)(2,1)} %pack_second.1), calls=%async_computation.1 | async-start | bytes 1572864 | tf_op jit(solution)/shard_map/all_to_all | solution.py:313
  45.8 26.9 %collective-permute-start.1 = (bf16[32,112,128]{2,1,0:T(8,128)(2,1)S(1)}, bf16[32,112,128]{2,1,0:T(8,128)(2,1)S(1)}, u32[]{:S(2)}, u32[]{:S(2)}) collective-permute-start(bf16[32,112,128]{2,1,0:T(8,128)(2,1)S(1)} %all-to-all-done.refs_1_.refs_2_), channel_id=1, source_target_pairs={{8,0},{0,8},{72,64},{64,72},{136,128},{128,136},{200,192},{192,200... | collective-permute-start | bytes 2752520 | tf_op jit(solution)/shard_map/ppermute | solution.py:305
  47.4 25.4 %collective-permute-start = (bf16[32,112,128]{2,1,0:T(8,128)(2,1)S(1)}, bf16[32,112,128]{2,1,0:T(8,128)(2,1)}, u32[]{:S(2)}, u32[]{:S(2)}) collective-permute-start(bf16[32,112,128]{2,1,0:T(8,128)(2,1)S(1)} %all-to-all-done.refs_1_.refs_2_), channel_id=1, source_target_pairs={{64,0},{72,8},{128,64},{136,72},{200,128},{192,136},{8,192},{0,200... | collective-permute-start | bytes 2752520 | tf_op jit(solution)/shard_map/ppermute | solution.py:305
  49.8 22.9 %collective-permute-start.2 = (bf16[32,112,128]{2,1,0:T(8,128)(2,1)S(1)}, bf16[32,112,128]{2,1,0:T(8,128)(2,1)}, u32[]{:S(2)}, u32[]{:S(2)}) collective-permute-start(bf16[32,112,128]{2,1,0:T(8,128)(2,1)S(1)} %all-to-all-done.refs_1_.refs_2_), channel_id=1, source_target_pairs={{192,0},{200,8},{0,64},{8,72},{64,128},{72,136},{128,192},{136,200... | collective-permute-start | bytes 2752520 | tf_op jit(solution)/shard_map/ppermute | solution.py:305
  65.7 11.3 %collective-permute-start.8 = (bf16[32,80,128]{2,1,0:T(8,128)(2,1)S(1)}, bf16[32,80,128]{2,1,0:T(8,128)(2,1)S(1)}, u32[]{:S(2)}, u32[]{:S(2)}) collective-permute-start(bf16[32,80,128]{2,1,0:T(8,128)(2,1)S(1)} %get-tuple-element.16.refs_2_.refs_3_), channel_id=1, source_target_pairs={{8,0},{0,8},{72,64},{64,72},{136,128},{128,136},{200,192},{192,200... | collective-permute-start | bytes 1966088 | tf_op jit(solution)/shard_map/ppermute | solution.py:305
  70.3 16.5 %collective-permute-start.6 = (bf16[32,80,128]{2,1,0:T(8,128)(2,1)S(1)}, bf16[32,80,128]{2,1,0:T(8,128)(2,1)S(1)}, u32[]{:S(2)}, u32[]{:S(2)}) collective-permute-start(bf16[32,80,128]{2,1,0:T(8,128)(2,1)S(1)} %get-tuple-element.16.refs_2_.refs_3_), channel_id=1, source_target_pairs={{64,0},{72,8},{128,64},{136,72},{200,128},{192,136},{8,192},{0,200... | collective-permute-start | bytes 1966088 | tf_op jit(solution)/shard_map/ppermute | solution.py:305
  72.7 17.1 %collective-permute-start.7 = (bf16[32,80,128]{2,1,0:T(8,128)(2,1)S(1)}, bf16[32,80,128]{2,1,0:T(8,128)(2,1)S(1)}, u32[]{:S(2)}, u32[]{:S(2)}) collective-permute-start(bf16[32,80,128]{2,1,0:T(8,128)(2,1)S(1)} %get-tuple-element.16.refs_2_.refs_3_), channel_id=1, source_target_pairs={{192,0},{200,8},{0,64},{8,72},{64,128},{72,136},{128,192},{136,200... | collective-permute-start | bytes 1966088 | tf_op jit(solution)/shard_map/ppermute | solution.py:305
  106.4 5.3 %collective-permute-start.10 = (f32[32,1,128]{2,1,0:T(1,128)S(1)}, f32[32,1,128]{2,1,0:T(1,128)S(1)}, u32[]{:S(2)}, u32[]{:S(2)}) collective-permute-start(f32[32,1,128]{2,1,0:T(1,128)S(1)} %all_to_all.15.own_ref), channel_id=1, source_target_pairs={{0,64},{8,72},{64,128},{72,136},{128,200},{136,192},{192,8},{200,0... | collective-permute-start | bytes 49160 | tf_op jit(solution)/shard_map/ppermute | solution.py:305
  106.4 6.1 %collective-permute-start.11 = (f32[32,1,128]{2,1,0:T(1,128)S(1)}, f32[32,1,128]{2,1,0:T(1,128)S(1)}, u32[]{:S(2)}, u32[]{:S(2)}) collective-permute-start(f32[32,1,128]{2,1,0:T(1,128)S(1)} %all_to_all.15.own_ref), channel_id=1, source_target_pairs={{0,192},{8,200},{64,0},{72,8},{128,64},{136,72},{192,128},{200,136... | collective-permute-start | bytes 49160 | tf_op jit(solution)/shard_map/ppermute | solution.py:305
  111.6 1.2 %collective-permute-start.9 = (f32[32,1,128]{2,1,0:T(1,128)S(1)}, f32[32,1,128]{2,1,0:T(1,128)S(1)}, u32[]{:S(2)}, u32[]{:S(2)}) collective-permute-start(f32[32,1,128]{2,1,0:T(1,128)S(1)} %all_to_all.15.own_ref), channel_id=1, source_target_pairs={{0,8},{8,0},{64,72},{72,64},{128,136},{136,128},{192,200},{200,192... | collective-permute-start | bytes 49160 | tf_op jit(solution)/shard_map/ppermute | solution.py:305

commit v9 on v8

--- a/solution.py
+++ b/solution.py
@@ -16,7 +16,7 @@
 PARTS = D // 128
 SIZE = {"x": 4, "y": 4, "c": 2, "z": 8}
 EARLY = 1
-CUTS = 4
+CUTS = 2
 LIMIT = 24 * 1024 * 1024
 NT = (((1,), (1,)), ((), ()))
 NN = (((1,), (0,)), ((), ()))
@@ -274,20 +274,17 @@
 
 
 def finish_kernel(own_ref, swap_ref, next_ref, last_ref, pos_ref, out_ref):
-    block = iota((GROUPS, 128), 1) // SLOTS
-    mine = last_ref[...].reshape(GROUPS, 128)
-    for index, ref in enumerate((own_ref, swap_ref, next_ref)):
-        mine = jnp.where(block == index, ref[...].reshape(GROUPS, 128), mine)
+    mine = own_ref[...].reshape(GROUPS, 128)
+    for index, ref in enumerate((swap_ref, next_ref, last_ref), 1):
+        lanes = ref[...].reshape(GROUPS, 128)
+        mine = jnp.maximum(mine, pltpu.roll(lanes, 128 - SLOTS * index, 1))
     position = pos_ref[...]
     member = bits(iota((GROUPS, ROWS), 0) == position // SLOTS)
-    found = jnp.zeros((128, ROWS), jnp.float32)
-    for part in three_parts(mine):
+    found = jnp.zeros((SLOTS, ROWS), jnp.float32)
+    for part in three_parts(mine[:, :SLOTS]):
         found += dot(part, member, TN)
-    best = functools.reduce(
-        jnp.maximum, [found[SLOTS * index : SLOTS * (index + 1)] for index in range(4)]
-    )
     here = iota((SLOTS, ROWS), 0) == (position & (SLOTS - 1))
-    out_ref[...] = jnp.sum(jnp.where(here, best, 0.0), axis=0, keepdims=True)
+    out_ref[...] = jnp.sum(jnp.where(here, found, 0.0), axis=0, keepdims=True)
 
 
 FROM_NEXT = [

time: 114 us -> 114 us (level)
  no operation moved by 1% of the time
where the time goes in v9:
time: 114 us
  starting transfers between devices  40.3 us (35%)
  waiting for transfers between devices  40.2 us (35%)
  Pallas kernels  18.2 us (16%)
  blocking collectives  14.7 us (13%)
    all_to_all x2, waiting for transfers between devices, to_home(): lax.all_to_all(array, ('y', 'z'), split_axis=0, concat_axis=0, tiled=True)  26.2 us
    all_to_all x2, starting transfers between devices, to_home(): lax.all_to_all(array, ('y', 'z'), split_axis=0, concat_axis=0, tiled=True)  20.5 us
    ppermute x12, starting transfers between devices, send(): return lax.ppermute(array, ('x', 'c'), pairs)  19.8 us
    pallas_call x9, Pallas kernels, call(): pl.pallas_call(kernel, out_shape=shapes, in_specs=[pl.BlockSpec(memory_sp...  18.2 us
    all_to_all x1, blocking collectives, to_home(): lax.all_to_all(array, ('y', 'z'), split_axis=0, concat_axis=0, tiled=True)  14.7 us
    ppermute x12, waiting for transfers between devices, send(): return lax.ppermute(array, ('x', 'c'), pairs)  14 us
  transfers between devices with their start and end apart: 14, of which 8 were waited for; matrix products, arithmetic and copies ran while one was open for 0% of the time, Pallas kernels for 11%

profile of v9, /device:TPU:1, one launch (start us, length us, event | category | flops | bytes accessed | tf_op | source)
XLA Modules:
  0.0 113.6 jit_solution(16208659034170719571)
XLA Ops:
  0.0 0.0 copy-start.2
  0.0 0.0 copy-start
  0.0 3.2 %pack_first.1 = (bf16[32,112,128]{2,1,0:T(8,128)(2,1)}, s32[1,512]{1,0:T(1,128)}) custom-call(f32[512,768]{1,0:T(8,128)} %emb_ref.1, s32[1,512]{1,0:T(1,128)} %bitcast.4), custom_call_target="tpu_custom_call" | custom-call | flops 402653184 | bytes 1574912 | tf_op jit(solution)/shard_map/pack_first/pallas_call | solution.py:130
  3.2 0.0 copy-start.1
  3.2 12.0 %all-to-all-start = ((bf16[32,112,128]{2,1,0:T(8,128)(2,1)}), bf16[32,112,128]{2,1,0:T(8,128)(2,1)S(1)}, u32[]{:S(2)}, u32[]{:S(2)}) async-start(bf16[32,112,128]{2,1,0:T(8,128)(2,1)} %get-tuple-element.12), calls=%async_computation | async-start | bytes 1835008 | tf_op jit(solution)/shard_map/all_to_all | solution.py:310
  15.3 0.0 copy-done.2
  15.3 0.0 copy-done.1
  15.3 0.4 pack_table.1.refs_0_
  15.7 1.0 collective-permute-start.3
  16.8 2.5 %collective-permute-start.4 = (bf16[32,16,128]{2,1,0:T(8,128)(2,1)S(1)}, bf16[32,16,128]{2,1,0:T(8,128)(2,1)S(1)}, u32[]{:S(2)}, u32[]{:S(2)}) collective-permute-start(bf16[32,16,128]{2,1,0:T(8,128)(2,1)S(1)} %pack_table.1.refs_0_), channel_id=1, source_target_pairs={{64,0},{72,8},{128,64},{136,72},{200,128},{192,136},{8,192},{0,200... | collective-permute-start | bytes 393224 | tf_op jit(solution)/shard_map/ppermute | solution.py:302
  19.2 0.0 collective-permute-start.5
  19.2 0.0 collective-permute-done.3.refs_1_
  19.2 2.8 %collective-permute-done.4.refs_2_ = bf16[32,16,128]{2,1,0:T(8,128)(2,1)S(1)} collective-permute-done((bf16[32,16,128]{2,1,0:T(8,128)(2,1)S(1)}, bf16[32,16,128]{2,1,0:T(8,128)(2,1)S(1)}, u32[]{:S(2)}, u32[]{:S(2)}) %collective-permute-start.4) | collective-permute-done | bytes 131104 | tf_op jit(solution)/shard_map/ppermute | solution.py:302
  22.0 3.1 %collective-permute-done.5.refs_3_ = bf16[32,16,128]{2,1,0:T(8,128)(2,1)S(1)} collective-permute-done((bf16[32,16,128]{2,1,0:T(8,128)(2,1)S(1)}, bf16[32,16,128]{2,1,0:T(8,128)(2,1)S(1)}, u32[]{:S(2)}, u32[]{:S(2)}) %collective-permute-start.5) | collective-permute-done | bytes 131104 | tf_op jit(solution)/shard_map/ppermute | solution.py:302
  25.1 0.0 copy-done
  25.1 1.7 %pack_second.1 = bf16[32,96,128]{2,1,0:T(8,128)(2,1)} custom-call(f32[512,768]{1,0:T(8,128)S(1)} %copy-done, s32[1,512]{1,0:T(1,128)S(1)} %copy-done.1, bf16[32,16,128]{2,1,0:T(8,128)(2,1)S(1)} %pack_table.1.refs_0_, bf16[32,16,128]{2,1,0:T(8,128)(2,1)S(1)} %collective-permute-done.3.refs_1_, bf16[32,16,128]{2,1,0:T(8,128)(2,1)S(1)} %collective-permute-done.4.refs_2_, ...), custom_call_target="tpu_custom_call" | custom-call | flops 402653184 | bytes 2099200 | tf_op jit(solution)/shard_map/pack_second/pallas_call | solution.py:130
  26.8 10.4 %all-to-all-done.refs_1_.refs_2_ = bf16[32,112,128]{2,1,0:T(8,128)(2,1)S(1)} async-done(((bf16[32,112,128]{2,1,0:T(8,128)(2,1)}), bf16[32,112,128]{2,1,0:T(8,128)(2,1)S(1)}, u32[]{:S(2)}, u32[]{:S(2)}) %all-to-all-start) | async-done | bytes 917536 | tf_op jit(solution)/shard_map/all_to_all | solution.py:310
  37.2 8.5 %all-to-all-start.1 = ((bf16[32,96,128]{2,1,0:T(8,128)(2,1)}), bf16[32,96,128]{2,1,0:T(8,128)(2,1)S(1)}, u32[]{:S(2)}, u32[]{:S(2)}) async-start(bf16[32,96,128]{2,1,0:T(8,128)(2,1)} %pack_second.1), calls=%async_computation.1 | async-start | bytes 1572864 | tf_op jit(solution)/shard_map/all_to_all | solution.py:310
  45.7 1.5 %collective-permute-start.1 = (bf16[32,112,128]{2,1,0:T(8,128)(2,1)S(1)}, bf16[32,112,128]{2,1,0:T(8,128)(2,1)S(1)}, u32[]{:S(2)}, u32[]{:S(2)}) collective-permute-start(bf16[32,112,128]{2,1,0:T(8,128)(2,1)S(1)} %all-to-all-done.refs_1_.refs_2_), channel_id=1, source_target_pairs={{8,0},{0,8},{72,64},{64,72},{136,128},{128,136},{200,192},{192,200... | collective-permute-start | bytes 2752520 | tf_op jit(solution)/shard_map/ppermute | solution.py:302
  47.2 2.5 %collective-permute-start = (bf16[32,112,128]{2,1,0:T(8,128)(2,1)S(1)}, bf16[32,112,128]{2,1,0:T(8,128)(2,1)}, u32[]{:S(2)}, u32[]{:S(2)}) collective-permute-start(bf16[32,112,128]{2,1,0:T(8,128)(2,1)S(1)} %all-to-all-done.refs_1_.refs_2_), channel_id=1, source_target_pairs={{64,0},{72,8},{128,64},{136,72},{200,128},{192,136},{8,192},{0,200... | collective-permute-start | bytes 2752520 | tf_op jit(solution)/shard_map/ppermute | solution.py:302
  49.7 0.0 collective-permute-start.2
  49.7 15.8 %all-to-all-done.1.home_ref = bf16[32,96,128]{2,1,0:T(8,128)(2,1)S(1)} async-done(((bf16[32,96,128]{2,1,0:T(8,128)(2,1)}), bf16[32,96,128]{2,1,0:T(8,128)(2,1)S(1)}, u32[]{:S(2)}, u32[]{:S(2)}) %all-to-all-start.1) | async-done | bytes 786464 | tf_op jit(solution)/shard_map/all_to_all | solution.py:310
  65.5 0.1 cut.1
  65.5 4.6 %collective-permute-start.8 = (bf16[32,80,128]{2,1,0:T(8,128)(2,1)S(1)}, bf16[32,80,128]{2,1,0:T(8,128)(2,1)S(1)}, u32[]{:S(2)}, u32[]{:S(2)}) collective-permute-start(bf16[32,80,128]{2,1,0:T(8,128)(2,1)S(1)} %get-tuple-element.16.refs_2_.refs_3_), channel_id=1, source_target_pairs={{8,0},{0,8},{72,64},{64,72},{136,128},{128,136},{200,192},{192,200... | collective-permute-start | bytes 1966088 | tf_op jit(solution)/shard_map/ppermute | solution.py:302
  70.1 2.5 %collective-permute-start.6 = (bf16[32,80,128]{2,1,0:T(8,128)(2,1)S(1)}, bf16[32,80,128]{2,1,0:T(8,128)(2,1)S(1)}, u32[]{:S(2)}, u32[]{:S(2)}) collective-permute-start(bf16[32,80,128]{2,1,0:T(8,128)(2,1)S(1)} %get-tuple-element.16.refs_2_.refs_3_), channel_id=1, source_target_pairs={{64,0},{72,8},{128,64},{136,72},{200,128},{192,136},{8,192},{0,200... | collective-permute-start | bytes 1966088 | tf_op jit(solution)/shard_map/ppermute | solution.py:302
  72.6 0.0 collective-permute-done.1.refs_2_.refs_3_.refs_4_
  72.6 0.0 collective-permute-start.7
  72.6 0.0 collective-permute-done.refs_0_
  72.6 0.0 collective-permute-done.2.refs_3_
  72.6 4.2 %score_first.1 = (f32[8,512]{1,0:T(8,128)S(1)}, bf16[32,112,128]{2,1,0:T(8,128)(2,1)S(1)}, bf16[32,112,128]{2,1,0:T(8,128)(2,1)S(1)}) custom-call(bf16[32,112,128]{2,1,0:T(8,128)(2,1)} %collective-permute-done.refs_0_, bf16[32,112,128]{2,1,0:T(8,128)(2,1)S(1)} %all-to-all-done.refs_1_.refs_2_, ...), custom_call_target="tpu_custom_call" | custom-call | flops 2013265920 | bytes 3801088 | tf_op jit(solution)/shard_map/score_first/pallas_call | solution.py:130
  76.8 0.0 collective-permute-done.8.refs_4_.refs_5_
  76.9 4.1 %score_second.1.refs_8_ = f32[8,512]{1,0:T(8,128)S(1)} custom-call(bf16[32,112,128]{2,1,0:T(8,128)(2,1)S(1)} %get-tuple-element.15.refs_0_, bf16[32,112,128]{2,1,0:T(8,128)(2,1)S(1)} %all-to-all-done.refs_1_.refs_2_, bf16[32,80,128]{2,1,0:T(8,128)(2,1)S(1)} %get-tuple-element.16.refs_2_.refs_3_, ...), custom_call_target="tpu_custom_call" | custom-call | flops 3221225472 | bytes 5128192 | tf_op jit(solution)/shard_map/score_second/pallas_call | solution.py:130
  81.0 5.6 %collective-permute-done.6.refs_1_ = bf16[32,80,128]{2,1,0:T(8,128)(2,1)S(1)} collective-permute-done((bf16[32,80,128]{2,1,0:T(8,128)(2,1)S(1)}, bf16[32,80,128]{2,1,0:T(8,128)(2,1)S(1)}, u32[]{:S(2)}, u32[]{:S(2)}) %collective-permute-start.6) | collective-permute-done | bytes 655392 | tf_op jit(solution)/shard_map/ppermute | solution.py:302
  86.6 1.7 %score_third.1.refs_5_ = f32[8,512]{1,0:T(8,128)S(1)} custom-call(bf16[32,112,128]{2,1,0:T(8,128)(2,1)S(1)} %get-tuple-element.15.refs_0_, bf16[32,80,128]{2,1,0:T(8,128)(2,1)S(1)} %collective-permute-done.6.refs_1_, bf16[32,112,128]{2,1,0:T(8,128)(2,1)S(1)} %all-to-all-done.refs_1_.refs_2_, bf16[32,80,128]{2,1,0:T(8,128)(2,1)S(1)} %get-tuple-element.16.refs_2_.refs_3_, ...), custom_call_target="tpu_custom_call" | custom-call | flops 1207959552 | bytes 5783552 | tf_op jit(solution)/shard_map/score_third/pallas_call | solution.py:130
  88.3 1.4 %collective-permute-done.7.refs_3_ = bf16[32,80,128]{2,1,0:T(8,128)(2,1)S(1)} collective-permute-done((bf16[32,80,128]{2,1,0:T(8,128)(2,1)S(1)}, bf16[32,80,128]{2,1,0:T(8,128)(2,1)S(1)}, u32[]{:S(2)}, u32[]{:S(2)}) %collective-permute-start.7) | collective-permute-done | bytes 655392 | tf_op jit(solution)/shard_map/ppermute | solution.py:302
  89.7 1.9 %score_fourth.1 = f32[32,1,128]{2,1,0:T(1,128)S(1)} custom-call(bf16[32,112,128]{2,1,0:T(8,128)(2,1)S(1)} %get-tuple-element.15.refs_0_, bf16[32,80,128]{2,1,0:T(8,128)(2,1)S(1)} %collective-permute-done.6.refs_1_, bf16[32,112,128]{2,1,0:T(8,128)(2,1)S(1)} %get-tuple-element.17.refs_5_.refs_6_.refs_2_, ...), custom_call_target="tpu_custom_call" | custom-call | flops 805306368 | bytes 3293184 | tf_op jit(solution)/shard_map/score_fourth/pallas_call | solution.py:130
  91.5 14.7 %all_to_all.15.own_ref = f32[32,1,128]{2,1,0:T(1,128)S(1)} all-to-all(f32[32,1,128]{2,1,0:T(1,128)S(1)} %score_fourth.1), channel_id=1, replica_groups=mesh['x'=4,'y'=4,'c'=2,'z'=8] {'y','z'}, dimensions={0} | all-to-all | bytes 32768 | tf_op jit(solution)/shard_map/all_to_all | solution.py:310
  106.3 0.0 collective-permute-start.10
  106.3 5.3 %collective-permute-start.11 = (f32[32,1,128]{2,1,0:T(1,128)S(1)}, f32[32,1,128]{2,1,0:T(1,128)S(1)}, u32[]{:S(2)}, u32[]{:S(2)}) collective-permute-start(f32[32,1,128]{2,1,0:T(1,128)S(1)} %all_to_all.15.own_ref), channel_id=1, source_target_pairs={{0,192},{8,200},{64,0},{72,8},{128,64},{136,72},{192,128},{200,136... | collective-permute-start | bytes 49160 | tf_op jit(solution)/shard_map/ppermute | solution.py:302
  111.5 0.0 collective-permute-start.9
  111.5 0.0 collective-permute-done.10.next_ref
  111.5 0.9 collective-permute-done.11.last_ref
  112.4 0.3 collective-permute-done.9.swap_ref
  112.7 0.9 finish.1
Async XLA Ops:
  0.0 15.3 %copy-start.2 = (s32[512]{0:T(512)S(1)}, s32[512]{0:T(512)}, u32[]{:S(2)}) copy-start(s32[512]{0:T(512)} %param.5) | copy-start | bytes 6148
  0.0 25.1 %copy-start = (f32[512,768]{1,0:T(8,128)S(1)}, f32[512,768]{1,0:T(8,128)}, u32[]{:S(2)}) copy-start(f32[512,768]{1,0:T(8,128)} %emb_ref.1) | copy-start | bytes 4718596
  3.2 12.1 %copy-start.1 = (s32[1,512]{1,0:T(1,128)S(1)}, s32[1,512]{1,0:T(1,128)}, u32[]{:S(2)}) copy-start(s32[1,512]{1,0:T(1,128)} %get-tuple-element.13.pos_ref) | copy-start | bytes 6148
  3.2 34.0 %all-to-all-start = ((bf16[32,112,128]{2,1,0:T(8,128)(2,1)}), bf16[32,112,128]{2,1,0:T(8,128)(2,1)S(1)}, u32[]{:S(2)}, u32[]{:S(2)}) async-start(bf16[32,112,128]{2,1,0:T(8,128)(2,1)} %get-tuple-element.12), calls=%async_computation | async-start | bytes 1835008 | tf_op jit(solution)/shard_map/all_to_all | solution.py:310
  15.7 3.5 %collective-permute-start.3 = (bf16[32,16,128]{2,1,0:T(8,128)(2,1)S(1)}, bf16[32,16,128]{2,1,0:T(8,128)(2,1)S(1)}, u32[]{:S(2)}, u32[]{:S(2)}) collective-permute-start(bf16[32,16,128]{2,1,0:T(8,128)(2,1)S(1)} %pack_table.1.refs_0_), channel_id=1, source_target_pairs={{8,0},{0,8},{72,64},{64,72},{136,128},{128,136},{200,192},{192,200... | collective-permute-start | bytes 393224 | tf_op jit(solution)/shard_map/ppermute | solution.py:302
  16.8 5.2 %collective-permute-start.4 = (bf16[32,16,128]{2,1,0:T(8,128)(2,1)S(1)}, bf16[32,16,128]{2,1,0:T(8,128)(2,1)S(1)}, u32[]{:S(2)}, u32[]{:S(2)}) collective-permute-start(bf16[32,16,128]{2,1,0:T(8,128)(2,1)S(1)} %pack_table.1.refs_0_), channel_id=1, source_target_pairs={{64,0},{72,8},{128,64},{136,72},{200,128},{192,136},{8,192},{0,200... | collective-permute-start | bytes 393224 | tf_op jit(solution)/shard_map/ppermute | solution.py:302
  19.2 5.9 %collective-permute-start.5 = (bf16[32,16,128]{2,1,0:T(8,128)(2,1)S(1)}, bf16[32,16,128]{2,1,0:T(8,128)(2,1)S(1)}, u32[]{:S(2)}, u32[]{:S(2)}) collective-permute-start(bf16[32,16,128]{2,1,0:T(8,128)(2,1)S(1)} %pack_table.1.refs_0_), channel_id=1, source_target_pairs={{192,0},{200,8},{0,64},{8,72},{64,128},{72,136},{128,192},{136,200... | collective-permute-start | bytes 393224 | tf_op jit(solution)/shard_map/ppermute | solution.py:302
  37.2 28.2 %all-to-all-start.1 = ((bf16[32,96,128]{2,1,0:T(8,128)(2,1)}), bf16[32,96,128]{2,1,0:T(8,128)(2,1)S(1)}, u32[]{:S(2)}, u32[]{:S(2)}) async-start(bf16[32,96,128]{2,1,0:T(8,128)(2,1)} %pack_second.1), calls=%async_computation.1 | async-start | bytes 1572864 | tf_op jit(solution)/shard_map/all_to_all | solution.py:310
  45.7 26.9 %collective-permute-start.1 = (bf16[32,112,128]{2,1,0:T(8,128)(2,1)S(1)}, bf16[32,112,128]{2,1,0:T(8,128)(2,1)S(1)}, u32[]{:S(2)}, u32[]{:S(2)}) collective-permute-start(bf16[32,112,128]{2,1,0:T(8,128)(2,1)S(1)} %all-to-all-done.refs_1_.refs_2_), channel_id=1, source_target_pairs={{8,0},{0,8},{72,64},{64,72},{136,128},{128,136},{200,192},{192,200... | collective-permute-start | bytes 2752520 | tf_op jit(solution)/shard_map/ppermute | solution.py:302
  47.2 25.4 %collective-permute-start = (bf16[32,112,128]{2,1,0:T(8,128)(2,1)S(1)}, bf16[32,112,128]{2,1,0:T(8,128)(2,1)}, u32[]{:S(2)}, u32[]{:S(2)}) collective-permute-start(bf16[32,112,128]{2,1,0:T(8,128)(2,1)S(1)} %all-to-all-done.refs_1_.refs_2_), channel_id=1, source_target_pairs={{64,0},{72,8},{128,64},{136,72},{200,128},{192,136},{8,192},{0,200... | collective-permute-start | bytes 2752520 | tf_op jit(solution)/shard_map/ppermute | solution.py:302
  49.7 22.9 %collective-permute-start.2 = (bf16[32,112,128]{2,1,0:T(8,128)(2,1)S(1)}, bf16[32,112,128]{2,1,0:T(8,128)(2,1)}, u32[]{:S(2)}, u32[]{:S(2)}) collective-permute-start(bf16[32,112,128]{2,1,0:T(8,128)(2,1)S(1)} %all-to-all-done.refs_1_.refs_2_), channel_id=1, source_target_pairs={{192,0},{200,8},{0,64},{8,72},{64,128},{72,136},{128,192},{136,200... | collective-permute-start | bytes 2752520 | tf_op jit(solution)/shard_map/ppermute | solution.py:302
  65.5 11.3 %collective-permute-start.8 = (bf16[32,80,128]{2,1,0:T(8,128)(2,1)S(1)}, bf16[32,80,128]{2,1,0:T(8,128)(2,1)S(1)}, u32[]{:S(2)}, u32[]{:S(2)}) collective-permute-start(bf16[32,80,128]{2,1,0:T(8,128)(2,1)S(1)} %get-tuple-element.16.refs_2_.refs_3_), channel_id=1, source_target_pairs={{8,0},{0,8},{72,64},{64,72},{136,128},{128,136},{200,192},{192,200... | collective-permute-start | bytes 1966088 | tf_op jit(solution)/shard_map/ppermute | solution.py:302
  70.1 16.5 %collective-permute-start.6 = (bf16[32,80,128]{2,1,0:T(8,128)(2,1)S(1)}, bf16[32,80,128]{2,1,0:T(8,128)(2,1)S(1)}, u32[]{:S(2)}, u32[]{:S(2)}) collective-permute-start(bf16[32,80,128]{2,1,0:T(8,128)(2,1)S(1)} %get-tuple-element.16.refs_2_.refs_3_), channel_id=1, source_target_pairs={{64,0},{72,8},{128,64},{136,72},{200,128},{192,136},{8,192},{0,200... | collective-permute-start | bytes 1966088 | tf_op jit(solution)/shard_map/ppermute | solution.py:302
  72.6 17.1 %collective-permute-start.7 = (bf16[32,80,128]{2,1,0:T(8,128)(2,1)S(1)}, bf16[32,80,128]{2,1,0:T(8,128)(2,1)S(1)}, u32[]{:S(2)}, u32[]{:S(2)}) collective-permute-start(bf16[32,80,128]{2,1,0:T(8,128)(2,1)S(1)} %get-tuple-element.16.refs_2_.refs_3_), channel_id=1, source_target_pairs={{192,0},{200,8},{0,64},{8,72},{64,128},{72,136},{128,192},{136,200... | collective-permute-start | bytes 1966088 | tf_op jit(solution)/shard_map/ppermute | solution.py:302
  106.3 5.3 %collective-permute-start.10 = (f32[32,1,128]{2,1,0:T(1,128)S(1)}, f32[32,1,128]{2,1,0:T(1,128)S(1)}, u32[]{:S(2)}, u32[]{:S(2)}) collective-permute-start(f32[32,1,128]{2,1,0:T(1,128)S(1)} %all_to_all.15.own_ref), channel_id=1, source_target_pairs={{0,64},{8,72},{64,128},{72,136},{128,200},{136,192},{192,8},{200,0... | collective-permute-start | bytes 49160 | tf_op jit(solution)/shard_map/ppermute | solution.py:302
  106.3 6.1 %collective-permute-start.11 = (f32[32,1,128]{2,1,0:T(1,128)S(1)}, f32[32,1,128]{2,1,0:T(1,128)S(1)}, u32[]{:S(2)}, u32[]{:S(2)}) collective-permute-start(f32[32,1,128]{2,1,0:T(1,128)S(1)} %all_to_all.15.own_ref), channel_id=1, source_target_pairs={{0,192},{8,200},{64,0},{72,8},{128,64},{136,72},{192,128},{200,136... | collective-permute-start | bytes 49160 | tf_op jit(solution)/shard_map/ppermute | solution.py:302
  111.5 1.2 %collective-permute-start.9 = (f32[32,1,128]{2,1,0:T(1,128)S(1)}, f32[32,1,128]{2,1,0:T(1,128)S(1)}, u32[]{:S(2)}, u32[]{:S(2)}) collective-permute-start(f32[32,1,128]{2,1,0:T(1,128)S(1)} %all_to_all.15.own_ref), channel_id=1, source_target_pairs={{0,8},{8,0},{64,72},{72,64},{128,136},{136,128},{192,200},{200,192... | collective-permute-start | bytes 49160 | tf_op jit(solution)/shard_map/ppermute | solution.py:302

commit v10 on v9

--- a/solution.py
+++ b/solution.py
@@ -169,14 +169,12 @@
 
 
 def homeward(best):
-    stacked = jnp.concatenate(best, axis=0)
-    widen = bits(iota((8, 128), 1) // HALF == iota((8, 128), 0))
-    own_lane = iota((PART, 128), 1) % HALF == iota((PART, 128), 0) % HALF
+    wide = jnp.concatenate([jnp.broadcast_to(row, (HALF, PART)) for row in best], axis=0)
+    own_slot = iota((128, PART), 0) % HALF == iota((128, PART), 1) % HALF
     gather = bits(iota((GROUPS, PART), 1) // HALF == iota((GROUPS, PART), 0))
     total = jnp.zeros((GROUPS, 128), jnp.float32)
-    for part in three_parts(stacked):
-        lanes = jnp.where(own_lane, dot(part, widen, TN), 0.0).astype(jnp.bfloat16)
-        total += dot(gather, lanes, NN)
+    for part in three_parts(jnp.where(own_slot, wide, 0.0)):
+        total += dot(gather, part, NT)
     return total
 
 

time: 114 us -> 114 us (level)
  no operation moved by 1% of the time
where the time goes in v10:
time: 114 us; the launch traced here: 113 us
  starting transfers between devices  40.3 us (35%)
  waiting for transfers between devices  40.2 us (35%)
  Pallas kernels  18 us (16%)
  blocking collectives  14.7 us (13%)
    all_to_all x2, waiting for transfers between devices, to_home(): lax.all_to_all(array, ('y', 'z'), split_axis=0, concat_axis=0, tiled=True)  26.2 us
    all_to_all x2, starting transfers between devices, to_home(): lax.all_to_all(array, ('y', 'z'), split_axis=0, concat_axis=0, tiled=True)  20.5 us
    ppermute x12, starting transfers between devices, send(): return lax.ppermute(array, ('x', 'c'), pairs)  19.8 us
    pallas_call x9, Pallas kernels, call(): pl.pallas_call(kernel, out_shape=shapes, in_specs=[pl.BlockSpec(memory_sp...  18 us
    all_to_all x1, blocking collectives, to_home(): lax.all_to_all(array, ('y', 'z'), split_axis=0, concat_axis=0, tiled=True)  14.7 us
    ppermute x12, waiting for transfers between devices, send(): return lax.ppermute(array, ('x', 'c'), pairs)  14 us
  transfers between devices with their start and end apart: 14, of which 8 were waited for; matrix products, arithmetic and copies ran while one was open for 0% of the time, Pallas kernels for 11%

profile of v10, /device:TPU:1, one launch (start us, length us, event | category | flops | bytes accessed | tf_op | source)
XLA Modules:
  0.0 113.4 jit_solution(12440584664100894701)
XLA Ops:
  0.0 0.0 copy-start.2
  0.0 0.0 copy-start
  0.0 3.2 %pack_first.1 = (bf16[32,112,128]{2,1,0:T(8,128)(2,1)}, s32[1,512]{1,0:T(1,128)}) custom-call(f32[512,768]{1,0:T(8,128)} %emb_ref.1, s32[1,512]{1,0:T(1,128)} %bitcast.4), custom_call_target="tpu_custom_call" | custom-call | flops 402653184 | bytes 1574912 | tf_op jit(solution)/shard_map/pack_first/pallas_call | solution.py:130
  3.2 0.0 copy-start.1
  3.2 12.0 %all-to-all-start = ((bf16[32,112,128]{2,1,0:T(8,128)(2,1)}), bf16[32,112,128]{2,1,0:T(8,128)(2,1)S(1)}, u32[]{:S(2)}, u32[]{:S(2)}) async-start(bf16[32,112,128]{2,1,0:T(8,128)(2,1)} %get-tuple-element.12), calls=%async_computation | async-start | bytes 1835008 | tf_op jit(solution)/shard_map/all_to_all | solution.py:308
  15.3 0.0 copy-done.2
  15.3 0.0 copy-done.1
  15.3 0.4 pack_table.1.refs_0_
  15.7 1.0 collective-permute-start.3
  16.8 2.5 %collective-permute-start.4 = (bf16[32,16,128]{2,1,0:T(8,128)(2,1)S(1)}, bf16[32,16,128]{2,1,0:T(8,128)(2,1)S(1)}, u32[]{:S(2)}, u32[]{:S(2)}) collective-permute-start(bf16[32,16,128]{2,1,0:T(8,128)(2,1)S(1)} %pack_table.1.refs_0_), channel_id=1, source_target_pairs={{64,0},{72,8},{128,64},{136,72},{200,128},{192,136},{8,192},{0,200... | collective-permute-start | bytes 393224 | tf_op jit(solution)/shard_map/ppermute | solution.py:300
  19.2 0.0 collective-permute-start.5
  19.2 0.0 collective-permute-done.3.refs_1_
  19.2 2.8 %collective-permute-done.4.refs_2_ = bf16[32,16,128]{2,1,0:T(8,128)(2,1)S(1)} collective-permute-done((bf16[32,16,128]{2,1,0:T(8,128)(2,1)S(1)}, bf16[32,16,128]{2,1,0:T(8,128)(2,1)S(1)}, u32[]{:S(2)}, u32[]{:S(2)}) %collective-permute-start.4) | collective-permute-done | bytes 131104 | tf_op jit(solution)/shard_map/ppermute | solution.py:300
  22.0 3.1 %collective-permute-done.5.refs_3_ = bf16[32,16,128]{2,1,0:T(8,128)(2,1)S(1)} collective-permute-done((bf16[32,16,128]{2,1,0:T(8,128)(2,1)S(1)}, bf16[32,16,128]{2,1,0:T(8,128)(2,1)S(1)}, u32[]{:S(2)}, u32[]{:S(2)}) %collective-permute-start.5) | collective-permute-done | bytes 131104 | tf_op jit(solution)/shard_map/ppermute | solution.py:300
  25.1 0.0 copy-done
  25.1 1.7 %pack_second.1 = bf16[32,96,128]{2,1,0:T(8,128)(2,1)} custom-call(f32[512,768]{1,0:T(8,128)S(1)} %copy-done, s32[1,512]{1,0:T(1,128)S(1)} %copy-done.1, bf16[32,16,128]{2,1,0:T(8,128)(2,1)S(1)} %pack_table.1.refs_0_, bf16[32,16,128]{2,1,0:T(8,128)(2,1)S(1)} %collective-permute-done.3.refs_1_, bf16[32,16,128]{2,1,0:T(8,128)(2,1)S(1)} %collective-permute-done.4.refs_2_, ...), custom_call_target="tpu_custom_call" | custom-call | flops 402653184 | bytes 2099200 | tf_op jit(solution)/shard_map/pack_second/pallas_call | solution.py:130
  26.8 10.4 %all-to-all-done.refs_1_.refs_2_ = bf16[32,112,128]{2,1,0:T(8,128)(2,1)S(1)} async-done(((bf16[32,112,128]{2,1,0:T(8,128)(2,1)}), bf16[32,112,128]{2,1,0:T(8,128)(2,1)S(1)}, u32[]{:S(2)}, u32[]{:S(2)}) %all-to-all-start) | async-done | bytes 917536 | tf_op jit(solution)/shard_map/all_to_all | solution.py:308
  37.2 8.5 %all-to-all-start.1 = ((bf16[32,96,128]{2,1,0:T(8,128)(2,1)}), bf16[32,96,128]{2,1,0:T(8,128)(2,1)S(1)}, u32[]{:S(2)}, u32[]{:S(2)}) async-start(bf16[32,96,128]{2,1,0:T(8,128)(2,1)} %pack_second.1), calls=%async_computation.1 | async-start | bytes 1572864 | tf_op jit(solution)/shard_map/all_to_all | solution.py:308
  45.7 1.5 %collective-permute-start.1 = (bf16[32,112,128]{2,1,0:T(8,128)(2,1)S(1)}, bf16[32,112,128]{2,1,0:T(8,128)(2,1)S(1)}, u32[]{:S(2)}, u32[]{:S(2)}) collective-permute-start(bf16[32,112,128]{2,1,0:T(8,128)(2,1)S(1)} %all-to-all-done.refs_1_.refs_2_), channel_id=1, source_target_pairs={{8,0},{0,8},{72,64},{64,72},{136,128},{128,136},{200,192},{192,200... | collective-permute-start | bytes 2752520 | tf_op jit(solution)/shard_map/ppermute | solution.py:300
  47.2 2.5 %collective-permute-start = (bf16[32,112,128]{2,1,0:T(8,128)(2,1)S(1)}, bf16[32,112,128]{2,1,0:T(8,128)(2,1)}, u32[]{:S(2)}, u32[]{:S(2)}) collective-permute-start(bf16[32,112,128]{2,1,0:T(8,128)(2,1)S(1)} %all-to-all-done.refs_1_.refs_2_), channel_id=1, source_target_pairs={{64,0},{72,8},{128,64},{136,72},{200,128},{192,136},{8,192},{0,200... | collective-permute-start | bytes 2752520 | tf_op jit(solution)/shard_map/ppermute | solution.py:300
  49.7 0.0 collective-permute-start.2
  49.7 15.8 %all-to-all-done.1.home_ref = bf16[32,96,128]{2,1,0:T(8,128)(2,1)S(1)} async-done(((bf16[32,96,128]{2,1,0:T(8,128)(2,1)}), bf16[32,96,128]{2,1,0:T(8,128)(2,1)S(1)}, u32[]{:S(2)}, u32[]{:S(2)}) %all-to-all-start.1) | async-done | bytes 786464 | tf_op jit(solution)/shard_map/all_to_all | solution.py:308
  65.5 0.1 cut.1
  65.5 4.6 %collective-permute-start.8 = (bf16[32,80,128]{2,1,0:T(8,128)(2,1)S(1)}, bf16[32,80,128]{2,1,0:T(8,128)(2,1)S(1)}, u32[]{:S(2)}, u32[]{:S(2)}) collective-permute-start(bf16[32,80,128]{2,1,0:T(8,128)(2,1)S(1)} %get-tuple-element.16.refs_2_.refs_3_), channel_id=1, source_target_pairs={{8,0},{0,8},{72,64},{64,72},{136,128},{128,136},{200,192},{192,200... | collective-permute-start | bytes 1966088 | tf_op jit(solution)/shard_map/ppermute | solution.py:300
  70.1 2.5 %collective-permute-start.6 = (bf16[32,80,128]{2,1,0:T(8,128)(2,1)S(1)}, bf16[32,80,128]{2,1,0:T(8,128)(2,1)S(1)}, u32[]{:S(2)}, u32[]{:S(2)}) collective-permute-start(bf16[32,80,128]{2,1,0:T(8,128)(2,1)S(1)} %get-tuple-element.16.refs_2_.refs_3_), channel_id=1, source_target_pairs={{64,0},{72,8},{128,64},{136,72},{200,128},{192,136},{8,192},{0,200... | collective-permute-start | bytes 1966088 | tf_op jit(solution)/shard_map/ppermute | solution.py:300
  72.6 0.0 collective-permute-done.1.refs_2_.refs_3_.refs_4_
  72.6 0.0 collective-permute-start.7
  72.6 0.0 collective-permute-done.refs_0_
  72.6 0.0 collective-permute-done.2.refs_3_
  72.6 4.2 %score_first.1 = (f32[8,512]{1,0:T(8,128)S(1)}, bf16[32,112,128]{2,1,0:T(8,128)(2,1)S(1)}, bf16[32,112,128]{2,1,0:T(8,128)(2,1)S(1)}) custom-call(bf16[32,112,128]{2,1,0:T(8,128)(2,1)} %collective-permute-done.refs_0_, bf16[32,112,128]{2,1,0:T(8,128)(2,1)S(1)} %all-to-all-done.refs_1_.refs_2_, ...), custom_call_target="tpu_custom_call" | custom-call | flops 2013265920 | bytes 3801088 | tf_op jit(solution)/shard_map/score_first/pallas_call | solution.py:130
  76.8 0.0 collective-permute-done.8.refs_4_.refs_5_
  76.9 4.1 %score_second.1.refs_8_ = f32[8,512]{1,0:T(8,128)S(1)} custom-call(bf16[32,112,128]{2,1,0:T(8,128)(2,1)S(1)} %get-tuple-element.15.refs_0_, bf16[32,112,128]{2,1,0:T(8,128)(2,1)S(1)} %all-to-all-done.refs_1_.refs_2_, bf16[32,80,128]{2,1,0:T(8,128)(2,1)S(1)} %get-tuple-element.16.refs_2_.refs_3_, ...), custom_call_target="tpu_custom_call" | custom-call | flops 3221225472 | bytes 5128192 | tf_op jit(solution)/shard_map/score_second/pallas_call | solution.py:130
  81.0 5.6 %collective-permute-done.6.refs_1_ = bf16[32,80,128]{2,1,0:T(8,128)(2,1)S(1)} collective-permute-done((bf16[32,80,128]{2,1,0:T(8,128)(2,1)S(1)}, bf16[32,80,128]{2,1,0:T(8,128)(2,1)S(1)}, u32[]{:S(2)}, u32[]{:S(2)}) %collective-permute-start.6) | collective-permute-done | bytes 655392 | tf_op jit(solution)/shard_map/ppermute | solution.py:300
  86.6 1.7 %score_third.1.refs_5_ = f32[8,512]{1,0:T(8,128)S(1)} custom-call(bf16[32,112,128]{2,1,0:T(8,128)(2,1)S(1)} %get-tuple-element.15.refs_0_, bf16[32,80,128]{2,1,0:T(8,128)(2,1)S(1)} %collective-permute-done.6.refs_1_, bf16[32,112,128]{2,1,0:T(8,128)(2,1)S(1)} %all-to-all-done.refs_1_.refs_2_, bf16[32,80,128]{2,1,0:T(8,128)(2,1)S(1)} %get-tuple-element.16.refs_2_.refs_3_, ...), custom_call_target="tpu_custom_call" | custom-call | flops 1207959552 | bytes 5783552 | tf_op jit(solution)/shard_map/score_third/pallas_call | solution.py:130
  88.3 1.4 %collective-permute-done.7.refs_3_ = bf16[32,80,128]{2,1,0:T(8,128)(2,1)S(1)} collective-permute-done((bf16[32,80,128]{2,1,0:T(8,128)(2,1)S(1)}, bf16[32,80,128]{2,1,0:T(8,128)(2,1)S(1)}, u32[]{:S(2)}, u32[]{:S(2)}) %collective-permute-start.7) | collective-permute-done | bytes 655392 | tf_op jit(solution)/shard_map/ppermute | solution.py:300
  89.7 1.6 %score_fourth.1 = f32[32,1,128]{2,1,0:T(1,128)S(1)} custom-call(bf16[32,112,128]{2,1,0:T(8,128)(2,1)S(1)} %get-tuple-element.15.refs_0_, bf16[32,80,128]{2,1,0:T(8,128)(2,1)S(1)} %collective-permute-done.6.refs_1_, bf16[32,112,128]{2,1,0:T(8,128)(2,1)S(1)} %get-tuple-element.17.refs_5_.refs_6_.refs_2_, ...), custom_call_target="tpu_custom_call" | custom-call | flops 805306368 | bytes 3293184 | tf_op jit(solution)/shard_map/score_fourth/pallas_call | solution.py:130
  91.3 14.7 %all_to_all.15.own_ref = f32[32,1,128]{2,1,0:T(1,128)S(1)} all-to-all(f32[32,1,128]{2,1,0:T(1,128)S(1)} %score_fourth.1), channel_id=1, replica_groups=mesh['x'=4,'y'=4,'c'=2,'z'=8] {'y','z'}, dimensions={0} | all-to-all | bytes 32768 | tf_op jit(solution)/shard_map/all_to_all | solution.py:308
  106.0 0.0 collective-permute-start.10
  106.0 5.3 %collective-permute-start.11 = (f32[32,1,128]{2,1,0:T(1,128)S(1)}, f32[32,1,128]{2,1,0:T(1,128)S(1)}, u32[]{:S(2)}, u32[]{:S(2)}) collective-permute-start(f32[32,1,128]{2,1,0:T(1,128)S(1)} %all_to_all.15.own_ref), channel_id=1, source_target_pairs={{0,192},{8,200},{64,0},{72,8},{128,64},{136,72},{192,128},{200,136... | collective-permute-start | bytes 49160 | tf_op jit(solution)/shard_map/ppermute | solution.py:300
  111.3 0.0 collective-permute-start.9
  111.3 0.0 collective-permute-done.10.next_ref
  111.3 0.9 collective-permute-done.11.last_ref
  112.1 0.3 collective-permute-done.9.swap_ref
  112.5 0.9 finish.1
Async XLA Ops:
  0.0 15.3 %copy-start.2 = (s32[512]{0:T(512)S(1)}, s32[512]{0:T(512)}, u32[]{:S(2)}) copy-start(s32[512]{0:T(512)} %param.5) | copy-start | bytes 6148
  0.0 25.1 %copy-start = (f32[512,768]{1,0:T(8,128)S(1)}, f32[512,768]{1,0:T(8,128)}, u32[]{:S(2)}) copy-start(f32[512,768]{1,0:T(8,128)} %emb_ref.1) | copy-start | bytes 4718596
  3.2 12.1 %copy-start.1 = (s32[1,512]{1,0:T(1,128)S(1)}, s32[1,512]{1,0:T(1,128)}, u32[]{:S(2)}) copy-start(s32[1,512]{1,0:T(1,128)} %get-tuple-element.13.pos_ref) | copy-start | bytes 6148
  3.2 34.0 %all-to-all-start = ((bf16[32,112,128]{2,1,0:T(8,128)(2,1)}), bf16[32,112,128]{2,1,0:T(8,128)(2,1)S(1)}, u32[]{:S(2)}, u32[]{:S(2)}) async-start(bf16[32,112,128]{2,1,0:T(8,128)(2,1)} %get-tuple-element.12), calls=%async_computation | async-start | bytes 1835008 | tf_op jit(solution)/shard_map/all_to_all | solution.py:308
  15.7 3.5 %collective-permute-start.3 = (bf16[32,16,128]{2,1,0:T(8,128)(2,1)S(1)}, bf16[32,16,128]{2,1,0:T(8,128)(2,1)S(1)}, u32[]{:S(2)}, u32[]{:S(2)}) collective-permute-start(bf16[32,16,128]{2,1,0:T(8,128)(2,1)S(1)} %pack_table.1.refs_0_), channel_id=1, source_target_pairs={{8,0},{0,8},{72,64},{64,72},{136,128},{128,136},{200,192},{192,200... | collective-permute-start | bytes 393224 | tf_op jit(solution)/shard_map/ppermute | solution.py:300
  16.8 5.2 %collective-permute-start.4 = (bf16[32,16,128]{2,1,0:T(8,128)(2,1)S(1)}, bf16[32,16,128]{2,1,0:T(8,128)(2,1)S(1)}, u32[]{:S(2)}, u32[]{:S(2)}) collective-permute-start(bf16[32,16,128]{2,1,0:T(8,128)(2,1)S(1)} %pack_table.1.refs_0_), channel_id=1, source_target_pairs={{64,0},{72,8},{128,64},{136,72},{200,128},{192,136},{8,192},{0,200... | collective-permute-start | bytes 393224 | tf_op jit(solution)/shard_map/ppermute | solution.py:300
  19.2 5.9 %collective-permute-start.5 = (bf16[32,16,128]{2,1,0:T(8,128)(2,1)S(1)}, bf16[32,16,128]{2,1,0:T(8,128)(2,1)S(1)}, u32[]{:S(2)}, u32[]{:S(2)}) collective-permute-start(bf16[32,16,128]{2,1,0:T(8,128)(2,1)S(1)} %pack_table.1.refs_0_), channel_id=1, source_target_pairs={{192,0},{200,8},{0,64},{8,72},{64,128},{72,136},{128,192},{136,200... | collective-permute-start | bytes 393224 | tf_op jit(solution)/shard_map/ppermute | solution.py:300
  37.2 28.2 %all-to-all-start.1 = ((bf16[32,96,128]{2,1,0:T(8,128)(2,1)}), bf16[32,96,128]{2,1,0:T(8,128)(2,1)S(1)}, u32[]{:S(2)}, u32[]{:S(2)}) async-start(bf16[32,96,128]{2,1,0:T(8,128)(2,1)} %pack_second.1), calls=%async_computation.1 | async-start | bytes 1572864 | tf_op jit(solution)/shard_map/all_to_all | solution.py:308
  45.7 26.9 %collective-permute-start.1 = (bf16[32,112,128]{2,1,0:T(8,128)(2,1)S(1)}, bf16[32,112,128]{2,1,0:T(8,128)(2,1)S(1)}, u32[]{:S(2)}, u32[]{:S(2)}) collective-permute-start(bf16[32,112,128]{2,1,0:T(8,128)(2,1)S(1)} %all-to-all-done.refs_1_.refs_2_), channel_id=1, source_target_pairs={{8,0},{0,8},{72,64},{64,72},{136,128},{128,136},{200,192},{192,200... | collective-permute-start | bytes 2752520 | tf_op jit(solution)/shard_map/ppermute | solution.py:300
  47.2 25.4 %collective-permute-start = (bf16[32,112,128]{2,1,0:T(8,128)(2,1)S(1)}, bf16[32,112,128]{2,1,0:T(8,128)(2,1)}, u32[]{:S(2)}, u32[]{:S(2)}) collective-permute-start(bf16[32,112,128]{2,1,0:T(8,128)(2,1)S(1)} %all-to-all-done.refs_1_.refs_2_), channel_id=1, source_target_pairs={{64,0},{72,8},{128,64},{136,72},{200,128},{192,136},{8,192},{0,200... | collective-permute-start | bytes 2752520 | tf_op jit(solution)/shard_map/ppermute | solution.py:300
  49.7 22.9 %collective-permute-start.2 = (bf16[32,112,128]{2,1,0:T(8,128)(2,1)S(1)}, bf16[32,112,128]{2,1,0:T(8,128)(2,1)}, u32[]{:S(2)}, u32[]{:S(2)}) collective-permute-start(bf16[32,112,128]{2,1,0:T(8,128)(2,1)S(1)} %all-to-all-done.refs_1_.refs_2_), channel_id=1, source_target_pairs={{192,0},{200,8},{0,64},{8,72},{64,128},{72,136},{128,192},{136,200... | collective-permute-start | bytes 2752520 | tf_op jit(solution)/shard_map/ppermute | solution.py:300
  65.5 11.3 %collective-permute-start.8 = (bf16[32,80,128]{2,1,0:T(8,128)(2,1)S(1)}, bf16[32,80,128]{2,1,0:T(8,128)(2,1)S(1)}, u32[]{:S(2)}, u32[]{:S(2)}) collective-permute-start(bf16[32,80,128]{2,1,0:T(8,128)(2,1)S(1)} %get-tuple-element.16.refs_2_.refs_3_), channel_id=1, source_target_pairs={{8,0},{0,8},{72,64},{64,72},{136,128},{128,136},{200,192},{192,200... | collective-permute-start | bytes 1966088 | tf_op jit(solution)/shard_map/ppermute | solution.py:300
  70.1 16.5 %collective-permute-start.6 = (bf16[32,80,128]{2,1,0:T(8,128)(2,1)S(1)}, bf16[32,80,128]{2,1,0:T(8,128)(2,1)S(1)}, u32[]{:S(2)}, u32[]{:S(2)}) collective-permute-start(bf16[32,80,128]{2,1,0:T(8,128)(2,1)S(1)} %get-tuple-element.16.refs_2_.refs_3_), channel_id=1, source_target_pairs={{64,0},{72,8},{128,64},{136,72},{200,128},{192,136},{8,192},{0,200... | collective-permute-start | bytes 1966088 | tf_op jit(solution)/shard_map/ppermute | solution.py:300
  72.6 17.1 %collective-permute-start.7 = (bf16[32,80,128]{2,1,0:T(8,128)(2,1)S(1)}, bf16[32,80,128]{2,1,0:T(8,128)(2,1)S(1)}, u32[]{:S(2)}, u32[]{:S(2)}) collective-permute-start(bf16[32,80,128]{2,1,0:T(8,128)(2,1)S(1)} %get-tuple-element.16.refs_2_.refs_3_), channel_id=1, source_target_pairs={{192,0},{200,8},{0,64},{8,72},{64,128},{72,136},{128,192},{136,200... | collective-permute-start | bytes 1966088 | tf_op jit(solution)/shard_map/ppermute | solution.py:300
  106.0 5.3 %collective-permute-start.10 = (f32[32,1,128]{2,1,0:T(1,128)S(1)}, f32[32,1,128]{2,1,0:T(1,128)S(1)}, u32[]{:S(2)}, u32[]{:S(2)}) collective-permute-start(f32[32,1,128]{2,1,0:T(1,128)S(1)} %all_to_all.15.own_ref), channel_id=1, source_target_pairs={{0,64},{8,72},{64,128},{72,136},{128,200},{136,192},{192,8},{200,0... | collective-permute-start | bytes 49160 | tf_op jit(solution)/shard_map/ppermute | solution.py:300
  106.0 6.1 %collective-permute-start.11 = (f32[32,1,128]{2,1,0:T(1,128)S(1)}, f32[32,1,128]{2,1,0:T(1,128)S(1)}, u32[]{:S(2)}, u32[]{:S(2)}) collective-permute-start(f32[32,1,128]{2,1,0:T(1,128)S(1)} %all_to_all.15.own_ref), channel_id=1, source_target_pairs={{0,192},{8,200},{64,0},{72,8},{128,64},{136,72},{192,128},{200,136... | collective-permute-start | bytes 49160 | tf_op jit(solution)/shard_map/ppermute | solution.py:300
  111.3 1.2 %collective-permute-start.9 = (f32[32,1,128]{2,1,0:T(1,128)S(1)}, f32[32,1,128]{2,1,0:T(1,128)S(1)}, u32[]{:S(2)}, u32[]{:S(2)}) collective-permute-start(f32[32,1,128]{2,1,0:T(1,128)S(1)} %all_to_all.15.own_ref), channel_id=1, source_target_pairs={{0,8},{8,0},{64,72},{72,64},{128,136},{136,128},{192,200},{200,192... | collective-permute-start | bytes 49160 | tf_op jit(solution)/shard_map/ppermute | solution.py:300

commit v11 on v10

--- a/solution.py
+++ b/solution.py
@@ -254,10 +254,12 @@
     ("o1", "o1", True, False),
     ("o0", "o1", True, True),
     ("o1", "b0", True, True),
+    ("o1", "z0", True, True),
+)
+SWAPPED = (
     ("o1", "s1", True, False),
     ("o0", "s1", True, True),
     ("s1", "b0", True, True),
-    ("o1", "z0", True, True),
     ("s1", "z0", True, True),
 )
 THIRD = (
@@ -358,6 +360,7 @@
     best, *kept = score(blocks, FIRST, None, False, "score_first")
     blocks.update(zip(KEPT, kept))
     best = score(blocks, SECOND, best, False, "score_second")
+    best = score(blocks, SWAPPED, best, False, "score_swapped")
     best = score(blocks, THIRD, best, False, "score_third")
     own = to_home(score(blocks, FOURTH, best, True, "score_fourth"))
     nearest = call(

time: 114 us -> 114 us (level)
    pallas_call x9 -> x10, Pallas kernels: 18 us -> 18.5 us  [call(): pl.pallas_call(kernel, out_shape=shapes, in_specs=[pl.BlockSpec(memory_sp...]
where the time goes in v11:
time: 114 us; the launch traced here: 113 us
  starting transfers between devices  40.3 us (35%)
  waiting for transfers between devices  39.7 us (35%)
  Pallas kernels  18.5 us (16%)
  blocking collectives  14.7 us (13%)
    all_to_all x2, waiting for transfers between devices, to_home(): lax.all_to_all(array, ('y', 'z'), split_axis=0, concat_axis=0, tiled=True)  26.2 us
    all_to_all x2, starting transfers between devices, to_home(): lax.all_to_all(array, ('y', 'z'), split_axis=0, concat_axis=0, tiled=True)  20.5 us
    ppermute x12, starting transfers between devices, send(): return lax.ppermute(array, ('x', 'c'), pairs)  19.8 us
    pallas_call x10, Pallas kernels, call(): pl.pallas_call(kernel, out_shape=shapes, in_specs=[pl.BlockSpec(memory_sp...  18.5 us
    all_to_all x1, blocking collectives, to_home(): lax.all_to_all(array, ('y', 'z'), split_axis=0, concat_axis=0, tiled=True)  14.7 us
    ppermute x12, waiting for transfers between devices, send(): return lax.ppermute(array, ('x', 'c'), pairs)  13.5 us
  transfers between devices with their start and end apart: 14, of which 8 were waited for; matrix products, arithmetic and copies ran while one was open for 0% of the time, Pallas kernels for 11%

profile of v11, /device:TPU:1, one launch (start us, length us, event | category | flops | bytes accessed | tf_op | source)
XLA Modules:
  0.0 113.4 jit_solution(9159141524145458951)
XLA Ops:
  0.0 0.0 copy-start.2
  0.0 0.0 copy-start
  0.0 3.2 %pack_first.1 = (bf16[32,112,128]{2,1,0:T(8,128)(2,1)}, s32[1,512]{1,0:T(1,128)}) custom-call(f32[512,768]{1,0:T(8,128)} %emb_ref.1, s32[1,512]{1,0:T(1,128)} %bitcast.4), custom_call_target="tpu_custom_call" | custom-call | flops 402653184 | bytes 1574912 | tf_op jit(solution)/shard_map/pack_first/pallas_call | solution.py:130
  3.2 0.0 copy-start.1
  3.2 12.0 %all-to-all-start = ((bf16[32,112,128]{2,1,0:T(8,128)(2,1)}), bf16[32,112,128]{2,1,0:T(8,128)(2,1)S(1)}, u32[]{:S(2)}, u32[]{:S(2)}) async-start(bf16[32,112,128]{2,1,0:T(8,128)(2,1)} %get-tuple-element.12), calls=%async_computation | async-start | bytes 1835008 | tf_op jit(solution)/shard_map/all_to_all | solution.py:310
  15.3 0.0 copy-done.2
  15.3 0.0 copy-done.1
  15.3 0.4 pack_table.1.refs_0_
  15.7 1.0 collective-permute-start.3
  16.8 2.5 %collective-permute-start.4 = (bf16[32,16,128]{2,1,0:T(8,128)(2,1)S(1)}, bf16[32,16,128]{2,1,0:T(8,128)(2,1)S(1)}, u32[]{:S(2)}, u32[]{:S(2)}) collective-permute-start(bf16[32,16,128]{2,1,0:T(8,128)(2,1)S(1)} %pack_table.1.refs_0_), channel_id=1, source_target_pairs={{64,0},{72,8},{128,64},{136,72},{200,128},{192,136},{8,192},{0,200... | collective-permute-start | bytes 393224 | tf_op jit(solution)/shard_map/ppermute | solution.py:302
  19.2 0.0 collective-permute-start.5
  19.2 0.0 collective-permute-done.3.refs_1_
  19.2 2.8 %collective-permute-done.4.refs_2_ = bf16[32,16,128]{2,1,0:T(8,128)(2,1)S(1)} collective-permute-done((bf16[32,16,128]{2,1,0:T(8,128)(2,1)S(1)}, bf16[32,16,128]{2,1,0:T(8,128)(2,1)S(1)}, u32[]{:S(2)}, u32[]{:S(2)}) %collective-permute-start.4) | collective-permute-done | bytes 131104 | tf_op jit(solution)/shard_map/ppermute | solution.py:302
  22.0 3.1 %collective-permute-done.5.refs_3_ = bf16[32,16,128]{2,1,0:T(8,128)(2,1)S(1)} collective-permute-done((bf16[32,16,128]{2,1,0:T(8,128)(2,1)S(1)}, bf16[32,16,128]{2,1,0:T(8,128)(2,1)S(1)}, u32[]{:S(2)}, u32[]{:S(2)}) %collective-permute-start.5) | collective-permute-done | bytes 131104 | tf_op jit(solution)/shard_map/ppermute | solution.py:302
  25.1 0.0 copy-done
  25.1 1.7 %pack_second.1 = bf16[32,96,128]{2,1,0:T(8,128)(2,1)} custom-call(f32[512,768]{1,0:T(8,128)S(1)} %copy-done, s32[1,512]{1,0:T(1,128)S(1)} %copy-done.1, bf16[32,16,128]{2,1,0:T(8,128)(2,1)S(1)} %pack_table.1.refs_0_, bf16[32,16,128]{2,1,0:T(8,128)(2,1)S(1)} %collective-permute-done.3.refs_1_, bf16[32,16,128]{2,1,0:T(8,128)(2,1)S(1)} %collective-permute-done.4.refs_2_, ...), custom_call_target="tpu_custom_call" | custom-call | flops 402653184 | bytes 2099200 | tf_op jit(solution)/shard_map/pack_second/pallas_call | solution.py:130
  26.8 10.4 %all-to-all-done.refs_1_.refs_2_ = bf16[32,112,128]{2,1,0:T(8,128)(2,1)S(1)} async-done(((bf16[32,112,128]{2,1,0:T(8,128)(2,1)}), bf16[32,112,128]{2,1,0:T(8,128)(2,1)S(1)}, u32[]{:S(2)}, u32[]{:S(2)}) %all-to-all-start) | async-done | bytes 917536 | tf_op jit(solution)/shard_map/all_to_all | solution.py:310
  37.2 8.5 %all-to-all-start.1 = ((bf16[32,96,128]{2,1,0:T(8,128)(2,1)}), bf16[32,96,128]{2,1,0:T(8,128)(2,1)S(1)}, u32[]{:S(2)}, u32[]{:S(2)}) async-start(bf16[32,96,128]{2,1,0:T(8,128)(2,1)} %pack_second.1), calls=%async_computation.1 | async-start | bytes 1572864 | tf_op jit(solution)/shard_map/all_to_all | solution.py:310
  45.7 1.5 %collective-permute-start.1 = (bf16[32,112,128]{2,1,0:T(8,128)(2,1)S(1)}, bf16[32,112,128]{2,1,0:T(8,128)(2,1)S(1)}, u32[]{:S(2)}, u32[]{:S(2)}) collective-permute-start(bf16[32,112,128]{2,1,0:T(8,128)(2,1)S(1)} %all-to-all-done.refs_1_.refs_2_), channel_id=1, source_target_pairs={{8,0},{0,8},{72,64},{64,72},{136,128},{128,136},{200,192},{192,200... | collective-permute-start | bytes 2752520 | tf_op jit(solution)/shard_map/ppermute | solution.py:302
  47.2 2.5 %collective-permute-start = (bf16[32,112,128]{2,1,0:T(8,128)(2,1)S(1)}, bf16[32,112,128]{2,1,0:T(8,128)(2,1)}, u32[]{:S(2)}, u32[]{:S(2)}) collective-permute-start(bf16[32,112,128]{2,1,0:T(8,128)(2,1)S(1)} %all-to-all-done.refs_1_.refs_2_), channel_id=1, source_target_pairs={{64,0},{72,8},{128,64},{136,72},{200,128},{192,136},{8,192},{0,200... | collective-permute-start | bytes 2752520 | tf_op jit(solution)/shard_map/ppermute | solution.py:302
  49.7 0.0 collective-permute-start.2
  49.7 15.8 %all-to-all-done.1.home_ref = bf16[32,96,128]{2,1,0:T(8,128)(2,1)S(1)} async-done(((bf16[32,96,128]{2,1,0:T(8,128)(2,1)}), bf16[32,96,128]{2,1,0:T(8,128)(2,1)S(1)}, u32[]{:S(2)}, u32[]{:S(2)}) %all-to-all-start.1) | async-done | bytes 786464 | tf_op jit(solution)/shard_map/all_to_all | solution.py:310
  65.5 0.1 cut.1
  65.5 4.6 %collective-permute-start.8 = (bf16[32,80,128]{2,1,0:T(8,128)(2,1)S(1)}, bf16[32,80,128]{2,1,0:T(8,128)(2,1)S(1)}, u32[]{:S(2)}, u32[]{:S(2)}) collective-permute-start(bf16[32,80,128]{2,1,0:T(8,128)(2,1)S(1)} %get-tuple-element.16.refs_2_.refs_3_), channel_id=1, source_target_pairs={{8,0},{0,8},{72,64},{64,72},{136,128},{128,136},{200,192},{192,200... | collective-permute-start | bytes 1966088 | tf_op jit(solution)/shard_map/ppermute | solution.py:302
  70.1 2.5 %collective-permute-start.6 = (bf16[32,80,128]{2,1,0:T(8,128)(2,1)S(1)}, bf16[32,80,128]{2,1,0:T(8,128)(2,1)S(1)}, u32[]{:S(2)}, u32[]{:S(2)}) collective-permute-start(bf16[32,80,128]{2,1,0:T(8,128)(2,1)S(1)} %get-tuple-element.16.refs_2_.refs_3_), channel_id=1, source_target_pairs={{64,0},{72,8},{128,64},{136,72},{200,128},{192,136},{8,192},{0,200... | collective-permute-start | bytes 1966088 | tf_op jit(solution)/shard_map/ppermute | solution.py:302
  72.6 0.0 collective-permute-done.1.refs_2_.refs_3_.refs_4_
  72.6 0.0 collective-permute-start.7
  72.6 0.0 collective-permute-done.refs_0_
  72.6 0.0 collective-permute-done.2.refs_3_
  72.6 4.2 %score_first.1 = (f32[8,512]{1,0:T(8,128)S(1)}, bf16[32,112,128]{2,1,0:T(8,128)(2,1)S(1)}, bf16[32,112,128]{2,1,0:T(8,128)(2,1)S(1)}) custom-call(bf16[32,112,128]{2,1,0:T(8,128)(2,1)} %collective-permute-done.refs_0_, bf16[32,112,128]{2,1,0:T(8,128)(2,1)S(1)} %all-to-all-done.refs_1_.refs_2_, ...), custom_call_target="tpu_custom_call" | custom-call | flops 2013265920 | bytes 3801088 | tf_op jit(solution)/shard_map/score_first/pallas_call | solution.py:130
  76.8 2.3 %score_second.1.refs_7_ = f32[8,512]{1,0:T(8,128)S(1)} custom-call(bf16[32,112,128]{2,1,0:T(8,128)(2,1)S(1)} %get-tuple-element.15.refs_0_, bf16[32,112,128]{2,1,0:T(8,128)(2,1)S(1)} %all-to-all-done.refs_1_.refs_2_, bf16[32,80,128]{2,1,0:T(8,128)(2,1)S(1)} %get-tuple-element.16.refs_2_.refs_3_, ...), custom_call_target="tpu_custom_call" | custom-call | flops 1610612736 | bytes 3555328 | tf_op jit(solution)/shard_map/score_second/pallas_call | solution.py:130
  79.1 0.0 collective-permute-done.8.refs_4_.refs_5_
  79.2 2.3 %score_swapped.1.refs_8_ = f32[8,512]{1,0:T(8,128)S(1)} custom-call(bf16[32,112,128]{2,1,0:T(8,128)(2,1)S(1)} %get-tuple-element.15.refs_0_, bf16[32,112,128]{2,1,0:T(8,128)(2,1)S(1)} %all-to-all-done.refs_1_.refs_2_, bf16[32,80,128]{2,1,0:T(8,128)(2,1)S(1)} %get-tuple-element.16.refs_2_.refs_3_, ...), custom_call_target="tpu_custom_call" | custom-call | flops 1610612736 | bytes 5128192 | tf_op jit(solution)/shard_map/score_swapped/pallas_call | solution.py:130
  81.5 5.1 %collective-permute-done.6.refs_1_ = bf16[32,80,128]{2,1,0:T(8,128)(2,1)S(1)} collective-permute-done((bf16[32,80,128]{2,1,0:T(8,128)(2,1)S(1)}, bf16[32,80,128]{2,1,0:T(8,128)(2,1)S(1)}, u32[]{:S(2)}, u32[]{:S(2)}) %collective-permute-start.6) | collective-permute-done | bytes 655392 | tf_op jit(solution)/shard_map/ppermute | solution.py:302
  86.6 1.7 %score_third.1.refs_5_ = f32[8,512]{1,0:T(8,128)S(1)} custom-call(bf16[32,112,128]{2,1,0:T(8,128)(2,1)S(1)} %get-tuple-element.15.refs_0_, bf16[32,80,128]{2,1,0:T(8,128)(2,1)S(1)} %collective-permute-done.6.refs_1_, bf16[32,112,128]{2,1,0:T(8,128)(2,1)S(1)} %all-to-all-done.refs_1_.refs_2_, bf16[32,80,128]{2,1,0:T(8,128)(2,1)S(1)} %get-tuple-element.16.refs_2_.refs_3_, ...), custom_call_target="tpu_custom_call" | custom-call | flops 1207959552 | bytes 5783552 | tf_op jit(solution)/shard_map/score_third/pallas_call | solution.py:130
  88.3 1.4 %collective-permute-done.7.refs_3_ = bf16[32,80,128]{2,1,0:T(8,128)(2,1)S(1)} collective-permute-done((bf16[32,80,128]{2,1,0:T(8,128)(2,1)S(1)}, bf16[32,80,128]{2,1,0:T(8,128)(2,1)S(1)}, u32[]{:S(2)}, u32[]{:S(2)}) %collective-permute-start.7) | collective-permute-done | bytes 655392 | tf_op jit(solution)/shard_map/ppermute | solution.py:302
  89.7 1.6 %score_fourth.1 = f32[32,1,128]{2,1,0:T(1,128)S(1)} custom-call(bf16[32,112,128]{2,1,0:T(8,128)(2,1)S(1)} %get-tuple-element.15.refs_0_, bf16[32,80,128]{2,1,0:T(8,128)(2,1)S(1)} %collective-permute-done.6.refs_1_, bf16[32,112,128]{2,1,0:T(8,128)(2,1)S(1)} %get-tuple-element.17.refs_3_.refs_5_.refs_6_.refs_2_, ...), custom_call_target="tpu_custom_call" | custom-call | flops 805306368 | bytes 3293184 | tf_op jit(solution)/shard_map/score_fourth/pallas_call | solution.py:130
  91.3 14.7 %all_to_all.15.own_ref = f32[32,1,128]{2,1,0:T(1,128)S(1)} all-to-all(f32[32,1,128]{2,1,0:T(1,128)S(1)} %score_fourth.1), channel_id=1, replica_groups=mesh['x'=4,'y'=4,'c'=2,'z'=8] {'y','z'}, dimensions={0} | all-to-all | bytes 32768 | tf_op jit(solution)/shard_map/all_to_all | solution.py:310
  106.0 0.0 collective-permute-start.10
  106.0 5.3 %collective-permute-start.11 = (f32[32,1,128]{2,1,0:T(1,128)S(1)}, f32[32,1,128]{2,1,0:T(1,128)S(1)}, u32[]{:S(2)}, u32[]{:S(2)}) collective-permute-start(f32[32,1,128]{2,1,0:T(1,128)S(1)} %all_to_all.15.own_ref), channel_id=1, source_target_pairs={{0,192},{8,200},{64,0},{72,8},{128,64},{136,72},{192,128},{200,136... | collective-permute-start | bytes 49160 | tf_op jit(solution)/shard_map/ppermute | solution.py:302
  111.3 0.0 collective-permute-start.9
  111.3 0.0 collective-permute-done.10.next_ref
  111.3 0.9 collective-permute-done.11.last_ref
  112.1 0.3 collective-permute-done.9.swap_ref
  112.5 0.9 finish.1
Async XLA Ops:
  0.0 15.3 %copy-start.2 = (s32[512]{0:T(512)S(1)}, s32[512]{0:T(512)}, u32[]{:S(2)}) copy-start(s32[512]{0:T(512)} %param.5) | copy-start | bytes 6148
  0.0 25.1 %copy-start = (f32[512,768]{1,0:T(8,128)S(1)}, f32[512,768]{1,0:T(8,128)}, u32[]{:S(2)}) copy-start(f32[512,768]{1,0:T(8,128)} %emb_ref.1) | copy-start | bytes 4718596
  3.2 12.1 %copy-start.1 = (s32[1,512]{1,0:T(1,128)S(1)}, s32[1,512]{1,0:T(1,128)}, u32[]{:S(2)}) copy-start(s32[1,512]{1,0:T(1,128)} %get-tuple-element.13.pos_ref) | copy-start | bytes 6148
  3.2 34.0 %all-to-all-start = ((bf16[32,112,128]{2,1,0:T(8,128)(2,1)}), bf16[32,112,128]{2,1,0:T(8,128)(2,1)S(1)}, u32[]{:S(2)}, u32[]{:S(2)}) async-start(bf16[32,112,128]{2,1,0:T(8,128)(2,1)} %get-tuple-element.12), calls=%async_computation | async-start | bytes 1835008 | tf_op jit(solution)/shard_map/all_to_all | solution.py:310
  15.7 3.5 %collective-permute-start.3 = (bf16[32,16,128]{2,1,0:T(8,128)(2,1)S(1)}, bf16[32,16,128]{2,1,0:T(8,128)(2,1)S(1)}, u32[]{:S(2)}, u32[]{:S(2)}) collective-permute-start(bf16[32,16,128]{2,1,0:T(8,128)(2,1)S(1)} %pack_table.1.refs_0_), channel_id=1, source_target_pairs={{8,0},{0,8},{72,64},{64,72},{136,128},{128,136},{200,192},{192,200... | collective-permute-start | bytes 393224 | tf_op jit(solution)/shard_map/ppermute | solution.py:302
  16.8 5.2 %collective-permute-start.4 = (bf16[32,16,128]{2,1,0:T(8,128)(2,1)S(1)}, bf16[32,16,128]{2,1,0:T(8,128)(2,1)S(1)}, u32[]{:S(2)}, u32[]{:S(2)}) collective-permute-start(bf16[32,16,128]{2,1,0:T(8,128)(2,1)S(1)} %pack_table.1.refs_0_), channel_id=1, source_target_pairs={{64,0},{72,8},{128,64},{136,72},{200,128},{192,136},{8,192},{0,200... | collective-permute-start | bytes 393224 | tf_op jit(solution)/shard_map/ppermute | solution.py:302
  19.2 5.9 %collective-permute-start.5 = (bf16[32,16,128]{2,1,0:T(8,128)(2,1)S(1)}, bf16[32,16,128]{2,1,0:T(8,128)(2,1)S(1)}, u32[]{:S(2)}, u32[]{:S(2)}) collective-permute-start(bf16[32,16,128]{2,1,0:T(8,128)(2,1)S(1)} %pack_table.1.refs_0_), channel_id=1, source_target_pairs={{192,0},{200,8},{0,64},{8,72},{64,128},{72,136},{128,192},{136,200... | collective-permute-start | bytes 393224 | tf_op jit(solution)/shard_map/ppermute | solution.py:302
  37.2 28.2 %all-to-all-start.1 = ((bf16[32,96,128]{2,1,0:T(8,128)(2,1)}), bf16[32,96,128]{2,1,0:T(8,128)(2,1)S(1)}, u32[]{:S(2)}, u32[]{:S(2)}) async-start(bf16[32,96,128]{2,1,0:T(8,128)(2,1)} %pack_second.1), calls=%async_computation.1 | async-start | bytes 1572864 | tf_op jit(solution)/shard_map/all_to_all | solution.py:310
  45.7 26.9 %collective-permute-start.1 = (bf16[32,112,128]{2,1,0:T(8,128)(2,1)S(1)}, bf16[32,112,128]{2,1,0:T(8,128)(2,1)S(1)}, u32[]{:S(2)}, u32[]{:S(2)}) collective-permute-start(bf16[32,112,128]{2,1,0:T(8,128)(2,1)S(1)} %all-to-all-done.refs_1_.refs_2_), channel_id=1, source_target_pairs={{8,0},{0,8},{72,64},{64,72},{136,128},{128,136},{200,192},{192,200... | collective-permute-start | bytes 2752520 | tf_op jit(solution)/shard_map/ppermute | solution.py:302
  47.2 25.4 %collective-permute-start = (bf16[32,112,128]{2,1,0:T(8,128)(2,1)S(1)}, bf16[32,112,128]{2,1,0:T(8,128)(2,1)}, u32[]{:S(2)}, u32[]{:S(2)}) collective-permute-start(bf16[32,112,128]{2,1,0:T(8,128)(2,1)S(1)} %all-to-all-done.refs_1_.refs_2_), channel_id=1, source_target_pairs={{64,0},{72,8},{128,64},{136,72},{200,128},{192,136},{8,192},{0,200... | collective-permute-start | bytes 2752520 | tf_op jit(solution)/shard_map/ppermute | solution.py:302
  49.7 22.9 %collective-permute-start.2 = (bf16[32,112,128]{2,1,0:T(8,128)(2,1)S(1)}, bf16[32,112,128]{2,1,0:T(8,128)(2,1)}, u32[]{:S(2)}, u32[]{:S(2)}) collective-permute-start(bf16[32,112,128]{2,1,0:T(8,128)(2,1)S(1)} %all-to-all-done.refs_1_.refs_2_), channel_id=1, source_target_pairs={{192,0},{200,8},{0,64},{8,72},{64,128},{72,136},{128,192},{136,200... | collective-permute-start | bytes 2752520 | tf_op jit(solution)/shard_map/ppermute | solution.py:302
  65.5 13.6 %collective-permute-start.8 = (bf16[32,80,128]{2,1,0:T(8,128)(2,1)S(1)}, bf16[32,80,128]{2,1,0:T(8,128)(2,1)S(1)}, u32[]{:S(2)}, u32[]{:S(2)}) collective-permute-start(bf16[32,80,128]{2,1,0:T(8,128)(2,1)S(1)} %get-tuple-element.16.refs_2_.refs_3_), channel_id=1, source_target_pairs={{8,0},{0,8},{72,64},{64,72},{136,128},{128,136},{200,192},{192,200... | collective-permute-start | bytes 1966088 | tf_op jit(solution)/shard_map/ppermute | solution.py:302
  70.1 16.5 %collective-permute-start.6 = (bf16[32,80,128]{2,1,0:T(8,128)(2,1)S(1)}, bf16[32,80,128]{2,1,0:T(8,128)(2,1)S(1)}, u32[]{:S(2)}, u32[]{:S(2)}) collective-permute-start(bf16[32,80,128]{2,1,0:T(8,128)(2,1)S(1)} %get-tuple-element.16.refs_2_.refs_3_), channel_id=1, source_target_pairs={{64,0},{72,8},{128,64},{136,72},{200,128},{192,136},{8,192},{0,200... | collective-permute-start | bytes 1966088 | tf_op jit(solution)/shard_map/ppermute | solution.py:302
  72.6 17.1 %collective-permute-start.7 = (bf16[32,80,128]{2,1,0:T(8,128)(2,1)S(1)}, bf16[32,80,128]{2,1,0:T(8,128)(2,1)S(1)}, u32[]{:S(2)}, u32[]{:S(2)}) collective-permute-start(bf16[32,80,128]{2,1,0:T(8,128)(2,1)S(1)} %get-tuple-element.16.refs_2_.refs_3_), channel_id=1, source_target_pairs={{192,0},{200,8},{0,64},{8,72},{64,128},{72,136},{128,192},{136,200... | collective-permute-start | bytes 1966088 | tf_op jit(solution)/shard_map/ppermute | solution.py:302
  106.0 5.3 %collective-permute-start.10 = (f32[32,1,128]{2,1,0:T(1,128)S(1)}, f32[32,1,128]{2,1,0:T(1,128)S(1)}, u32[]{:S(2)}, u32[]{:S(2)}) collective-permute-start(f32[32,1,128]{2,1,0:T(1,128)S(1)} %all_to_all.15.own_ref), channel_id=1, source_target_pairs={{0,64},{8,72},{64,128},{72,136},{128,200},{136,192},{192,8},{200,0... | collective-permute-start | bytes 49160 | tf_op jit(solution)/shard_map/ppermute | solution.py:302
  106.0 6.1 %collective-permute-start.11 = (f32[32,1,128]{2,1,0:T(1,128)S(1)}, f32[32,1,128]{2,1,0:T(1,128)S(1)}, u32[]{:S(2)}, u32[]{:S(2)}) collective-permute-start(f32[32,1,128]{2,1,0:T(1,128)S(1)} %all_to_all.15.own_ref), channel_id=1, source_target_pairs={{0,192},{8,200},{64,0},{72,8},{128,64},{136,72},{192,128},{200,136... | collective-permute-start | bytes 49160 | tf_op jit(solution)/shard_map/ppermute | solution.py:302
  111.3 1.2 %collective-permute-start.9 = (f32[32,1,128]{2,1,0:T(1,128)S(1)}, f32[32,1,128]{2,1,0:T(1,128)S(1)}, u32[]{:S(2)}, u32[]{:S(2)}) collective-permute-start(f32[32,1,128]{2,1,0:T(1,128)S(1)} %all_to_all.15.own_ref), channel_id=1, source_target_pairs={{0,8},{8,0},{64,72},{72,64},{128,136},{136,128},{192,200},{200,192... | collective-permute-start | bytes 49160 | tf_op jit(solution)/shard_map/ppermute | solution.py:302
